TPU v7x, 32 devices: a whole 2x2x4 slice. The times are simulated.
32 devices in a mesh: ctx: 8 (over z, x), head: 4 (over y, core).
Axes of the slice: x: 2, y: 2, z: 4, core: 2. Of those that a mesh axis runs over, the one named last changes fastest.
Arguments:
- queries: bfloat16 [2048, 2560], P('ctx', 'head'), may hold values from -130 to 130
- keys: bfloat16 [2048, 2560], P('ctx', 'head'), may hold values from -7 to 7
- values: bfloat16 [2048, 2560], P('ctx', 'head'), may hold values from -6 to 6
- out_weight: bfloat16 [2560, 5120], P('head'), may hold values from -0.125 to 0.125
- reward_grad: bfloat16 [2048, 5120], P('ctx', 'head'), may hold values from -6 to 6
- tile_mask: int32 [16, 10], replicated, may hold values from 0 to 1, as said below
Outputs:
- grad_queries: bfloat16 [2048, 2560], P('ctx', 'head')
- grad_keys: bfloat16 [2048, 2560], P('ctx', 'head')
- grad_values: bfloat16 [2048, 2560], P('ctx', 'head')
Inputs may be any that keep to these rules, and one draw needn't show every extreme that they name: `tile_mask`: entries are 0 or 1. The column 4 + (row % 2), a query tile's own tile, is always 1; columns that name a tile outside the sequence are 0.
All inputs are finite; a program needn't handle non-finite values.
Results may differ from a plain program's by a relative error of at most 0.033.
Values may be sent and summed in bfloat16 or wider, within the bound.
No kernel may reach another device: no remote copies, remote signals or barrier semaphores. Data moves between devices by JAX's collectives and lax.ppermute only.
A program may use at most 128 MiB of HBM per device.

v0:
```python
import math

import jax
import jax.numpy as jnp
from jax import lax
from jax.sharding import PartitionSpec as P

HEAD_DIM = 128
TILE = 128
SPAN = 2


def from_behind(array, axis, by):
    length = lax.axis_size(axis)
    pairs = [(i, i + by) for i in range(length) if 0 <= i + by < length]
    return lax.ppermute(array, axis, pairs)


def attend_local(query_blk, key_win, value_win, grad_blk, live_pairs, score_scale):
    scores = (
        jnp.einsum("qhd,khd->hqk", query_blk, key_win, preferred_element_type=jnp.float32)
        * score_scale
    )
    live_three = live_pairs[None, :, :]
    row_max = jnp.max(jnp.where(live_three, scores, -jnp.inf), axis=-1, keepdims=True)
    weights = jnp.where(live_three, jnp.exp(scores - row_max), 0.0)
    totals = jnp.sum(weights, axis=-1, keepdims=True)
    attn_out = (
        jnp.einsum(
            "hqk,khd->hqd",
            weights.astype(jnp.bfloat16),
            value_win,
            preferred_element_type=jnp.float32,
        )
        / totals
    ).astype(jnp.bfloat16)
    grad_heads = jnp.transpose(grad_blk, (1, 0, 2))
    delta = jnp.sum(
        grad_heads.astype(jnp.float32) * attn_out.astype(jnp.float32), axis=-1, keepdims=True
    )
    probs = weights / totals
    grad_value_win = jnp.einsum(
        "hqk,hqd->khd", probs.astype(jnp.bfloat16), grad_heads, preferred_element_type=jnp.float32
    )
    dprobs = jnp.einsum("hqd,khd->hqk", grad_heads, value_win, preferred_element_type=jnp.float32)
    dscores = (probs * (dprobs - delta)).astype(jnp.bfloat16)
    grad_query_blk = (
        jnp.einsum("hqk,khd->qhd", dscores, key_win, preferred_element_type=jnp.float32)
        * score_scale
    ).astype(jnp.bfloat16)
    grad_key_win = (
        jnp.einsum("hqk,qhd->khd", dscores, query_blk, preferred_element_type=jnp.float32)
        * score_scale
    )
    return (grad_query_blk, grad_key_win, grad_value_win)


def local(queries, keys, values, out_weight, reward_grad, tile_mask):
    rows_dev = queries.shape[0]
    feat_width = queries.shape[1]
    head_count = feat_width // HEAD_DIM
    tiles_dev = rows_dev // TILE
    win_tiles = (2 * SPAN + 1) * tiles_dev
    total_tiles = tile_mask.shape[0]
    score_scale = 1.0 / math.sqrt(HEAD_DIM)
    position = lax.axis_index("ctx")
    kv_pair = jnp.stack([keys, values])
    from_below = []
    from_above = []
    for offset in range(1, SPAN + 1):
        from_below.append(from_behind(kv_pair, "ctx", offset))
        from_above.append(from_behind(kv_pair, "ctx", -offset))
    window = jnp.concatenate(from_below[::-1] + [kv_pair] + from_above, axis=1)
    grad_sum = lax.dot_general(
        lax.all_gather(reward_grad, "head", axis=1, tiled=True),
        out_weight,
        (((1,), (1,)), ((), ())),
        preferred_element_type=jnp.float32,
    )
    d_out = grad_sum.astype(jnp.bfloat16)
    mask_rows = lax.dynamic_slice_in_dim(tile_mask, position * tiles_dev, tiles_dev, 0)
    target = (position - SPAN) * tiles_dev + jnp.arange(win_tiles, dtype=jnp.int32)
    tile_live = (mask_rows > 0) & ((target >= 0) & (target < total_tiles))[None, :]
    live_pairs = jnp.broadcast_to(
        tile_live[:, None, :, None], (tiles_dev, TILE, win_tiles, TILE)
    ).reshape(rows_dev, win_tiles * TILE)
    window_len = window.shape[1]
    grad_query_blk, grad_key_win, grad_value_win = attend_local(
        queries.reshape(rows_dev, head_count, HEAD_DIM),
        window[0].reshape(window_len, head_count, HEAD_DIM),
        window[1].reshape(window_len, head_count, HEAD_DIM),
        d_out.reshape(rows_dev, head_count, HEAD_DIM),
        live_pairs,
        score_scale,
    )
    grad_window = jnp.stack(
        [
            grad_key_win.reshape(window_len, feat_width),
            grad_value_win.reshape(window_len, feat_width),
        ]
    ).reshape(2, 2 * SPAN + 1, rows_dev, feat_width)
    slices = [grad_window[:, index] for index in range(2 * SPAN + 1)]
    summed = slices[SPAN]
    for offset in range(1, SPAN + 1):
        summed = summed + from_behind(slices[SPAN - offset], "ctx", -offset)
        summed = summed + from_behind(slices[SPAN + offset], "ctx", offset)
    grad_queries = grad_query_blk.reshape(rows_dev, feat_width)
    return (grad_queries, summed[0].astype(jnp.bfloat16), summed[1].astype(jnp.bfloat16))


def solution(mesh):
    placed = (
        P("ctx", "head"),
        P("ctx", "head"),
        P("ctx", "head"),
        P("head", None),
        P("ctx", "head"),
        P(),
    )
    return jax.shard_map(
        local,
        mesh=mesh,
        in_specs=placed,
        out_specs=(P("ctx", "head"), P("ctx", "head"), P("ctx", "head")),
        check_vma=False,
    )
```

profile of v0, /device:TPU:8, one launch (start us, length us, event | category | flops | bytes accessed | tf_op | source)
XLA Modules:
  0.0 173.7 jit_solution(9461125544688394173)
XLA Ops:
  10.3 3.5 %collective-permute-start = (bf16[2,256,640]{1,2,0:T(8,128)(2,1)S(1)}, bf16[2,256,640]{1,2,0:T(8,128)(2,1)}, u32[]{:S(2)}, u32[]{:S(2)}) collective-permute-start(bf16[2,256,640]{1,2,0:T(8,128)(2,1)S(1)} %pad_maximum_fusion.1), channel_id=1, source_target_pairs={{0,8},{4,12},{8,16},{12,20},{16,24},{20,28},{1,9},{5,13},{9,17},{1... | collective-permute-start | bytes 1966088 | tf_op jit(solution)/shard_map/ppermute | solution.py:16
  13.8 3.4 %collective-permute-start.1 = (bf16[2,256,640]{1,2,0:T(8,128)(2,1)S(1)}, bf16[2,256,640]{1,2,0:T(8,128)(2,1)}, u32[]{:S(2)}, u32[]{:S(2)}) collective-permute-start(bf16[2,256,640]{1,2,0:T(8,128)(2,1)S(1)} %pad_maximum_fusion.1), channel_id=1, source_target_pairs={{0,4},{4,8},{8,12},{12,16},{16,20},{20,24},{24,28},{1,5},{5,9},{9,... | collective-permute-start | bytes 1966088 | tf_op jit(solution)/shard_map/ppermute | solution.py:16
  17.2 4.0 %collective-permute-start.3 = (bf16[2,256,640]{1,2,0:T(8,128)(2,1)S(1)}, bf16[2,256,640]{1,2,0:T(8,128)(2,1)S(1)}, u32[]{:S(2)}, u32[]{:S(2)}) collective-permute-start(bf16[2,256,640]{1,2,0:T(8,128)(2,1)S(1)} %pad_maximum_fusion.1), channel_id=1, source_target_pairs={{8,0},{12,4},{16,8},{20,12},{24,16},{28,20},{9,1},{13,5},{17,9},{2... | collective-permute-start | bytes 1966088 | tf_op jit(solution)/shard_map/ppermute | solution.py:16
  21.2 1.9 %collective-permute-start.2 = (bf16[2,256,640]{1,2,0:T(8,128)(2,1)S(1)}, bf16[2,256,640]{1,2,0:T(8,128)(2,1)}, u32[]{:S(2)}, u32[]{:S(2)}) collective-permute-start(bf16[2,256,640]{1,2,0:T(8,128)(2,1)S(1)} %pad_maximum_fusion.1), channel_id=1, source_target_pairs={{4,0},{8,4},{12,8},{16,12},{20,16},{24,20},{28,24},{5,1},{9,5},{13... | collective-permute-start | bytes 1966088 | tf_op jit(solution)/shard_map/ppermute | solution.py:16
  25.0 3.7 %collective-permute-done = bf16[2,256,640]{1,2,0:T(8,128)(2,1)} collective-permute-done((bf16[2,256,640]{1,2,0:T(8,128)(2,1)S(1)}, bf16[2,256,640]{1,2,0:T(8,128)(2,1)}, u32[]{:S(2)}, u32[]{:S(2)}) %collective-permute-start) | collective-permute-done | bytes 655392 | tf_op jit(solution)/shard_map/ppermute | solution.py:16
  29.9 13.9 %collective-permute-done.1 = bf16[2,256,640]{1,2,0:T(8,128)(2,1)} collective-permute-done((bf16[2,256,640]{1,2,0:T(8,128)(2,1)S(1)}, bf16[2,256,640]{1,2,0:T(8,128)(2,1)}, u32[]{:S(2)}, u32[]{:S(2)}) %collective-permute-start.1) | collective-permute-done | bytes 655392 | tf_op jit(solution)/shard_map/ppermute | solution.py:16
  45.0 7.9 %collective-permute-done.2 = bf16[2,256,640]{1,2,0:T(8,128)(2,1)} collective-permute-done((bf16[2,256,640]{1,2,0:T(8,128)(2,1)S(1)}, bf16[2,256,640]{1,2,0:T(8,128)(2,1)}, u32[]{:S(2)}, u32[]{:S(2)}) %collective-permute-start.2) | collective-permute-done | bytes 655392 | tf_op jit(solution)/shard_map/ppermute | solution.py:16
  54.1 1.4 fusion.46
  55.5 5.9 %fusion.47 = (f32[5,256]{1,0:T(8,128)S(1)}, f32[5,256,1280]{1,2,0:T(8,128)}) fusion(pred[256,1280]{0,1:T(8,128)(4,1)S(1)} %copy.24, bf16[1280,5,128]{0,2,1:T(8,128)(2,1)S(1)} %bitcast.84, bf16[256,5,128]{0,2,1:T(8,128)(2,1)S(1)} %bitcast.98), kind=kOutput, calls=%fused_computation.64 | convolution fusion | flops 848692480 | bytes 8852480 | tf_op jit(solution)/shard_map/sub | solution.py:26
  61.4 5.9 %convolution_convert_fusion = bf16[256,640]{1,0:T(8,128)(2,1)S(1)} fusion(bf16[256,5120]{1,0:T(8,128)(2,1)} %all-gather.2.cloned.1.call-done, bf16[640,5120]{1,0:T(8,128)(2,1)} %param.9), kind=kOutput, calls=%fused_computation.48 | convolution fusion | flops 1677885440 | bytes 9502720 | tf_op jit(solution)/shard_map/dot_general | solution.py:74
  67.5 6.0 %convolution_bitcast_fusion = f32[1280,5,128]{0,2,1:T(8,128)} fusion(bf16[5,256,128]{1,2,0:T(8,128)(2,1)S(1)} %bitcast.93, f32[5,256,1280]{1,2,0:T(8,128)} %get-tuple-element.18, f32[5,256]{1,0:T(8,128)S(1)} %get-tuple-element.17), kind=kOutput, calls=%fused_computation.18 | convolution fusion | flops 422707200 | bytes 10163200 | tf_op jit(solution)/shard_map/hqk,hqd->khd/dot_general | solution.py:42
  77.3 8.3 %copy.35 = f32[1280,5,128]{2,1,0:T(8,128)} copy(f32[1280,5,128]{2,0,1:T(8,128)S(1)} %fusion.5) | data formatting | bytes 6553600 | tf_op jit(solution)/shard_map/mul | solution.py:52
  85.6 3.6 %stack.19 = f32[1,5,256,640]{3,2,1,0:T(8,128)S(1)} reshape(f32[1280,5,128]{2,1,0:T(8,128)} %copy.35) | data formatting | bytes 6553600 | tf_op jit(solution)/shard_map/stack | solution.py:96
  89.2 5.1 %reshape.37 = f32[1,5,256,640]{2,1,3,0:T(8,128)} reshape(f32[1280,5,128]{0,2,1:T(8,128)} %convolution_bitcast_fusion) | data formatting | bytes 6553600 | tf_op jit(solution)/shard_map/stack | solution.py:96
  94.3 5.4 %copy.52 = f32[1,5,256,640]{3,2,1,0:T(8,128)} copy(f32[1,5,256,640]{2,1,3,0:T(8,128)} %reshape.37) | data formatting | bytes 6553600 | tf_op jit(solution)/shard_map/stack | solution.py:96
  99.7 4.2 %fusion.22 = (f32[2,256,640]{2,1,0:T(8,128)}, f32[2,256,640]{2,1,0:T(8,128)}, f32[2,256,640]{2,1,0:T(8,128)}, f32[2,256,640]{2,1,0:T(8,128)}) fusion(f32[1,5,256,640]{3,2,1,0:T(8,128)S(1)} %stack.19, f32[1,5,256,640]{3,2,1,0:T(8,128)} %copy.52), kind=kLoop, calls=%fused_computation.36 | loop fusion | flops 1310720 | bytes 11796480 | tf_op jit(solution)/shard_map/squeeze | solution.py:102
  103.9 1.9 %collective-permute-start.4 = (f32[2,256,640]{2,1,0:T(8,128)}, f32[2,256,640]{2,1,0:T(8,128)}, u32[]{:S(2)}, u32[]{:S(2)}) collective-permute-start(f32[2,256,640]{2,1,0:T(8,128)} %get-tuple-element.9), channel_id=1, source_target_pairs={{4,0},{8,4},{12,8},{16,12},{20,16},{24,20},{28,24},{5,1},{9,5},{13... | collective-permute-start | bytes 3932168 | tf_op jit(solution)/shard_map/ppermute | solution.py:16
  105.8 3.9 %collective-permute-start.5 = (f32[2,256,640]{2,1,0:T(8,128)}, f32[2,256,640]{2,1,0:T(8,128)}, u32[]{:S(2)}, u32[]{:S(2)}) collective-permute-start(f32[2,256,640]{2,1,0:T(8,128)} %get-tuple-element.10), channel_id=1, source_target_pairs={{0,4},{4,8},{8,12},{12,16},{16,20},{20,24},{24,28},{1,5},{5,9},{9,... | collective-permute-start | bytes 3932168 | tf_op jit(solution)/shard_map/ppermute | solution.py:16
  109.8 1.9 %collective-permute-start.7 = (f32[2,256,640]{2,1,0:T(8,128)}, f32[2,256,640]{2,1,0:T(8,128)}, u32[]{:S(2)}, u32[]{:S(2)}) collective-permute-start(f32[2,256,640]{2,1,0:T(8,128)} %get-tuple-element.11), channel_id=1, source_target_pairs={{0,8},{4,12},{8,16},{12,20},{16,24},{20,28},{1,9},{5,13},{9,17},{1... | collective-permute-start | bytes 3932168 | tf_op jit(solution)/shard_map/ppermute | solution.py:16
  111.7 5.1 %collective-permute-start.6 = (f32[2,256,640]{2,1,0:T(8,128)}, f32[2,256,640]{2,1,0:T(8,128)}, u32[]{:S(2)}, u32[]{:S(2)}) collective-permute-start(f32[2,256,640]{2,1,0:T(8,128)} %get-tuple-element.12), channel_id=1, source_target_pairs={{8,0},{12,4},{16,8},{20,12},{24,16},{28,20},{9,1},{13,5},{17,9},{2... | collective-permute-start | bytes 3932168 | tf_op jit(solution)/shard_map/ppermute | solution.py:16
  116.8 1.4 fusion.29
  118.2 1.9 %copy.42 = bf16[256,640]{1,0:T(8,128)(2,1)} copy(bf16[256,640]{0,1:T(8,128)(2,1)} %bitcast.96) | data formatting | bytes 655360
  120.0 42.9 %collective-permute-done.4 = f32[2,256,640]{2,1,0:T(8,128)} collective-permute-done((f32[2,256,640]{2,1,0:T(8,128)}, f32[2,256,640]{2,1,0:T(8,128)}, u32[]{:S(2)}, u32[]{:S(2)}) %collective-permute-start.4) | collective-permute-done | bytes 1310752 | tf_op jit(solution)/shard_map/ppermute | solution.py:16
  163.0 2.9 %fusion.20 = bf16[2,256,640]{2,1,0:T(8,128)(2,1)S(1)} fusion(f32[2,256,640]{2,1,0:T(8,128)} %collective-permute-done.7, f32[2,256,640]{2,1,0:T(8,128)} %collective-permute-done.6, f32[2,256,640]{2,1,0:T(8,128)} %collective-permute-done.5, f32[2,256,640]{2,1,0:T(8,128)} %collective-permute-done.4, f32[1,5,256,640]{3,2,1,0:T(8,128)S(1)} %stack.19, ...), kind=kLoop, calls=%fused_computation.34 | loop fusion | flops 1966080 | bytes 12451840 | tf_op jit(solution)/shard_map/convert.1
  (43 shorter events, 13.2 us)
Async XLA Ops:
  7.2 16.0 %copy-start.5 = (bf16[256,640]{1,0:T(8,128)(2,1)S(1)}, bf16[256,640]{1,0:T(8,128)(2,1)}, u32[]{:S(2)}) copy-start(bf16[256,640]{1,0:T(8,128)(2,1)} %param.6) | copy-start | bytes 983044
  7.2 54.2 %all-gather.2.cloned.1.call-start = ((), (), s32[]{:S(2)}) async-start(), calls=%async_computation | async-start | bytes 3276800 | tf_op jit(solution)/shard_map/all_gather | solution.py:75
  10.3 18.5 %collective-permute-start = (bf16[2,256,640]{1,2,0:T(8,128)(2,1)S(1)}, bf16[2,256,640]{1,2,0:T(8,128)(2,1)}, u32[]{:S(2)}, u32[]{:S(2)}) collective-permute-start(bf16[2,256,640]{1,2,0:T(8,128)(2,1)S(1)} %pad_maximum_fusion.1), channel_id=1, source_target_pairs={{0,8},{4,12},{8,16},{12,20},{16,24},{20,28},{1,9},{5,13},{9,17},{1... | collective-permute-start | bytes 1966088 | tf_op jit(solution)/shard_map/ppermute | solution.py:16
  13.8 30.1 %collective-permute-start.1 = (bf16[2,256,640]{1,2,0:T(8,128)(2,1)S(1)}, bf16[2,256,640]{1,2,0:T(8,128)(2,1)}, u32[]{:S(2)}, u32[]{:S(2)}) collective-permute-start(bf16[2,256,640]{1,2,0:T(8,128)(2,1)S(1)} %pad_maximum_fusion.1), channel_id=1, source_target_pairs={{0,4},{4,8},{8,12},{12,16},{16,20},{20,24},{24,28},{1,5},{5,9},{9,... | collective-permute-start | bytes 1966088 | tf_op jit(solution)/shard_map/ppermute | solution.py:16
  17.2 36.9 %collective-permute-start.3 = (bf16[2,256,640]{1,2,0:T(8,128)(2,1)S(1)}, bf16[2,256,640]{1,2,0:T(8,128)(2,1)S(1)}, u32[]{:S(2)}, u32[]{:S(2)}) collective-permute-start(bf16[2,256,640]{1,2,0:T(8,128)(2,1)S(1)} %pad_maximum_fusion.1), channel_id=1, source_target_pairs={{8,0},{12,4},{16,8},{20,12},{24,16},{28,20},{9,1},{13,5},{17,9},{2... | collective-permute-start | bytes 1966088 | tf_op jit(solution)/shard_map/ppermute | solution.py:16
  21.2 31.7 %collective-permute-start.2 = (bf16[2,256,640]{1,2,0:T(8,128)(2,1)S(1)}, bf16[2,256,640]{1,2,0:T(8,128)(2,1)}, u32[]{:S(2)}, u32[]{:S(2)}) collective-permute-start(bf16[2,256,640]{1,2,0:T(8,128)(2,1)S(1)} %pad_maximum_fusion.1), channel_id=1, source_target_pairs={{4,0},{8,4},{12,8},{16,12},{20,16},{24,20},{28,24},{5,1},{9,5},{13... | collective-permute-start | bytes 1966088 | tf_op jit(solution)/shard_map/ppermute | solution.py:16
  55.5 5.9 %copy-start.2 = (bf16[1,1280,640]{1,2,0:T(8,128)(2,1)}, bf16[1,1280,640]{1,2,0:T(8,128)(2,1)S(1)}, u32[]{:S(2)}) copy-start(bf16[1,1280,640]{1,2,0:T(8,128)(2,1)S(1)} %get-tuple-element.14) | copy-start | bytes 4915204
  67.3 6.2 %slice-start = ((s8[6553600]{0:T(1024)(128)(4,1)}), s8[2359296]{0:T(1024)(128)(4,1)S(1)}, s32[]{:S(2)}) async-start(s8[6553600]{0:T(1024)(128)(4,1)} %bitcast.82), calls=%async_computation.1 | async-start | bytes 4718592
  67.5 6.0 %slice-start.1 = ((s8[6553600]{0:T(1024)(128)(4,1)}), s8[4194304]{0:T(1024)(128)(4,1)S(1)}, s32[]{:S(2)}) async-start(s8[6553600]{0:T(1024)(128)(4,1)} %bitcast.82), calls=%async_computation.2 | async-start | bytes 8388608
  67.5 6.0 %copy-start.4 = (bf16[1,1280,640]{1,2,0:T(8,128)(2,1)S(1)}, bf16[1,1280,640]{1,2,0:T(8,128)(2,1)}, u32[]{:S(2)}) copy-start(bf16[1,1280,640]{1,2,0:T(8,128)(2,1)} %get-tuple-element.13) | copy-start | bytes 4915204
  75.6 1.7 copy-start
  99.7 17.1 %copy-start.1 = (bf16[5,256,1280]{1,2,0:T(8,128)(2,1)S(1)}, bf16[5,256,1280]{1,2,0:T(8,128)(2,1)}, u32[]{:S(2)}) copy-start(bf16[5,256,1280]{1,2,0:T(8,128)(2,1)} %copy-done) | copy-start | bytes 9830404
  99.7 17.1 %copy-start.3 = (bf16[1,1280,640]{1,2,0:T(8,128)(2,1)S(1)}, bf16[1,1280,640]{1,2,0:T(8,128)(2,1)}, u32[]{:S(2)}) copy-start(bf16[1,1280,640]{1,2,0:T(8,128)(2,1)} %copy-done.2) | copy-start | bytes 4915204
  103.9 59.0 %collective-permute-start.4 = (f32[2,256,640]{2,1,0:T(8,128)}, f32[2,256,640]{2,1,0:T(8,128)}, u32[]{:S(2)}, u32[]{:S(2)}) collective-permute-start(f32[2,256,640]{2,1,0:T(8,128)} %get-tuple-element.9), channel_id=1, source_target_pairs={{4,0},{8,4},{12,8},{16,12},{20,16},{24,20},{28,24},{5,1},{9,5},{13... | collective-permute-start | bytes 3932168 | tf_op jit(solution)/shard_map/ppermute | solution.py:16
  105.8 57.1 %collective-permute-start.5 = (f32[2,256,640]{2,1,0:T(8,128)}, f32[2,256,640]{2,1,0:T(8,128)}, u32[]{:S(2)}, u32[]{:S(2)}) collective-permute-start(f32[2,256,640]{2,1,0:T(8,128)} %get-tuple-element.10), channel_id=1, source_target_pairs={{0,4},{4,8},{8,12},{12,16},{16,20},{20,24},{24,28},{1,5},{5,9},{9,... | collective-permute-start | bytes 3932168 | tf_op jit(solution)/shard_map/ppermute | solution.py:16
  109.8 53.2 %collective-permute-start.7 = (f32[2,256,640]{2,1,0:T(8,128)}, f32[2,256,640]{2,1,0:T(8,128)}, u32[]{:S(2)}, u32[]{:S(2)}) collective-permute-start(f32[2,256,640]{2,1,0:T(8,128)} %get-tuple-element.11), channel_id=1, source_target_pairs={{0,8},{4,12},{8,16},{12,20},{16,24},{20,28},{1,9},{5,13},{9,17},{1... | collective-permute-start | bytes 3932168 | tf_op jit(solution)/shard_map/ppermute | solution.py:16
  111.7 51.3 %collective-permute-start.6 = (f32[2,256,640]{2,1,0:T(8,128)}, f32[2,256,640]{2,1,0:T(8,128)}, u32[]{:S(2)}, u32[]{:S(2)}) collective-permute-start(f32[2,256,640]{2,1,0:T(8,128)} %get-tuple-element.12), channel_id=1, source_target_pairs={{8,0},{12,4},{16,8},{20,12},{24,16},{28,20},{9,1},{13,5},{17,9},{2... | collective-permute-start | bytes 3932168 | tf_op jit(solution)/shard_map/ppermute | solution.py:16
Sparse Core Ops, SparseCore 0:
  9.6 26.7 all-gather.1
where the time goes:
time: 176 us; the launch traced here: 174 us
  waiting for transfers between devices  69.2 us (39%)
  local copies, waits for them, and re-layouts  34.3 us (19%)
  starting transfers between devices  25.7 us (15%)
  matrix products  22.1 us (13%)
  between operations  14.3 us (8%)
  other arithmetic  7.97 us (5%)
    ppermute x8, waiting for transfers between devices, from_behind(): return lax.ppermute(array, axis, pairs)  68.5 us
    ppermute x8, starting transfers between devices, from_behind(): return lax.ppermute(array, axis, pairs)  25.7 us
    another operation x3, local copies, waits for them, and re-layouts, local(): jnp.stack([grad_key_win.reshape(window_len, feat_width), grad_value_win.r...  14.1 us
    unnamed x24, local copies, waits for them, and re-layouts  8.57 us
    mul x1, local copies, waits for them, and re-layouts, attend_local(): jnp.einsum('hqk,qhd->khd', dscores, query_blk, preferred_element_type=jnp...  8.34 us
    dot_general x1, matrix products, attend_local(): jnp.einsum('hqk,hqd->khd', probs.astype(jnp.bfloat16), grad_heads, prefer...  5.96 us
    dot_general x1, matrix products, local(): lax.dot_general(lax.all_gather(reward_grad, 'head', axis=1, tiled=True),...  5.88 us
    sub x1, matrix products, attend_local(): weights = jnp.where(live_three, jnp.exp(scores - row_max), 0.0)  5.87 us
  transfers between devices with their start and end apart: 9, of which 4 were waited for; matrix products, arithmetic and copies ran while one was open for 10% of the time, Pallas kernels for 0%

commit v1 on v0

v1 whole, which is shorter than its diff:
```python
import functools
import math

import jax
import jax.numpy as jnp
from jax import lax
from jax.experimental import pallas as pl
from jax.experimental.pallas import tpu as pltpu
from jax.sharding import PartitionSpec as P

HEAD_DIM = 128
TILE = 128
SPAN = 2
STAT_ROWS = 16
SCALE = 1.0 / math.sqrt(HEAD_DIM)
SCALE_LOG2 = SCALE * math.log2(math.e)
BOTH = ("ctx", "head")
NT = (((1,), (1,)), ((), ()))
TN = (((0,), (0,)), ((), ()))
NN = (((1,), (0,)), ((), ()))
VMEM_LIMIT = 48 * 1024 * 1024


def dot(a, b, dims):
    return lax.dot_general(a, b, dims, preferred_element_type=jnp.float32)


def send(array, rule):
    n_ctx, n_head = lax.axis_size("ctx"), lax.axis_size("head")
    pairs = []
    for c in range(n_ctx):
        for h in range(n_head):
            to = rule(c, h)
            if to is not None and 0 <= to[0] < n_ctx:
                pairs.append((c * n_head + h, to[0] * n_head + to[1]))
    return lax.ppermute(array, BOTH, pairs)


def pair_up(c, h):
    return (c ^ 1, h)


def upward(c, h):
    return (c + 2, h)


def downward(c, h):
    return (c - 2, h)


def across(c, h):
    return (c + 1, h) if c & 1 else (c - 1, h)


def forward(c, h):
    if h & 1:
        return (c ^ 1, h)
    return (c - 2, h) if c & 1 else (c + 2, h)


def after(value, *others):
    return lax.optimization_barrier((value,) + others)[0]


def matmul_kernel(first, last, order_ref, w_a, w_b, g_a, g_b, *rest):
    if first:
        out_ref, acc_ref = rest
    else:
        begin_ref, out_ref, acc_ref = rest
    step = pl.program_id(0)
    part = dot(w_a[...], g_a[...], NT) + dot(w_b[...], g_b[...], NT)

    @pl.when(step == 0)
    def _():
        acc_ref[...] = part if first else part + begin_ref[...]

    @pl.when(step > 0)
    def _():
        acc_ref[...] += part

    @pl.when(step == pl.num_programs(0) - 1)
    def _():
        out_ref[...] = acc_ref[...].astype(out_ref.dtype)


def partial_out(order, out_weight, g_a, g_b, begin, dtype):
    feat, width = out_weight.shape
    rows, cols = g_a.shape
    steps = 5
    block = cols // steps
    first = begin is None
    in_specs = [
        pl.BlockSpec((feat, block), lambda s, o: (0, o[0] * steps + s)),
        pl.BlockSpec((feat, block), lambda s, o: (0, o[1] * steps + s)),
        pl.BlockSpec((rows, block), lambda s, o: (0, s)),
        pl.BlockSpec((rows, block), lambda s, o: (0, s)),
    ]
    args = [order, out_weight, out_weight, g_a, g_b]
    if not first:
        in_specs.append(pl.BlockSpec((feat, rows), lambda s, o: (0, 0)))
        args.append(begin)
    return pl.pallas_call(
        functools.partial(matmul_kernel, first, not first),
        grid_spec=pltpu.PrefetchScalarGridSpec(
            num_scalar_prefetch=1,
            grid=(steps,),
            in_specs=in_specs,
            out_specs=pl.BlockSpec((feat, rows), lambda s, o: (0, 0)),
            scratch_shapes=[pltpu.VMEM((feat, rows), jnp.float32)],
        ),
        out_shape=jax.ShapeDtypeStruct((feat, rows), dtype),
        compiler_params=pltpu.CompilerParams(vmem_limit_bytes=VMEM_LIMIT),
        cost_estimate=pl.CostEstimate(
            flops=4 * feat * rows * cols, bytes_accessed=4 * feat * cols, transcendentals=0
        ),
    )(*args)


def bias_row(live_flags):
    parts = [
        jnp.full((1, TILE), jnp.where(flag, 0.0, -jnp.inf).astype(jnp.float32))
        for flag in live_flags
    ]
    return jnp.concatenate(parts, axis=1)


def query_kernel(pos_ref, mask_ref, q_ref, k_ref, v_ref, kx, vx, kg, vg, ku, vu, kd, vd, d_ref,
                 dq_ref, send_ref):
    pos = pos_ref[0]
    rows = q_ref.shape[0]
    tiles = rows // TILE
    pair_off = 1 - 2 * lax.rem(pos, 2)
    blocks = [
        (k_ref, v_ref, 0), (kx, vx, pair_off), (ku, vu, -2), (kd, vd, 2), (kg, vg, -pair_off)
    ]
    q = q_ref[...]
    shifted = []
    top = None
    for keys, _, off in blocks:
        scores = dot(keys[...], q, NT)
        for b in range(tiles):
            column = (off + SPAN) * tiles + b
            flags = [mask_ref[pos * tiles + a, column] > 0 for a in range(tiles)]
            value = scores[b * TILE:(b + 1) * TILE] * SCALE_LOG2 + bias_row(flags)
            shifted.append(value)
            peak = jnp.max(value, axis=0, keepdims=True)
            top = peak if top is None else jnp.maximum(top, peak)
    weights = []
    totals = None
    for value in shifted:
        weight = jnp.exp2(value - top)
        weights.append(weight)
        part = jnp.sum(weight, axis=0, keepdims=True)
        totals = part if totals is None else totals + part
    out = None
    for n, (_, values, _) in enumerate(blocks):
        w = jnp.concatenate(weights[n * tiles:(n + 1) * tiles], axis=0)
        part = dot(values[...], w.astype(jnp.bfloat16), TN)
        out = part if out is None else out + part
    inverse = 1.0 / totals
    attn_out = (out / totals).astype(jnp.bfloat16).astype(jnp.float32)
    grad = d_ref[...]
    delta = jnp.sum(grad.astype(jnp.float32) * attn_out, axis=0, keepdims=True)
    dq = None
    for n, (keys, values, _) in enumerate(blocks):
        w = jnp.concatenate(weights[n * tiles:(n + 1) * tiles], axis=0)
        dprobs = dot(values[...], grad, NN)
        dscores = (w * inverse * (dprobs - delta)).astype(jnp.bfloat16)
        part = dot(keys[...], dscores, TN)
        dq = part if dq is None else dq + part
    dq_ref[...] = jnp.transpose(dq * SCALE).astype(dq_ref.dtype)
    lse = top + jnp.log2(totals)
    pieces = []
    for stat in (lse, delta):
        for _ in range(3):
            piece = stat.astype(jnp.bfloat16).astype(jnp.float32)
            pieces.append(piece)
            stat = stat - piece
    row = lax.broadcasted_iota(jnp.int32, (STAT_ROWS, rows), 0)
    stats = jnp.zeros((STAT_ROWS, rows), jnp.float32)
    for n, piece in enumerate(pieces):
        stats = jnp.where(row == n, piece, stats)
    send_ref[:HEAD_DIM, :] = grad
    send_ref[HEAD_DIM:, :] = stats.astype(jnp.bfloat16)


def query_side(pos, tile_mask, queries, keys, values, windows, d_out_t):
    rows, feat = queries.shape
    heads = feat // HEAD_DIM
    own = pl.BlockSpec((rows, HEAD_DIM), lambda h, *_: (0, h))
    second = pl.BlockSpec((rows, HEAD_DIM), lambda h, *_: (1, h))
    in_specs = [own, own, own]
    args = [queries, keys, values]
    for window in windows:
        in_specs += [own, second]
        args += [window, window]
    in_specs.append(pl.BlockSpec((HEAD_DIM, rows), lambda h, *_: (h, 0)))
    args.append(d_out_t)
    packed = HEAD_DIM + STAT_ROWS
    return pl.pallas_call(
        query_kernel,
        grid_spec=pltpu.PrefetchScalarGridSpec(
            num_scalar_prefetch=2,
            grid=(heads,),
            in_specs=in_specs,
            out_specs=[own, pl.BlockSpec((packed, rows), lambda h, *_: (h, 0))],
        ),
        out_shape=[
            jax.ShapeDtypeStruct((rows, feat), jnp.bfloat16),
            jax.ShapeDtypeStruct((heads * packed, rows), jnp.bfloat16),
        ],
        compiler_params=pltpu.CompilerParams(vmem_limit_bytes=VMEM_LIMIT),
        cost_estimate=pl.CostEstimate(
            flops=2 * 4 * 5 * rows * rows * feat, bytes_accessed=2 * 15 * rows * feat,
            transcendentals=5 * rows * rows * heads,
        ),
    )(pos, tile_mask, *args)


def key_kernel(offsets, pos_ref, mask_ref, k_ref, v_ref, *rest):
    count = len(offsets)
    pairs = [(rest[2 * n], rest[2 * n + 1]) for n in range(count)]
    dk_ref, dv_ref = rest[2 * count:]
    pos = pos_ref[0]
    rows = k_ref.shape[0]
    tiles = rows // TILE
    total_tiles = mask_ref.shape[0]
    pair_off = 1 - 2 * lax.rem(pos, 2)
    keys, values = k_ref[...], v_ref[...]
    dk = dv = None
    for (q_ref, packed), offset in zip(pairs, offsets):
        off = {"pair": pair_off, "across": -pair_off}.get(offset, offset)
        q = q_ref[...]
        grad = packed[:HEAD_DIM, :]
        stats = packed[HEAD_DIM:, :].astype(jnp.float32)
        lse = stats[0:1] + stats[1:2] + stats[2:3]
        delta = stats[3:4] + stats[4:5] + stats[5:6]
        scores = dot(keys, q, NT)
        probs = []
        for b in range(tiles):
            flags = []
            for a in range(tiles):
                tile = (pos + off) * tiles + a
                inside = (tile >= 0) & (tile < total_tiles)
                column = (SPAN - off) * tiles + b
                flags.append(inside & (mask_ref[jnp.clip(tile, 0, total_tiles - 1), column] > 0))
            shift = bias_row(flags) - lse
            probs.append(jnp.exp2(scores[b * TILE:(b + 1) * TILE] * SCALE_LOG2 + shift))
        probs = jnp.concatenate(probs, axis=0)
        dv_part = dot(probs.astype(jnp.bfloat16), grad, NT)
        dprobs = dot(values, grad, NN)
        dscores = (probs * (dprobs - delta)).astype(jnp.bfloat16)
        dk_part = dot(dscores, q, NN)
        dk = dk_part if dk is None else dk + dk_part
        dv = dv_part if dv is None else dv + dv_part
    dk_ref[...] = (dk * SCALE).astype(dk_ref.dtype)
    dv_ref[...] = dv.astype(dv_ref.dtype)


def key_side(pos, tile_mask, keys, values, sources):
    rows, feat = keys.shape
    heads = feat // HEAD_DIM
    own = pl.BlockSpec((rows, HEAD_DIM), lambda h, *_: (0, h))
    packed = pl.BlockSpec((HEAD_DIM + STAT_ROWS, rows), lambda h, *_: (h, 0))
    in_specs = [own, own]
    args = [keys, values]
    for q, p, _ in sources:
        in_specs += [own, packed]
        args += [q, p]
    return pl.pallas_call(
        functools.partial(key_kernel, [offset for _, _, offset in sources]),
        grid_spec=pltpu.PrefetchScalarGridSpec(
            num_scalar_prefetch=2,
            grid=(heads,),
            in_specs=in_specs,
            out_specs=[own, own],
        ),
        out_shape=[jax.ShapeDtypeStruct((rows, feat), jnp.bfloat16)] * 2,
        compiler_params=pltpu.CompilerParams(vmem_limit_bytes=VMEM_LIMIT),
        cost_estimate=pl.CostEstimate(
            flops=2 * 4 * 5 * rows * rows * feat, bytes_accessed=2 * 14 * rows * feat,
            transcendentals=5 * rows * rows * heads,
        ),
    )(pos, tile_mask, *args)


def local(queries, keys, values, out_weight, reward_grad, tile_mask):
    ctx = lax.axis_index("ctx").astype(jnp.int32)
    head = lax.axis_index("head").astype(jnp.int32)
    pos = ctx.reshape(1)

    far = send(reward_grad, lambda c, h: (c, h ^ 2))
    near = send(reward_grad, lambda c, h: (c, h ^ 1))
    kv = jnp.concatenate([keys, values], axis=0)
    kv_x = send(kv, pair_up)
    kv_u = send(kv, upward)
    kv_d = send(kv, downward)
    begun = partial_out(
        jnp.stack([head, head ^ 1]), out_weight, reward_grad, near, None, jnp.float32
    )

    def second_step(x, u, d):
        held = jnp.where(ctx % 2 == 1, u, d)
        return send(jnp.where(head % 2 == 1, held, x), forward)

    kv_g = second_step(kv_x, kv_u, kv_d)
    far_near = send(far, lambda c, h: (c, h ^ 1))
    queries_late = after(queries, kv_x, kv_u, kv_d)
    q_x = send(queries_late, pair_up)
    q_u = send(queries_late, upward)
    q_d = send(queries_late, downward)
    d_out_t = partial_out(
        jnp.stack([head ^ 2, head ^ 3]), out_weight, far, far_near, begun, jnp.bfloat16
    )
    grad_queries, packed = query_side(
        pos, tile_mask, queries, keys, values, [kv_x, kv_g, kv_u, kv_d], d_out_t
    )
    q_g = second_step(q_x, q_u, q_d)
    p_g = send(packed, across)
    p_x = send(packed, pair_up)
    p_u = send(packed, upward)
    p_d = send(packed, downward)
    grad_keys, grad_values = key_side(
        pos,
        tile_mask,
        keys,
        values,
        [
            (queries, packed, 0),
            (q_x, p_x, "pair"),
            (q_u, p_u, -2),
            (q_d, p_d, 2),
            (q_g, p_g, "across"),
        ],
    )
    return (grad_queries, grad_keys, grad_values)


def solution(mesh):
    placed = (
        P("ctx", "head"),
        P("ctx", "head"),
        P("ctx", "head"),
        P("head", None),
        P("ctx", "head"),
        P(),
    )
    return jax.shard_map(
        local,
        mesh=mesh,
        in_specs=placed,
        out_specs=(P("ctx", "head"), P("ctx", "head"), P("ctx", "head")),
        check_vma=False,
    )
```

time: 176 us -> 88 us (0.50)
  the two profiles are of different devices: /device:TPU:8 before, /device:TPU:11 now
where the time goes in v1:
time: 88 us; the launch traced here: 87.4 us
  starting transfers between devices  30.6 us (35%)
  Pallas kernels  27.4 us (31%)
  waiting for transfers between devices  24.2 us (28%)
  local copies, waits for them, and re-layouts  3.13 us (4%)
  other arithmetic  1.16 us (1%)
    ppermute x15, starting transfers between devices, send(): return lax.ppermute(array, BOTH, pairs)  30.6 us
    ppermute x15, waiting for transfers between devices, send(): return lax.ppermute(array, BOTH, pairs)  24.2 us
    pallas_call x2, Pallas kernels, partial_out(): pl.pallas_call(functools.partial(matmul_kernel, first, not first), grid_s...  10.6 us
    pallas_call x1, Pallas kernels, query_side(): pl.pallas_call(query_kernel, grid_spec=pltpu.PrefetchScalarGridSpec(num_s...  10 us
    pallas_call x1, Pallas kernels, key_side(): pl.pallas_call(functools.partial(key_kernel, [offset for _, _, offset in...  6.76 us
    unnamed x11, local copies, waits for them, and re-layouts  2.11 us
  transfers between devices with their start and end apart: 15, of which 5 were waited for; matrix products, arithmetic and copies ran while one was open for 4% of the time, Pallas kernels for 24%

profile of v1, /device:TPU:11, one launch (start us, length us, event | category | flops | bytes accessed | tf_op | source)
XLA Modules:
  0.0 87.4 jit_solution(7983975746847945049)
XLA Ops:
  0.6 1.3 %collective-permute-start.4 = (bf16[256,1280]{1,0:T(8,128)(2,1)}, bf16[256,1280]{1,0:T(8,128)(2,1)S(1)}, u32[]{:S(2)}, u32[]{:S(2)}) collective-permute-start(bf16[256,1280]{1,0:T(8,128)(2,1)} %g_a.1), channel_id=1, source_target_pairs={{0,2},{1,3},{2,0},{3,1},{4,6},{5,7},{6,4},{7,5},{8,10},{9,11},{10,... | collective-permute-start | bytes 1966088 | tf_op jit(solution)/shard_map/ppermute | solution.py:36
  2.9 1.0 %constant_dynamic-update-slice_fusion = bf16[512,640]{1,0:T(8,128)(2,1)S(1)} fusion(bf16[512,640]{1,0:T(8,128)(2,1)S(1)} %constant_dynamic-update-slice_fusion.1, bf16[256,640]{1,0:T(8,128)(2,1)} %v_ref.3), kind=kLoop, calls=%fused_computation.2 | loop fusion | bytes 655360 | tf_op jit(solution)/shard_map/concatenate | solution.py:294
  4.3 3.2 %collective-permute-start.1 = (bf16[512,640]{1,0:T(8,128)(2,1)S(1)}, bf16[512,640]{1,0:T(8,128)(2,1)S(1)}, u32[]{:S(2)}, u32[]{:S(2)}) collective-permute-start(bf16[512,640]{1,0:T(8,128)(2,1)S(1)} %constant_dynamic-update-slice_fusion), channel_id=1, source_target_pairs={{0,8},{1,9},{2,10},{3,11},{4,12},{5,13},{6,14},{7,15},{8,16},{9,17... | collective-permute-start | bytes 1966088 | tf_op jit(solution)/shard_map/ppermute | solution.py:36
  7.5 2.1 %collective-permute-start.2 = (bf16[512,640]{1,0:T(8,128)(2,1)S(1)}, bf16[512,640]{1,0:T(8,128)(2,1)S(1)}, u32[]{:S(2)}, u32[]{:S(2)}) collective-permute-start(bf16[512,640]{1,0:T(8,128)(2,1)S(1)} %constant_dynamic-update-slice_fusion), channel_id=1, source_target_pairs={{8,0},{9,1},{10,2},{11,3},{12,4},{13,5},{14,6},{15,7},{16,8},{17,9... | collective-permute-start | bytes 1966088 | tf_op jit(solution)/shard_map/ppermute | solution.py:36
  9.6 1.9 %collective-permute-start.6 = (bf16[256,1280]{1,0:T(8,128)(2,1)}, bf16[256,1280]{1,0:T(8,128)(2,1)}, u32[]{:S(2)}, u32[]{:S(2)}) collective-permute-start(bf16[256,1280]{1,0:T(8,128)(2,1)} %g_a.1), channel_id=1, source_target_pairs={{0,1},{1,0},{2,3},{3,2},{4,5},{5,4},{6,7},{7,6},{8,9},{9,8},{10,11... | collective-permute-start | bytes 1966088 | tf_op jit(solution)/shard_map/ppermute | solution.py:36
  11.5 5.0 %collective-permute-done.4.g_a = bf16[256,1280]{1,0:T(8,128)(2,1)S(1)} collective-permute-done((bf16[256,1280]{1,0:T(8,128)(2,1)}, bf16[256,1280]{1,0:T(8,128)(2,1)S(1)}, u32[]{:S(2)}, u32[]{:S(2)}) %collective-permute-start.4) | collective-permute-done | bytes 655392 | tf_op jit(solution)/shard_map/ppermute | solution.py:36
  16.5 1.5 %collective-permute-start.5 = (bf16[256,1280]{1,0:T(8,128)(2,1)S(1)}, bf16[256,1280]{1,0:T(8,128)(2,1)}, u32[]{:S(2)}, u32[]{:S(2)}) collective-permute-start(bf16[256,1280]{1,0:T(8,128)(2,1)S(1)} %collective-permute-done.4.g_a), channel_id=1, source_target_pairs={{0,1},{1,0},{2,3},{3,2},{4,5},{5,4},{6,7},{7,6},{8,9},{9,8},{10,11... | collective-permute-start | bytes 1966088 | tf_op jit(solution)/shard_map/ppermute | solution.py:36
  18.1 1.3 %collective-permute-done.kx.vx = bf16[512,640]{1,0:T(8,128)(2,1)S(1)} collective-permute-done((bf16[512,640]{1,0:T(8,128)(2,1)S(1)}, bf16[512,640]{1,0:T(8,128)(2,1)S(1)}, u32[]{:S(2)}, u32[]{:S(2)}) %collective-permute-start) | collective-permute-done | bytes 655392 | tf_op jit(solution)/shard_map/ppermute | solution.py:36
  19.3 1.8 %collective-permute-done.1.ku.vu = bf16[512,640]{1,0:T(8,128)(2,1)S(1)} collective-permute-done((bf16[512,640]{1,0:T(8,128)(2,1)S(1)}, bf16[512,640]{1,0:T(8,128)(2,1)S(1)}, u32[]{:S(2)}, u32[]{:S(2)}) %collective-permute-start.1) | collective-permute-done | bytes 655392 | tf_op jit(solution)/shard_map/ppermute | solution.py:36
  21.1 2.9 %collective-permute-done.2.kd.vd = bf16[512,640]{1,0:T(8,128)(2,1)S(1)} collective-permute-done((bf16[512,640]{1,0:T(8,128)(2,1)S(1)}, bf16[512,640]{1,0:T(8,128)(2,1)S(1)}, u32[]{:S(2)}, u32[]{:S(2)}) %collective-permute-start.2) | collective-permute-done | bytes 655392 | tf_op jit(solution)/shard_map/ppermute | solution.py:36
  25.0 3.1 %collective-permute-start.3 = (bf16[512,640]{1,0:T(8,128)(2,1)}, bf16[512,640]{1,0:T(8,128)(2,1)S(1)}, u32[]{:S(2)}, u32[]{:S(2)}) collective-permute-start(bf16[512,640]{1,0:T(8,128)(2,1)} %select_select_fusion), channel_id=1, source_target_pairs={{0,8},{1,5},{2,10},{3,7},{5,1},{7,3},{8,16},{9,13},{10,18},{11,15}... | collective-permute-start | bytes 1966088 | tf_op jit(solution)/shard_map/ppermute | solution.py:36
  28.5 3.2 %collective-permute-start.9 = (bf16[256,640]{1,0:T(8,128)(2,1)}, bf16[256,640]{1,0:T(8,128)(2,1)S(1)}, u32[]{:S(2)}, u32[]{:S(2)}) collective-permute-start(bf16[256,640]{1,0:T(8,128)(2,1)} %rest_0_.1), channel_id=1, source_target_pairs={{0,8},{1,9},{2,10},{3,11},{4,12},{5,13},{6,14},{7,15},{8,16},{9,17... | collective-permute-start | bytes 983048 | tf_op jit(solution)/shard_map/ppermute | solution.py:36
  31.7 2.1 %collective-permute-start.11 = (bf16[256,640]{1,0:T(8,128)(2,1)}, bf16[256,640]{1,0:T(8,128)(2,1)S(1)}, u32[]{:S(2)}, u32[]{:S(2)}) collective-permute-start(bf16[256,640]{1,0:T(8,128)(2,1)} %rest_0_.1), channel_id=1, source_target_pairs={{8,0},{9,1},{10,2},{11,3},{12,4},{13,5},{14,6},{15,7},{16,8},{17,9... | collective-permute-start | bytes 983048 | tf_op jit(solution)/shard_map/ppermute | solution.py:36
  33.9 1.1 %copy-done.2 = bf16[256,1280]{1,0:T(8,128)(2,1)S(1)} copy-done((bf16[256,1280]{1,0:T(8,128)(2,1)S(1)}, bf16[256,1280]{1,0:T(8,128)(2,1)}, u32[]{:S(2)}) %copy-start.2) | copy-done | bytes 655384
  35.0 5.3 %shard_map.85.rest_0_ = f32[640,256]{1,0:T(8,128)S(1)} custom-call(s32[2]{0:T(128)S(1)} %pad_add_fusion.1.order_ref, bf16[640,5120]{1,0:T(8,128)(2,1)} %w_b.3, bf16[640,5120]{1,0:T(8,128)(2,1)} %w_b.3, bf16[256,1280]{1,0:T(8,128)(2,1)S(1)} %copy-done.2, bf16[256,1280]{1,0:T(8,128)(2,1)} %collective-permute-done.6.g_b), custom_call_target="tpu_custom_call" | custom-call | flops 838860800 | bytes 3276800 | tf_op jit(solution)/shard_map/pallas_call | solution.py:102
  40.3 5.3 %shard_map.86.d_ref = bf16[640,256]{1,0:T(8,128)(2,1)S(1)} custom-call(s32[2]{0:T(128)S(1)} %pad_add_fusion.order_ref, bf16[640,5120]{1,0:T(8,128)(2,1)} %w_b.3, bf16[640,5120]{1,0:T(8,128)(2,1)} %w_b.3, bf16[256,1280]{1,0:T(8,128)(2,1)S(1)} %collective-permute-done.4.g_a, bf16[256,1280]{1,0:T(8,128)(2,1)} %collective-permute-done.5.g_b, ...), custom_call_target="tpu_custom_call" | custom-call | flops 838860800 | bytes 3276800 | tf_op jit(solution)/shard_map/pallas_call | solution.py:102
  45.7 10.0 %shard_map.87 = (bf16[256,640]{1,0:T(8,128)(2,1)}, bf16[720,256]{1,0:T(8,128)(2,1)S(1)}) custom-call(s32[1]{0:T(128)} %bitcast.pos_ref, s32[16,10]{1,0:T(8,128)S(1)} %copy-done.4, bf16[256,640]{1,0:T(8,128)(2,1)S(1)} %copy-done.3, bf16[256,640]{1,0:T(8,128)(2,1)S(1)} %copy-done, bf16[256,640]{1,0:T(8,128)(2,1)S(1)} %copy-done.1, ...), custom_call_target="tpu_custom_call" | custom-call | flops 1677721600 | bytes 4915200 | tf_op jit(solution)/shard_map/pallas_call | solution.py:200
  55.8 1.2 %collective-permute-start.8 = (bf16[720,256]{1,0:T(8,128)(2,1)S(1)}, bf16[720,256]{1,0:T(8,128)(2,1)S(1)}, u32[]{:S(2)}, u32[]{:S(2)}) collective-permute-start(bf16[720,256]{1,0:T(8,128)(2,1)S(1)} %get-tuple-element.9.rest_1_), channel_id=1, source_target_pairs={{0,4},{1,5},{2,6},{3,7},{4,0},{5,1},{6,2},{7,3},{8,12},{9,13},{10,... | collective-permute-start | bytes 1105928 | tf_op jit(solution)/shard_map/ppermute | solution.py:36
  57.0 3.2 %collective-permute-start.10 = (bf16[720,256]{1,0:T(8,128)(2,1)S(1)}, bf16[720,256]{1,0:T(8,128)(2,1)S(1)}, u32[]{:S(2)}, u32[]{:S(2)}) collective-permute-start(bf16[720,256]{1,0:T(8,128)(2,1)S(1)} %get-tuple-element.9.rest_1_), channel_id=1, source_target_pairs={{0,8},{1,9},{2,10},{3,11},{4,12},{5,13},{6,14},{7,15},{8,16},{9,17... | collective-permute-start | bytes 1105928 | tf_op jit(solution)/shard_map/ppermute | solution.py:36
  60.2 2.1 %collective-permute-start.12 = (bf16[720,256]{1,0:T(8,128)(2,1)S(1)}, bf16[720,256]{1,0:T(8,128)(2,1)S(1)}, u32[]{:S(2)}, u32[]{:S(2)}) collective-permute-start(bf16[720,256]{1,0:T(8,128)(2,1)S(1)} %get-tuple-element.9.rest_1_), channel_id=1, source_target_pairs={{8,0},{9,1},{10,2},{11,3},{12,4},{13,5},{14,6},{15,7},{16,8},{17,9... | collective-permute-start | bytes 1105928 | tf_op jit(solution)/shard_map/ppermute | solution.py:36
  62.3 3.1 %collective-permute-start.14 = (bf16[720,256]{1,0:T(8,128)(2,1)S(1)}, bf16[720,256]{1,0:T(8,128)(2,1)S(1)}, u32[]{:S(2)}, u32[]{:S(2)}) collective-permute-start(bf16[720,256]{1,0:T(8,128)(2,1)S(1)} %get-tuple-element.9.rest_1_), channel_id=1, source_target_pairs={{4,8},{5,9},{6,10},{7,11},{8,4},{9,5},{10,6},{11,7},{12,16},{13,17... | collective-permute-start | bytes 1105928 | tf_op jit(solution)/shard_map/ppermute | solution.py:36
  65.5 1.9 %collective-permute-start.13 = (bf16[256,640]{1,0:T(8,128)(2,1)S(1)}, bf16[256,640]{1,0:T(8,128)(2,1)S(1)}, u32[]{:S(2)}, u32[]{:S(2)}) collective-permute-start(bf16[256,640]{1,0:T(8,128)(2,1)S(1)} %select_select_fusion.1), channel_id=1, source_target_pairs={{0,8},{1,5},{2,10},{3,7},{5,1},{7,3},{8,16},{9,13},{10,18},{11,15}... | collective-permute-start | bytes 983048 | tf_op jit(solution)/shard_map/ppermute | solution.py:36
  67.4 13.1 %collective-permute-done.13.rest_8_ = bf16[256,640]{1,0:T(8,128)(2,1)S(1)} collective-permute-done((bf16[256,640]{1,0:T(8,128)(2,1)S(1)}, bf16[256,640]{1,0:T(8,128)(2,1)S(1)}, u32[]{:S(2)}, u32[]{:S(2)}) %collective-permute-start.13) | collective-permute-done | bytes 327712 | tf_op jit(solution)/shard_map/ppermute | solution.py:36
  80.6 6.8 %shard_map.88 = (bf16[256,640]{1,0:T(8,128)(2,1)}, bf16[256,640]{1,0:T(8,128)(2,1)}) custom-call(s32[1]{0:T(128)} %bitcast.pos_ref, s32[16,10]{1,0:T(8,128)S(1)} %copy-done.4, bf16[256,640]{1,0:T(8,128)(2,1)S(1)} %copy-done, bf16[256,640]{1,0:T(8,128)(2,1)S(1)} %copy-done.1, bf16[256,640]{1,0:T(8,128)(2,1)S(1)} %copy-done.3, ...), custom_call_target="tpu_custom_call" | custom-call | flops 1677721600 | bytes 4587520 | tf_op jit(solution)/shard_map/pallas_call | solution.py:270
  (26 shorter events, 2.8 us)
Async XLA Ops:
  0.6 15.9 %collective-permute-start.4 = (bf16[256,1280]{1,0:T(8,128)(2,1)}, bf16[256,1280]{1,0:T(8,128)(2,1)S(1)}, u32[]{:S(2)}, u32[]{:S(2)}) collective-permute-start(bf16[256,1280]{1,0:T(8,128)(2,1)} %g_a.1), channel_id=1, source_target_pairs={{0,2},{1,3},{2,0},{3,1},{4,6},{5,7},{6,4},{7,5},{8,10},{9,11},{10,... | collective-permute-start | bytes 1966088 | tf_op jit(solution)/shard_map/ppermute | solution.py:36
  4.0 15.3 %collective-permute-start = (bf16[512,640]{1,0:T(8,128)(2,1)S(1)}, bf16[512,640]{1,0:T(8,128)(2,1)S(1)}, u32[]{:S(2)}, u32[]{:S(2)}) collective-permute-start(bf16[512,640]{1,0:T(8,128)(2,1)S(1)} %constant_dynamic-update-slice_fusion), channel_id=1, source_target_pairs={{0,4},{1,5},{2,6},{3,7},{4,0},{5,1},{6,2},{7,3},{8,12},{9,13},{10,... | collective-permute-start | bytes 1966088 | tf_op jit(solution)/shard_map/ppermute | solution.py:36
  4.3 16.9 %collective-permute-start.1 = (bf16[512,640]{1,0:T(8,128)(2,1)S(1)}, bf16[512,640]{1,0:T(8,128)(2,1)S(1)}, u32[]{:S(2)}, u32[]{:S(2)}) collective-permute-start(bf16[512,640]{1,0:T(8,128)(2,1)S(1)} %constant_dynamic-update-slice_fusion), channel_id=1, source_target_pairs={{0,8},{1,9},{2,10},{3,11},{4,12},{5,13},{6,14},{7,15},{8,16},{9,17... | collective-permute-start | bytes 1966088 | tf_op jit(solution)/shard_map/ppermute | solution.py:36
  7.5 16.6 %collective-permute-start.2 = (bf16[512,640]{1,0:T(8,128)(2,1)S(1)}, bf16[512,640]{1,0:T(8,128)(2,1)S(1)}, u32[]{:S(2)}, u32[]{:S(2)}) collective-permute-start(bf16[512,640]{1,0:T(8,128)(2,1)S(1)} %constant_dynamic-update-slice_fusion), channel_id=1, source_target_pairs={{8,0},{9,1},{10,2},{11,3},{12,4},{13,5},{14,6},{15,7},{16,8},{17,9... | collective-permute-start | bytes 1966088 | tf_op jit(solution)/shard_map/ppermute | solution.py:36
  9.6 22.1 %collective-permute-start.6 = (bf16[256,1280]{1,0:T(8,128)(2,1)}, bf16[256,1280]{1,0:T(8,128)(2,1)}, u32[]{:S(2)}, u32[]{:S(2)}) collective-permute-start(bf16[256,1280]{1,0:T(8,128)(2,1)} %g_a.1), channel_id=1, source_target_pairs={{0,1},{1,0},{2,3},{3,2},{4,5},{5,4},{6,7},{7,6},{8,9},{9,8},{10,11... | collective-permute-start | bytes 1966088 | tf_op jit(solution)/shard_map/ppermute | solution.py:36
  16.5 23.8 %collective-permute-start.5 = (bf16[256,1280]{1,0:T(8,128)(2,1)S(1)}, bf16[256,1280]{1,0:T(8,128)(2,1)}, u32[]{:S(2)}, u32[]{:S(2)}) collective-permute-start(bf16[256,1280]{1,0:T(8,128)(2,1)S(1)} %collective-permute-done.4.g_a), channel_id=1, source_target_pairs={{0,1},{1,0},{2,3},{3,2},{4,5},{5,4},{6,7},{7,6},{8,9},{9,8},{10,11... | collective-permute-start | bytes 1966088 | tf_op jit(solution)/shard_map/ppermute | solution.py:36
  25.0 20.6 %collective-permute-start.3 = (bf16[512,640]{1,0:T(8,128)(2,1)}, bf16[512,640]{1,0:T(8,128)(2,1)S(1)}, u32[]{:S(2)}, u32[]{:S(2)}) collective-permute-start(bf16[512,640]{1,0:T(8,128)(2,1)} %select_select_fusion), channel_id=1, source_target_pairs={{0,8},{1,5},{2,10},{3,7},{5,1},{7,3},{8,16},{9,13},{10,18},{11,15}... | collective-permute-start | bytes 1966088 | tf_op jit(solution)/shard_map/ppermute | solution.py:36
  28.2 31.9 %collective-permute-start.7 = (bf16[256,640]{1,0:T(8,128)(2,1)}, bf16[256,640]{1,0:T(8,128)(2,1)S(1)}, u32[]{:S(2)}, u32[]{:S(2)}) collective-permute-start(bf16[256,640]{1,0:T(8,128)(2,1)} %rest_0_.1), channel_id=1, source_target_pairs={{0,4},{1,5},{2,6},{3,7},{4,0},{5,1},{6,2},{7,3},{8,12},{9,13},{10,... | collective-permute-start | bytes 983048 | tf_op jit(solution)/shard_map/ppermute | solution.py:36
  28.5 33.8 %collective-permute-start.9 = (bf16[256,640]{1,0:T(8,128)(2,1)}, bf16[256,640]{1,0:T(8,128)(2,1)S(1)}, u32[]{:S(2)}, u32[]{:S(2)}) collective-permute-start(bf16[256,640]{1,0:T(8,128)(2,1)} %rest_0_.1), channel_id=1, source_target_pairs={{0,8},{1,9},{2,10},{3,11},{4,12},{5,13},{6,14},{7,15},{8,16},{9,17... | collective-permute-start | bytes 983048 | tf_op jit(solution)/shard_map/ppermute | solution.py:36
  31.7 33.8 %collective-permute-start.11 = (bf16[256,640]{1,0:T(8,128)(2,1)}, bf16[256,640]{1,0:T(8,128)(2,1)S(1)}, u32[]{:S(2)}, u32[]{:S(2)}) collective-permute-start(bf16[256,640]{1,0:T(8,128)(2,1)} %rest_0_.1), channel_id=1, source_target_pairs={{8,0},{9,1},{10,2},{11,3},{12,4},{13,5},{14,6},{15,7},{16,8},{17,9... | collective-permute-start | bytes 983048 | tf_op jit(solution)/shard_map/ppermute | solution.py:36
  33.9 1.1 %copy-start.2 = (bf16[256,1280]{1,0:T(8,128)(2,1)S(1)}, bf16[256,1280]{1,0:T(8,128)(2,1)}, u32[]{:S(2)}) copy-start(bf16[256,1280]{1,0:T(8,128)(2,1)} %g_a.1) | copy-start | bytes 1966084
  40.3 5.4 %copy-start = (bf16[256,640]{1,0:T(8,128)(2,1)S(1)}, bf16[256,640]{1,0:T(8,128)(2,1)}, u32[]{:S(2)}) copy-start(bf16[256,640]{1,0:T(8,128)(2,1)} %k_ref.3) | copy-start | bytes 983044
  40.3 5.4 %copy-start.1 = (bf16[256,640]{1,0:T(8,128)(2,1)S(1)}, bf16[256,640]{1,0:T(8,128)(2,1)}, u32[]{:S(2)}) copy-start(bf16[256,640]{1,0:T(8,128)(2,1)} %v_ref.3) | copy-start | bytes 983044
  40.3 5.4 %copy-start.3 = (bf16[256,640]{1,0:T(8,128)(2,1)S(1)}, bf16[256,640]{1,0:T(8,128)(2,1)}, u32[]{:S(2)}) copy-start(bf16[256,640]{1,0:T(8,128)(2,1)} %rest_0_.1) | copy-start | bytes 983044
  40.3 5.4 %copy-start.4 = (s32[16,10]{1,0:T(8,128)S(1)}, s32[16,10]{1,0:T(8,128)}, u32[]{:S(2)}) copy-start(s32[16,10]{1,0:T(8,128)} %mask_ref.3) | copy-start | bytes 1924
  55.8 24.8 %collective-permute-start.8 = (bf16[720,256]{1,0:T(8,128)(2,1)S(1)}, bf16[720,256]{1,0:T(8,128)(2,1)S(1)}, u32[]{:S(2)}, u32[]{:S(2)}) collective-permute-start(bf16[720,256]{1,0:T(8,128)(2,1)S(1)} %get-tuple-element.9.rest_1_), channel_id=1, source_target_pairs={{0,4},{1,5},{2,6},{3,7},{4,0},{5,1},{6,2},{7,3},{8,12},{9,13},{10,... | collective-permute-start | bytes 1105928 | tf_op jit(solution)/shard_map/ppermute | solution.py:36
  57.0 23.6 %collective-permute-start.10 = (bf16[720,256]{1,0:T(8,128)(2,1)S(1)}, bf16[720,256]{1,0:T(8,128)(2,1)S(1)}, u32[]{:S(2)}, u32[]{:S(2)}) collective-permute-start(bf16[720,256]{1,0:T(8,128)(2,1)S(1)} %get-tuple-element.9.rest_1_), channel_id=1, source_target_pairs={{0,8},{1,9},{2,10},{3,11},{4,12},{5,13},{6,14},{7,15},{8,16},{9,17... | collective-permute-start | bytes 1105928 | tf_op jit(solution)/shard_map/ppermute | solution.py:36
  60.2 20.4 %collective-permute-start.12 = (bf16[720,256]{1,0:T(8,128)(2,1)S(1)}, bf16[720,256]{1,0:T(8,128)(2,1)S(1)}, u32[]{:S(2)}, u32[]{:S(2)}) collective-permute-start(bf16[720,256]{1,0:T(8,128)(2,1)S(1)} %get-tuple-element.9.rest_1_), channel_id=1, source_target_pairs={{8,0},{9,1},{10,2},{11,3},{12,4},{13,5},{14,6},{15,7},{16,8},{17,9... | collective-permute-start | bytes 1105928 | tf_op jit(solution)/shard_map/ppermute | solution.py:36
  62.3 18.3 %collective-permute-start.14 = (bf16[720,256]{1,0:T(8,128)(2,1)S(1)}, bf16[720,256]{1,0:T(8,128)(2,1)S(1)}, u32[]{:S(2)}, u32[]{:S(2)}) collective-permute-start(bf16[720,256]{1,0:T(8,128)(2,1)S(1)} %get-tuple-element.9.rest_1_), channel_id=1, source_target_pairs={{4,8},{5,9},{6,10},{7,11},{8,4},{9,5},{10,6},{11,7},{12,16},{13,17... | collective-permute-start | bytes 1105928 | tf_op jit(solution)/shard_map/ppermute | solution.py:36
  65.5 15.1 %collective-permute-start.13 = (bf16[256,640]{1,0:T(8,128)(2,1)S(1)}, bf16[256,640]{1,0:T(8,128)(2,1)S(1)}, u32[]{:S(2)}, u32[]{:S(2)}) collective-permute-start(bf16[256,640]{1,0:T(8,128)(2,1)S(1)} %select_select_fusion.1), channel_id=1, source_target_pairs={{0,8},{1,5},{2,10},{3,7},{5,1},{7,3},{8,16},{9,13},{10,18},{11,15}... | collective-permute-start | bytes 983048 | tf_op jit(solution)/shard_map/ppermute | solution.py:36

commit v2 on v0

v2 whole, which is shorter than its diff:
```python
import functools
import math

import jax
import jax.numpy as jnp
from jax import lax
from jax.experimental import pallas as pl
from jax.experimental.pallas import tpu as pltpu
from jax.sharding import PartitionSpec as P

HEAD_DIM = 128
TILE = 128
SPAN = 2
STAT_ROWS = 16
SCALE = 1.0 / math.sqrt(HEAD_DIM)
SCALE_LOG2 = SCALE * math.log2(math.e)
BOTH = ("ctx", "head")
NT = (((1,), (1,)), ((), ()))
TN = (((0,), (0,)), ((), ()))
NN = (((1,), (0,)), ((), ()))
VMEM_LIMIT = 24 * 1024 * 1024
VMEM = pl.BlockSpec(memory_space=pltpu.VMEM)
SMEM = pl.BlockSpec(memory_space=pltpu.SMEM)


def dot(a, b, dims):
    return lax.dot_general(a, b, dims, preferred_element_type=jnp.float32)


def kernel_call(kernel, out_shape, operands, flops, transcendentals=0):
    moved = sum(x.size * x.dtype.itemsize for x in operands)
    return pl.pallas_call(
        kernel,
        in_specs=[SMEM if x.dtype == jnp.int32 else VMEM for x in operands],
        out_specs=jax.tree.map(lambda _: VMEM, out_shape),
        out_shape=out_shape,
        compiler_params=pltpu.CompilerParams(vmem_limit_bytes=VMEM_LIMIT),
        cost_estimate=pl.CostEstimate(
            flops=flops, bytes_accessed=moved, transcendentals=transcendentals
        ),
    )(*operands)


def send(array, rule):
    n_ctx, n_head = lax.axis_size("ctx"), lax.axis_size("head")
    pairs = []
    for c in range(n_ctx):
        for h in range(n_head):
            to = rule(c, h)
            if 0 <= to[0] < n_ctx:
                pairs.append((c * n_head + h, to[0] * n_head + to[1]))
    return lax.ppermute(array, BOTH, pairs)


def in_pair(c, h):
    return (c ^ 1, h)


def even_chain(c, h):
    return (c ^ 2, h)


def odd_chain(c, h):
    return (c + 2, h) if c & 2 else (c - 2, h)


def across(c, h):
    return (c + 1, h) if c & 1 else (c - 1, h)


def forward(c, h):
    if h & 1:
        return (c ^ 1, h)
    return (c - 2, h) if c & 1 else (c + 2, h)


def offsets(pos):
    pair = 1 - 2 * lax.rem(pos, 2)
    chain = 2 - 4 * lax.rem(pos // 2, 2)
    return pair, chain, -chain, -pair


def after(value, *others):
    return lax.optimization_barrier((value,) + others)[0]


def project_kernel(order_ref, w_ref, g_a, g_b, *rest):
    cols = g_a.shape[1]
    total = None
    for n, g_ref in enumerate((g_a, g_b)):
        start = pl.multiple_of(order_ref[n] * cols, cols)
        part = dot(w_ref[:, pl.ds(start, cols)], g_ref[...], NT)
        total = part if total is None else total + part
    out_ref = rest[-1]
    if len(rest) == 2:
        total = total + rest[0][...]
    out_ref[...] = total.astype(out_ref.dtype)


def project(order, out_weight, g_a, g_b, begun=None):
    rows, cols = g_a.shape
    feat = out_weight.shape[0]
    operands = [order, out_weight, g_a, g_b] + ([] if begun is None else [begun])
    dtype = jnp.float32 if begun is None else jnp.bfloat16
    return kernel_call(
        project_kernel,
        jax.ShapeDtypeStruct((feat, rows), dtype),
        operands,
        4 * rows * cols * feat,
    )


def bias_row(live_flags):
    parts = [
        jnp.full((1, TILE), jnp.where(flag, 0.0, -jnp.inf).astype(jnp.float32))
        for flag in live_flags
    ]
    return jnp.concatenate(parts, axis=1)


def over_keys(reduce, values):
    return reduce(values.reshape(TILE // 8, 8, values.shape[1]), axis=0)


def query_kernel(pos_ref, mask_ref, q_ref, k_ref, v_ref, w_x, w_a, w_b, w_g, d_ref,
                 dq_ref, packed_ref, stats_ref):
    pos = pos_ref[0]
    rows, feat = q_ref.shape
    tiles, heads = rows // TILE, feat // HEAD_DIM
    windows = [None, w_x, w_a, w_b, w_g]
    biases = []
    for off in (0,) + offsets(pos):
        for b in range(tiles):
            column = (off + SPAN) * tiles + b
            flags = [mask_ref[pos * tiles + a, column] > 0 for a in range(tiles)]
            biases.append(bias_row(flags))

    def keys_of(n, cols):
        return k_ref[:, cols] if windows[n] is None else windows[n][:rows, cols]

    def values_of(n, cols):
        return v_ref[:, cols] if windows[n] is None else windows[n][rows:, cols]

    def score(head):
        cols = slice(head * HEAD_DIM, (head + 1) * HEAD_DIM)
        q = q_ref[:, cols]
        return [dot(keys_of(n, cols), q, NT) for n in range(len(windows))]

    def finish(head, scores):
        cols = slice(head * HEAD_DIM, (head + 1) * HEAD_DIM)
        shifted = []
        top = None
        for n, block in enumerate(scores):
            for b in range(tiles):
                value = block[b * TILE:(b + 1) * TILE] * SCALE_LOG2 + biases[n * tiles + b]
                shifted.append(value)
                peak = over_keys(jnp.max, value)
                top = peak if top is None else jnp.maximum(top, peak)
        top = jnp.max(top, axis=0, keepdims=True)
        weights = []
        totals = out = None
        for n in range(len(windows)):
            parts = []
            for b in range(tiles):
                weight = jnp.exp2(shifted[n * tiles + b] - top)
                parts.append(weight)
                part = over_keys(jnp.sum, weight)
                totals = part if totals is None else totals + part
            weights.append(jnp.concatenate(parts, axis=0))
            part = dot(values_of(n, cols), weights[-1].astype(jnp.bfloat16), TN)
            out = part if out is None else out + part
        totals = jnp.sum(totals, axis=0, keepdims=True)
        inverse = 1.0 / totals
        attn_out = (out / totals).astype(jnp.bfloat16).astype(jnp.float32)
        grad = d_ref[cols, :]
        delta = jnp.sum(grad.astype(jnp.float32) * attn_out, axis=0, keepdims=True)
        dq = None
        for n in range(len(windows)):
            dprobs = dot(values_of(n, cols), grad, NN)
            dscores = (weights[n] * ((dprobs - delta) * inverse)).astype(jnp.bfloat16)
            part = dot(keys_of(n, cols), dscores, TN)
            dq = part if dq is None else dq + part
        dq_ref[:, cols] = jnp.transpose(dq * SCALE).astype(dq_ref.dtype)
        stats = jnp.zeros((STAT_ROWS, rows), jnp.float32)
        row = lax.broadcasted_iota(jnp.int32, (STAT_ROWS, rows), 0)
        at = 0
        for stat in (top + jnp.log2(totals), delta):
            for _ in range(3):
                piece = stat.astype(jnp.bfloat16).astype(jnp.float32)
                stats = jnp.where(row == at, piece, stats)
                stat = stat - piece
                at += 1
        stats = stats.astype(jnp.bfloat16)
        packed_ref[cols, :] = grad
        packed_ref[feat + head * STAT_ROWS:feat + (head + 1) * STAT_ROWS, :] = stats
        stats_ref[head * STAT_ROWS:(head + 1) * STAT_ROWS, :] = stats

    ahead = score(0)
    for head in range(heads):
        scores = ahead
        if head + 1 < heads:
            ahead = score(head + 1)
        finish(head, scores)


def query_side(pos, tile_mask, queries, keys, values, windows, d_out_t):
    rows, feat = queries.shape
    stat_rows = feat // HEAD_DIM * STAT_ROWS
    return kernel_call(
        query_kernel,
        [
            jax.ShapeDtypeStruct((rows, feat), jnp.bfloat16),
            jax.ShapeDtypeStruct((feat + stat_rows, rows), jnp.bfloat16),
            jax.ShapeDtypeStruct((stat_rows, rows), jnp.bfloat16),
        ],
        [pos, tile_mask, queries, keys, values, *windows, d_out_t],
        40 * rows * rows * feat,
        5 * rows * rows * feat // HEAD_DIM,
    )


def key_kernel(which, stats_at, final, pos_ref, mask_ref, k_ref, v_ref, *rest):
    count = len(which)
    sources = [rest[3 * n:3 * n + 3] for n in range(count)]
    rest = rest[3 * count:]
    begun, (dk_ref, dv_ref) = (rest[:2], rest[2:]) if final else (None, rest)
    pos = pos_ref[0]
    rows, feat = k_ref.shape
    tiles, heads = rows // TILE, feat // HEAD_DIM
    total_tiles = mask_ref.shape[0]
    offs = (0,) + offsets(pos)
    biases = []
    for n in which:
        for b in range(tiles):
            flags = []
            for a in range(tiles):
                tile = (pos + offs[n]) * tiles + a
                inside = (tile >= 0) & (tile < total_tiles)
                column = (SPAN - offs[n]) * tiles + b
                flags.append(inside & (mask_ref[jnp.clip(tile, 0, total_tiles - 1), column] > 0))
            biases.append(bias_row(flags))

    def columns(head):
        return slice(head * HEAD_DIM, (head + 1) * HEAD_DIM)

    def products(head, n):
        cols = columns(head)
        q_ref, d_ref, _ = sources[n]
        return dot(k_ref[:, cols], q_ref[:, cols], NT), dot(v_ref[:, cols], d_ref[cols, :], NN)

    def finish(head, n, scores, dprobs):
        cols = columns(head)
        q_ref, d_ref, s_ref = sources[n]
        at = stats_at[n] + head * STAT_ROWS
        stats = s_ref[at:at + STAT_ROWS, :].astype(jnp.float32)
        lse = stats[0:1] + stats[1:2] + stats[2:3]
        delta = stats[3:4] + stats[4:5] + stats[5:6]
        probs = jnp.concatenate(
            [
                jnp.exp2(
                    scores[b * TILE:(b + 1) * TILE] * SCALE_LOG2 + (biases[n * tiles + b] - lse)
                )
                for b in range(tiles)
            ],
            axis=0,
        )
        dv = dot(probs.astype(jnp.bfloat16), d_ref[cols, :], NT)
        dscores = (probs * (dprobs - delta)).astype(jnp.bfloat16)
        return dot(dscores, q_ref[:, cols], NN), dv

    steps = [(head, n) for head in range(heads) for n in range(count)]
    ahead = products(*steps[0])
    for at, (head, n) in enumerate(steps):
        now = ahead
        if at + 1 < len(steps):
            ahead = products(*steps[at + 1])
        dk_part, dv_part = finish(head, n, *now)
        cols = columns(head)
        if n == 0:
            dk, dv = dk_part, dv_part
            if final:
                dk, dv = dk + begun[0][:, cols], dv + begun[1][:, cols]
        else:
            dk, dv = dk + dk_part, dv + dv_part
        if n == count - 1:
            dk_ref[:, cols] = (dk * SCALE if final else dk).astype(dk_ref.dtype)
            dv_ref[:, cols] = dv.astype(dv_ref.dtype)


def key_side(pos, tile_mask, keys, values, sources, begun=()):
    rows, feat = keys.shape
    operands = [pos, tile_mask, keys, values]
    for _, q, d, s in sources:
        operands += [q, d, s]
    operands += begun
    which = [n for n, _, _, _ in sources]
    stats_at = [s.shape[0] - feat // HEAD_DIM * STAT_ROWS for _, _, _, s in sources]
    dtype = jnp.bfloat16 if begun else jnp.float32
    return kernel_call(
        functools.partial(key_kernel, which, stats_at, bool(begun)),
        [jax.ShapeDtypeStruct((rows, feat), dtype)] * 2,
        operands,
        8 * len(which) * rows * rows * feat,
        len(which) * rows * rows * feat // HEAD_DIM,
    )


def local(queries, keys, values, out_weight, reward_grad, tile_mask):
    ctx = lax.axis_index("ctx").astype(jnp.int32)
    head = lax.axis_index("head").astype(jnp.int32)
    pos = ctx.reshape(1)

    def second_step(x, a, b):
        a_is_held = (ctx % 2 == 0) == (ctx // 2 % 2 == 0)
        return jnp.where(head % 2 == 1, jnp.where(a_is_held, a, b), x)

    far = send(reward_grad, lambda c, h: (c, h ^ 2))
    kv = jnp.concatenate([keys, values], axis=0)
    kv_a = send(kv, even_chain)
    kv_b = send(kv, odd_chain)
    kv_x = send(kv, in_pair)
    near = send(reward_grad, lambda c, h: (c, h ^ 1))
    begun = project(jnp.stack([head, head ^ 1]), out_weight, reward_grad, near)
    far_near = send(far, lambda c, h: (c, h ^ 1))
    late_queries = after(queries, begun, far)
    q_a = send(late_queries, even_chain)
    q_b = send(late_queries, odd_chain)
    q_x = send(late_queries, in_pair)
    kv_g = send(second_step(kv_x, kv_a, kv_b), forward)
    d_out_t = project(jnp.stack([head ^ 2, head ^ 3]), out_weight, far, far_near, begun)
    d_g = send(d_out_t, across)
    q_g = send(second_step(q_x, q_a, q_b), forward)
    grad_queries, packed, stats = query_side(
        pos, tile_mask, queries, keys, values, [kv_x, kv_a, kv_b, kv_g], d_out_t
    )
    p_a = send(packed, even_chain)
    p_b = send(packed, odd_chain)
    p_x = send(packed, in_pair)
    s_g = send(stats, across)
    begun_keys = key_side(
        pos,
        tile_mask,
        keys,
        values,
        [(0, queries, packed, packed), (4, q_g, d_g, s_g)],
    )
    grad_keys, grad_values = key_side(
        pos,
        tile_mask,
        keys,
        values,
        [(1, q_x, p_x, p_x), (2, q_a, p_a, p_a), (3, q_b, p_b, p_b)],
        begun_keys,
    )
    return (grad_queries, grad_keys, grad_values)


def solution(mesh):
    placed = (
        P("ctx", "head"),
        P("ctx", "head"),
        P("ctx", "head"),
        P("head", None),
        P("ctx", "head"),
        P(),
    )
    return jax.shard_map(
        local,
        mesh=mesh,
        in_specs=placed,
        out_specs=(P("ctx", "head"), P("ctx", "head"), P("ctx", "head")),
        check_vma=False,
    )
```

time: 176 us -> 72.6 us (0.41)
  waiting for transfers between devices: 69.2 us -> 10.7 us
  local copies, waits for them, and re-layouts: 34.3 us -> 10.3 us
  matrix products: 22.1 us -> 0 us
  Pallas kernels: 0 us -> 17.1 us
  between operations: 14.3 us -> 0.86 us
  other arithmetic: 7.97 us -> 2.42 us
  starting transfers between devices: 25.7 us -> 30.5 us
    ppermute x8 -> x16, waiting for transfers between devices: 68.5 us -> 10.7 us  [send(): return lax.ppermute(array, BOTH, pairs)]
    pallas_call x0 -> x5, Pallas kernels: none -> 17.1 us  [kernel_call(): pl.pallas_call(kernel, in_specs=[SMEM if x.dtype == jnp.int32 else VMEM f...]
    dot_general x6 -> x0, matrix products: 16.3 us -> none  [the longest x1 5.96 us: attend_local(): jnp.einsum('hqk,hqd->khd', probs.astype(jnp.bfloat16), grad_heads, prefer...]
    another operation x3 -> x0, local copies, waits for them, and re-layouts: 14.1 us -> none  [local(): jnp.stack([grad_key_win.reshape(window_len, feat_width), grad_value_win.r...]
    mul x1 -> x0, local copies, waits for them, and re-layouts: 8.34 us -> none  [attend_local(): jnp.einsum('hqk,qhd->khd', dscores, query_blk, preferred_element_type=jnp...]
    sub x1 -> x0, matrix products: 5.87 us -> none  [attend_local(): weights = jnp.where(live_three, jnp.exp(scores - row_max), 0.0)]
    ppermute x8 -> x16, starting transfers between devices: 25.7 us -> 30.5 us  [send(): return lax.ppermute(array, BOTH, pairs)]
    squeeze x1 -> x0, other arithmetic: 4.2 us -> none  [local(): slices = [grad_window[:, index] for index in range(2 * SPAN + 1)]]
  transfers between devices with their start and end apart: 9 -> 16, of which waited for: 4 -> 6; matrix products, arithmetic and copies ran while one was open for 10% -> 8% of each run, Pallas kernels for 0% -> 19%
where the time goes in v2:
time: 72.6 us; the launch traced here: 71.9 us
  starting transfers between devices  30.5 us (42%)
  Pallas kernels  17.1 us (24%)
  waiting for transfers between devices  10.7 us (15%)
  local copies, waits for them, and re-layouts  10.3 us (14%)
  other arithmetic  2.42 us (3%)
  between operations  0.86 us (1%)
    ppermute x16, starting transfers between devices, send(): return lax.ppermute(array, BOTH, pairs)  30.5 us
    pallas_call x5, Pallas kernels, kernel_call(): pl.pallas_call(kernel, in_specs=[SMEM if x.dtype == jnp.int32 else VMEM f...  17.1 us
    ppermute x16, waiting for transfers between devices, send(): return lax.ppermute(array, BOTH, pairs)  10.7 us
    unnamed x15, local copies, waits for them, and re-layouts  8.55 us
    select_n x2, other arithmetic, second_step(): return jnp.where(head % 2 == 1, jnp.where(a_is_held, a, b), x)  2.27 us
    concatenate x1, local copies, waits for them, and re-layouts, local(): kv = jnp.concatenate([keys, values], axis=0)  1.73 us
  transfers between devices with their start and end apart: 16, of which 6 were waited for; matrix products, arithmetic and copies ran while one was open for 8% of the time, Pallas kernels for 19%

profile of v2, /device:TPU:8, one launch (start us, length us, event | category | flops | bytes accessed | tf_op | source)
XLA Modules:
  0.0 71.9 jit_solution(16549574483514403239)
XLA Ops:
  0.6 1.6 %collective-permute-start.4 = (bf16[256,1280]{1,0:T(8,128)(2,1)}, bf16[256,1280]{1,0:T(8,128)(2,1)S(1)}, u32[]{:S(2)}, u32[]{:S(2)}) collective-permute-start(bf16[256,1280]{1,0:T(8,128)(2,1)} %g_a.1), channel_id=1, source_target_pairs={{0,2},{1,3},{2,0},{3,1},{4,6},{5,7},{6,4},{7,5},{8,10},{9,11},{10,... | collective-permute-start | bytes 1966088 | tf_op jit(solution)/shard_map/ppermute | solution.py:52
  2.2 1.7 %constant_dynamic-update-slice_fusion.1 = bf16[512,640]{1,0:T(8,128)(2,1)} fusion(bf16[256,640]{1,0:T(8,128)(2,1)} %k_ref.5), kind=kLoop, calls=%fused_computation.3 | loop fusion | bytes 655360
  4.0 1.7 %constant_dynamic-update-slice_fusion = bf16[512,640]{1,0:T(8,128)(2,1)} fusion(bf16[512,640]{1,0:T(8,128)(2,1)} %constant_dynamic-update-slice_fusion.1, bf16[256,640]{1,0:T(8,128)(2,1)} %v_ref.5), kind=kLoop, calls=%fused_computation.2 | loop fusion | bytes 655360 | tf_op jit(solution)/shard_map/concatenate | solution.py:318
  5.7 3.5 %collective-permute-start.2 = (bf16[512,640]{1,0:T(8,128)(2,1)}, bf16[512,640]{1,0:T(8,128)(2,1)}, u32[]{:S(2)}, u32[]{:S(2)}) collective-permute-start(bf16[512,640]{1,0:T(8,128)(2,1)} %constant_dynamic-update-slice_fusion), channel_id=1, source_target_pairs={{8,16},{9,17},{10,18},{11,19},{12,20},{13,21},{14,22},{15,23},{16,... | collective-permute-start | bytes 1966088 | tf_op jit(solution)/shard_map/ppermute | solution.py:52
  9.3 1.6 %collective-permute-start = (bf16[512,640]{1,0:T(8,128)(2,1)}, bf16[512,640]{1,0:T(8,128)(2,1)}, u32[]{:S(2)}, u32[]{:S(2)}) collective-permute-start(bf16[512,640]{1,0:T(8,128)(2,1)} %constant_dynamic-update-slice_fusion), channel_id=1, source_target_pairs={{0,4},{1,5},{2,6},{3,7},{4,0},{5,1},{6,2},{7,3},{8,12},{9,13},{10,... | collective-permute-start | bytes 1966088 | tf_op jit(solution)/shard_map/ppermute | solution.py:52
  10.9 2.9 %copy-done = bf16[640,5120]{1,0:T(8,128)(2,1)S(1)} copy-done((bf16[640,5120]{1,0:T(8,128)(2,1)S(1)}, bf16[640,5120]{1,0:T(8,128)(2,1)}, u32[]{:S(2)}) %copy-start) | copy-done | bytes 6553624
  13.7 1.1 %copy-done.4 = bf16[256,1280]{1,0:T(8,128)(2,1)S(1)} copy-done((bf16[256,1280]{1,0:T(8,128)(2,1)S(1)}, bf16[256,1280]{1,0:T(8,128)(2,1)}, u32[]{:S(2)}) %copy-start.4) | copy-done | bytes 655384
  14.8 1.6 %shard_map.85.rest_0_ = f32[640,256]{1,0:T(8,128)S(1)} custom-call(s32[2]{0:T(128)S(1)} %pad_add_fusion.1.order_ref, bf16[640,5120]{1,0:T(8,128)(2,1)S(1)} %copy-done, bf16[256,1280]{1,0:T(8,128)(2,1)S(1)} %copy-done.4, bf16[256,1280]{1,0:T(8,128)(2,1)S(1)} %collective-permute-done.6.g_b), custom_call_target="tpu_custom_call" | custom-call | flops 838860800 | bytes 7864328 | tf_op jit(solution)/shard_map/pallas_call | solution.py:32
  17.4 3.5 %collective-permute-start.11 = (bf16[256,640]{1,0:T(8,128)(2,1)S(1)}, bf16[256,640]{1,0:T(8,128)(2,1)S(1)}, u32[]{:S(2)}, u32[]{:S(2)}) collective-permute-start(bf16[256,640]{1,0:T(8,128)(2,1)S(1)} %copy-done.6), channel_id=1, source_target_pairs={{8,16},{9,17},{10,18},{11,19},{12,20},{13,21},{14,22},{15,23},{16,... | collective-permute-start | bytes 983048 | tf_op jit(solution)/shard_map/ppermute | solution.py:52
  21.0 4.5 %collective-permute-done.2.w_b = bf16[512,640]{1,0:T(8,128)(2,1)} collective-permute-done((bf16[512,640]{1,0:T(8,128)(2,1)}, bf16[512,640]{1,0:T(8,128)(2,1)}, u32[]{:S(2)}, u32[]{:S(2)}) %collective-permute-start.2) | collective-permute-done | bytes 655392 | tf_op jit(solution)/shard_map/ppermute | solution.py:52
  25.4 1.5 %collective-permute-start.7 = (bf16[256,640]{1,0:T(8,128)(2,1)S(1)}, bf16[256,640]{1,0:T(8,128)(2,1)S(1)}, u32[]{:S(2)}, u32[]{:S(2)}) collective-permute-start(bf16[256,640]{1,0:T(8,128)(2,1)S(1)} %copy-done.6), channel_id=1, source_target_pairs={{0,4},{1,5},{2,6},{3,7},{4,0},{5,1},{6,2},{7,3},{8,12},{9,13},{10,... | collective-permute-start | bytes 983048 | tf_op jit(solution)/shard_map/ppermute | solution.py:52
  27.1 2.2 %select_select_fusion = bf16[512,640]{1,0:T(8,128)(2,1)} fusion(bf16[512,640]{1,0:T(8,128)(2,1)} %collective-permute-done.w_x, bf16[512,640]{1,0:T(8,128)(2,1)} %collective-permute-done.1.w_a, bf16[512,640]{1,0:T(8,128)(2,1)} %collective-permute-done.2.w_b, pred[]{:T(512)S(6)} %eq.26, pred[]{:T(512)S(6)} %eq.23), kind=kLoop, calls=%fused_computation | loop fusion | flops 655360 | bytes 2621442 | tf_op jit(solution)/shard_map/jit(_where)/select_n | solution.py:315
  29.3 3.3 %collective-permute-start.3 = (bf16[512,640]{1,0:T(8,128)(2,1)}, bf16[512,640]{1,0:T(8,128)(2,1)}, u32[]{:S(2)}, u32[]{:S(2)}) collective-permute-start(bf16[512,640]{1,0:T(8,128)(2,1)} %select_select_fusion), channel_id=1, source_target_pairs={{0,8},{1,5},{2,10},{3,7},{5,1},{7,3},{8,16},{9,13},{10,18},{11,15}... | collective-permute-start | bytes 1966088 | tf_op jit(solution)/shard_map/ppermute | solution.py:52
  33.3 1.0 %collective-permute-done.7.rest_0_ = bf16[256,640]{1,0:T(8,128)(2,1)S(1)} collective-permute-done((bf16[256,640]{1,0:T(8,128)(2,1)S(1)}, bf16[256,640]{1,0:T(8,128)(2,1)S(1)}, u32[]{:S(2)}, u32[]{:S(2)}) %collective-permute-start.7) | collective-permute-done | bytes 327712 | tf_op jit(solution)/shard_map/ppermute | solution.py:52
  34.4 3.7 %collective-permute-start.13 = (bf16[256,640]{1,0:T(8,128)(2,1)S(1)}, bf16[256,640]{1,0:T(8,128)(2,1)S(1)}, u32[]{:S(2)}, u32[]{:S(2)}) collective-permute-start(bf16[256,640]{1,0:T(8,128)(2,1)S(1)} %select_select_fusion.1), channel_id=1, source_target_pairs={{0,8},{1,5},{2,10},{3,7},{5,1},{7,3},{8,16},{9,13},{10,18},{11,15}... | collective-permute-start | bytes 983048 | tf_op jit(solution)/shard_map/ppermute | solution.py:52
  38.1 2.9 %copy-done.1 = bf16[640,5120]{1,0:T(8,128)(2,1)S(1)} copy-done((bf16[640,5120]{1,0:T(8,128)(2,1)S(1)}, bf16[640,5120]{1,0:T(8,128)(2,1)}, u32[]{:S(2)}) %copy-start.1) | copy-done | bytes 6553624
  41.0 2.2 %shard_map.86.d_ref = bf16[640,256]{1,0:T(8,128)(2,1)S(1)} custom-call(s32[2]{0:T(128)S(1)} %pad_add_fusion.order_ref, bf16[640,5120]{1,0:T(8,128)(2,1)S(1)} %copy-done.1, bf16[256,1280]{1,0:T(8,128)(2,1)S(1)} %collective-permute-done.4.g_a, bf16[256,1280]{1,0:T(8,128)(2,1)} %collective-permute-done.5.g_b, f32[640,256]{1,0:T(8,128)S(1)} %shard_map.85.rest_0_), custom_call_target="tpu_custom_call" | custom-call | flops 838860800 | bytes 8519688 | tf_op jit(solution)/shard_map/pallas_call | solution.py:32
  43.1 1.9 %collective-permute-start.14 = (bf16[640,256]{1,0:T(8,128)(2,1)S(1)}, bf16[640,256]{1,0:T(8,128)(2,1)S(1)}, u32[]{:S(2)}, u32[]{:S(2)}) collective-permute-start(bf16[640,256]{1,0:T(8,128)(2,1)S(1)} %shard_map.86.d_ref), channel_id=1, source_target_pairs={{4,8},{5,9},{6,10},{7,11},{8,4},{9,5},{10,6},{11,7},{12,16},{13,17... | collective-permute-start | bytes 983048 | tf_op jit(solution)/shard_map/ppermute | solution.py:52
  45.1 7.3 %shard_map.87 = (bf16[256,640]{1,0:T(8,128)(2,1)}, bf16[720,256]{1,0:T(8,128)(2,1)S(1)}, bf16[80,256]{1,0:T(8,128)(2,1)S(1)}) custom-call(s32[1]{0:T(128)} %bitcast.pos_ref, s32[16,10]{1,0:T(8,128)S(1)} %copy-done.5, bf16[256,640]{1,0:T(8,128)(2,1)S(1)} %copy-done.6, bf16[256,640]{1,0:T(8,128)(2,1)S(1)} %copy-done.2, bf16[256,640]{1,0:T(8,128)(2,1)S(1)} %copy-done.3, ...), custom_call_target="tpu_custom_call" | custom-call | flops 1677721600 | bytes 3932804 | tf_op jit(solution)/shard_map/pallas_call | solution.py:32
  52.4 4.5 %collective-permute-start.12 = (bf16[720,256]{1,0:T(8,128)(2,1)S(1)}, bf16[720,256]{1,0:T(8,128)(2,1)S(1)}, u32[]{:S(2)}, u32[]{:S(2)}) collective-permute-start(bf16[720,256]{1,0:T(8,128)(2,1)S(1)} %get-tuple-element.13.rest_1_.rest_2_), channel_id=1, source_target_pairs={{8,16},{9,17},{10,18},{11,19},{12,20},{13,21},{14,22},{15,23},{16,... | collective-permute-start | bytes 1105928 | tf_op jit(solution)/shard_map/ppermute | solution.py:52
  57.1 5.3 %collective-permute-start.15 = (bf16[80,256]{1,0:T(8,128)(2,1)S(1)}, bf16[80,256]{1,0:T(8,128)(2,1)S(1)}, u32[]{:S(2)}, u32[]{:S(2)}) collective-permute-start(bf16[80,256]{1,0:T(8,128)(2,1)S(1)} %get-tuple-element.14), channel_id=1, source_target_pairs={{4,8},{5,9},{6,10},{7,11},{8,4},{9,5},{10,6},{11,7},{12,16},{13,17... | collective-permute-start | bytes 122888 | tf_op jit(solution)/shard_map/ppermute | solution.py:52
  62.4 3.5 %collective-permute-done.15.rest_5_ = bf16[80,256]{1,0:T(8,128)(2,1)S(1)} collective-permute-done((bf16[80,256]{1,0:T(8,128)(2,1)S(1)}, bf16[80,256]{1,0:T(8,128)(2,1)S(1)}, u32[]{:S(2)}, u32[]{:S(2)}) %collective-permute-start.15) | collective-permute-done | bytes 40992 | tf_op jit(solution)/shard_map/ppermute | solution.py:52
  65.8 2.3 %shard_map.88 = (f32[256,640]{1,0:T(8,128)S(1)}, f32[256,640]{1,0:T(8,128)S(1)}) custom-call(s32[1]{0:T(128)} %bitcast.pos_ref, s32[16,10]{1,0:T(8,128)S(1)} %copy-done.5, bf16[256,640]{1,0:T(8,128)(2,1)S(1)} %copy-done.2, bf16[256,640]{1,0:T(8,128)(2,1)S(1)} %copy-done.3, bf16[256,640]{1,0:T(8,128)(2,1)S(1)} %copy-done.6, ...), custom_call_target="tpu_custom_call" | custom-call | flops 671088640 | bytes 2417284 | tf_op jit(solution)/shard_map/pallas_call | solution.py:32
  68.1 3.8 %shard_map.89 = (bf16[256,640]{1,0:T(8,128)(2,1)}, bf16[256,640]{1,0:T(8,128)(2,1)}) custom-call(s32[1]{0:T(128)} %bitcast.pos_ref, s32[16,10]{1,0:T(8,128)S(1)} %copy-done.5, bf16[256,640]{1,0:T(8,128)(2,1)S(1)} %copy-done.2, bf16[256,640]{1,0:T(8,128)(2,1)S(1)} %copy-done.3, bf16[256,640]{1,0:T(8,128)(2,1)S(1)} %collective-permute-done.7.rest_0_, ...), custom_call_target="tpu_custom_call" | custom-call | flops 1006632960 | bytes 5161604 | tf_op jit(solution)/shard_map/pallas_call | solution.py:32
  (33 shorter events, 2.3 us)
Async XLA Ops:
  0.6 16.8 %copy-start.6 = (bf16[256,640]{1,0:T(8,128)(2,1)S(1)}, bf16[256,640]{1,0:T(8,128)(2,1)}, u32[]{:S(2)}) copy-start(bf16[256,640]{1,0:T(8,128)(2,1)} %rest_0_.1) | copy-start | bytes 983044
  0.6 16.7 %collective-permute-start.4 = (bf16[256,1280]{1,0:T(8,128)(2,1)}, bf16[256,1280]{1,0:T(8,128)(2,1)S(1)}, u32[]{:S(2)}, u32[]{:S(2)}) collective-permute-start(bf16[256,1280]{1,0:T(8,128)(2,1)} %g_a.1), channel_id=1, source_target_pairs={{0,2},{1,3},{2,0},{3,1},{4,6},{5,7},{6,4},{7,5},{8,10},{9,11},{10,... | collective-permute-start | bytes 1966088 | tf_op jit(solution)/shard_map/ppermute | solution.py:52
  2.2 8.7 %collective-permute-start.6 = (bf16[256,1280]{1,0:T(8,128)(2,1)}, bf16[256,1280]{1,0:T(8,128)(2,1)S(1)}, u32[]{:S(2)}, u32[]{:S(2)}) collective-permute-start(bf16[256,1280]{1,0:T(8,128)(2,1)} %g_a.1), channel_id=1, source_target_pairs={{0,1},{1,0},{2,3},{3,2},{4,5},{5,4},{6,7},{7,6},{8,9},{9,8},{10,11... | collective-permute-start | bytes 1966088 | tf_op jit(solution)/shard_map/ppermute | solution.py:52
  5.7 19.7 %collective-permute-start.2 = (bf16[512,640]{1,0:T(8,128)(2,1)}, bf16[512,640]{1,0:T(8,128)(2,1)}, u32[]{:S(2)}, u32[]{:S(2)}) collective-permute-start(bf16[512,640]{1,0:T(8,128)(2,1)} %constant_dynamic-update-slice_fusion), channel_id=1, source_target_pairs={{8,16},{9,17},{10,18},{11,19},{12,20},{13,21},{14,22},{15,23},{16,... | collective-permute-start | bytes 1966088 | tf_op jit(solution)/shard_map/ppermute | solution.py:52
  9.2 17.9 %collective-permute-start.1 = (bf16[512,640]{1,0:T(8,128)(2,1)}, bf16[512,640]{1,0:T(8,128)(2,1)}, u32[]{:S(2)}, u32[]{:S(2)}) collective-permute-start(bf16[512,640]{1,0:T(8,128)(2,1)} %constant_dynamic-update-slice_fusion), channel_id=1, source_target_pairs={{0,8},{1,9},{2,10},{3,11},{4,12},{5,13},{6,14},{7,15},{8,0},{9,1},... | collective-permute-start | bytes 1966088 | tf_op jit(solution)/shard_map/ppermute | solution.py:52
  9.3 17.9 %collective-permute-start = (bf16[512,640]{1,0:T(8,128)(2,1)}, bf16[512,640]{1,0:T(8,128)(2,1)}, u32[]{:S(2)}, u32[]{:S(2)}) collective-permute-start(bf16[512,640]{1,0:T(8,128)(2,1)} %constant_dynamic-update-slice_fusion), channel_id=1, source_target_pairs={{0,4},{1,5},{2,6},{3,7},{4,0},{5,1},{6,2},{7,3},{8,12},{9,13},{10,... | collective-permute-start | bytes 1966088 | tf_op jit(solution)/shard_map/ppermute | solution.py:52
  10.9 2.9 %copy-start = (bf16[640,5120]{1,0:T(8,128)(2,1)S(1)}, bf16[640,5120]{1,0:T(8,128)(2,1)}, u32[]{:S(2)}) copy-start(bf16[640,5120]{1,0:T(8,128)(2,1)} %w_ref.3) | copy-start | bytes 19660804
  13.7 1.1 %copy-start.4 = (bf16[256,1280]{1,0:T(8,128)(2,1)S(1)}, bf16[256,1280]{1,0:T(8,128)(2,1)}, u32[]{:S(2)}) copy-start(bf16[256,1280]{1,0:T(8,128)(2,1)} %g_a.1) | copy-start | bytes 1966084
  16.4 28.6 %copy-start.2 = (bf16[256,640]{1,0:T(8,128)(2,1)S(1)}, bf16[256,640]{1,0:T(8,128)(2,1)}, u32[]{:S(2)}) copy-start(bf16[256,640]{1,0:T(8,128)(2,1)} %k_ref.5) | copy-start | bytes 983044
  16.5 28.6 %copy-start.3 = (bf16[256,640]{1,0:T(8,128)(2,1)S(1)}, bf16[256,640]{1,0:T(8,128)(2,1)}, u32[]{:S(2)}) copy-start(bf16[256,640]{1,0:T(8,128)(2,1)} %v_ref.5) | copy-start | bytes 983044
  16.5 28.6 %copy-start.5 = (s32[16,10]{1,0:T(8,128)S(1)}, s32[16,10]{1,0:T(8,128)}, u32[]{:S(2)}) copy-start(s32[16,10]{1,0:T(8,128)} %mask_ref.5) | copy-start | bytes 1924
  17.4 15.3 %collective-permute-start.11 = (bf16[256,640]{1,0:T(8,128)(2,1)S(1)}, bf16[256,640]{1,0:T(8,128)(2,1)S(1)}, u32[]{:S(2)}, u32[]{:S(2)}) collective-permute-start(bf16[256,640]{1,0:T(8,128)(2,1)S(1)} %copy-done.6), channel_id=1, source_target_pairs={{8,16},{9,17},{10,18},{11,19},{12,20},{13,21},{14,22},{15,23},{16,... | collective-permute-start | bytes 983048 | tf_op jit(solution)/shard_map/ppermute | solution.py:52
  20.9 12.5 %collective-permute-start.9 = (bf16[256,640]{1,0:T(8,128)(2,1)S(1)}, bf16[256,640]{1,0:T(8,128)(2,1)S(1)}, u32[]{:S(2)}, u32[]{:S(2)}) collective-permute-start(bf16[256,640]{1,0:T(8,128)(2,1)S(1)} %copy-done.6), channel_id=1, source_target_pairs={{0,8},{1,9},{2,10},{3,11},{4,12},{5,13},{6,14},{7,15},{8,0},{9,1},... | collective-permute-start | bytes 983048 | tf_op jit(solution)/shard_map/ppermute | solution.py:52
  25.4 9.0 %collective-permute-start.7 = (bf16[256,640]{1,0:T(8,128)(2,1)S(1)}, bf16[256,640]{1,0:T(8,128)(2,1)S(1)}, u32[]{:S(2)}, u32[]{:S(2)}) collective-permute-start(bf16[256,640]{1,0:T(8,128)(2,1)S(1)} %copy-done.6), channel_id=1, source_target_pairs={{0,4},{1,5},{2,6},{3,7},{4,0},{5,1},{6,2},{7,3},{8,12},{9,13},{10,... | collective-permute-start | bytes 983048 | tf_op jit(solution)/shard_map/ppermute | solution.py:52
  27.1 11.0 %collective-permute-start.5 = (bf16[256,1280]{1,0:T(8,128)(2,1)S(1)}, bf16[256,1280]{1,0:T(8,128)(2,1)}, u32[]{:S(2)}, u32[]{:S(2)}) collective-permute-start(bf16[256,1280]{1,0:T(8,128)(2,1)S(1)} %collective-permute-done.4.g_a), channel_id=1, source_target_pairs={{0,1},{1,0},{2,3},{3,2},{4,5},{5,4},{6,7},{7,6},{8,9},{9,8},{10,11... | collective-permute-start | bytes 1966088 | tf_op jit(solution)/shard_map/ppermute | solution.py:52
  29.3 15.7 %collective-permute-start.3 = (bf16[512,640]{1,0:T(8,128)(2,1)}, bf16[512,640]{1,0:T(8,128)(2,1)}, u32[]{:S(2)}, u32[]{:S(2)}) collective-permute-start(bf16[512,640]{1,0:T(8,128)(2,1)} %select_select_fusion), channel_id=1, source_target_pairs={{0,8},{1,5},{2,10},{3,7},{5,1},{7,3},{8,16},{9,13},{10,18},{11,15}... | collective-permute-start | bytes 1966088 | tf_op jit(solution)/shard_map/ppermute | solution.py:52
  34.4 22.6 %collective-permute-start.13 = (bf16[256,640]{1,0:T(8,128)(2,1)S(1)}, bf16[256,640]{1,0:T(8,128)(2,1)S(1)}, u32[]{:S(2)}, u32[]{:S(2)}) collective-permute-start(bf16[256,640]{1,0:T(8,128)(2,1)S(1)} %select_select_fusion.1), channel_id=1, source_target_pairs={{0,8},{1,5},{2,10},{3,7},{5,1},{7,3},{8,16},{9,13},{10,18},{11,15}... | collective-permute-start | bytes 983048 | tf_op jit(solution)/shard_map/ppermute | solution.py:52
  38.1 2.9 %copy-start.1 = (bf16[640,5120]{1,0:T(8,128)(2,1)S(1)}, bf16[640,5120]{1,0:T(8,128)(2,1)}, u32[]{:S(2)}) copy-start(bf16[640,5120]{1,0:T(8,128)(2,1)} %w_ref.3) | copy-start | bytes 19660804
  43.1 22.7 %collective-permute-start.14 = (bf16[640,256]{1,0:T(8,128)(2,1)S(1)}, bf16[640,256]{1,0:T(8,128)(2,1)S(1)}, u32[]{:S(2)}, u32[]{:S(2)}) collective-permute-start(bf16[640,256]{1,0:T(8,128)(2,1)S(1)} %shard_map.86.d_ref), channel_id=1, source_target_pairs={{4,8},{5,9},{6,10},{7,11},{8,4},{9,5},{10,6},{11,7},{12,16},{13,17... | collective-permute-start | bytes 983048 | tf_op jit(solution)/shard_map/ppermute | solution.py:52
  52.4 15.7 %collective-permute-start.12 = (bf16[720,256]{1,0:T(8,128)(2,1)S(1)}, bf16[720,256]{1,0:T(8,128)(2,1)S(1)}, u32[]{:S(2)}, u32[]{:S(2)}) collective-permute-start(bf16[720,256]{1,0:T(8,128)(2,1)S(1)} %get-tuple-element.13.rest_1_.rest_2_), channel_id=1, source_target_pairs={{8,16},{9,17},{10,18},{11,19},{12,20},{13,21},{14,22},{15,23},{16,... | collective-permute-start | bytes 1105928 | tf_op jit(solution)/shard_map/ppermute | solution.py:52
  56.9 11.2 %collective-permute-start.10 = (bf16[720,256]{1,0:T(8,128)(2,1)S(1)}, bf16[720,256]{1,0:T(8,128)(2,1)S(1)}, u32[]{:S(2)}, u32[]{:S(2)}) collective-permute-start(bf16[720,256]{1,0:T(8,128)(2,1)S(1)} %get-tuple-element.13.rest_1_.rest_2_), channel_id=1, source_target_pairs={{0,8},{1,9},{2,10},{3,11},{4,12},{5,13},{6,14},{7,15},{8,0},{9,1},... | collective-permute-start | bytes 1105928 | tf_op jit(solution)/shard_map/ppermute | solution.py:52
  57.0 11.1 %collective-permute-start.8 = (bf16[720,256]{1,0:T(8,128)(2,1)S(1)}, bf16[720,256]{1,0:T(8,128)(2,1)S(1)}, u32[]{:S(2)}, u32[]{:S(2)}) collective-permute-start(bf16[720,256]{1,0:T(8,128)(2,1)S(1)} %get-tuple-element.13.rest_1_.rest_2_), channel_id=1, source_target_pairs={{0,4},{1,5},{2,6},{3,7},{4,0},{5,1},{6,2},{7,3},{8,12},{9,13},{10,... | collective-permute-start | bytes 1105928 | tf_op jit(solution)/shard_map/ppermute | solution.py:52
  57.1 8.7 %collective-permute-start.15 = (bf16[80,256]{1,0:T(8,128)(2,1)S(1)}, bf16[80,256]{1,0:T(8,128)(2,1)S(1)}, u32[]{:S(2)}, u32[]{:S(2)}) collective-permute-start(bf16[80,256]{1,0:T(8,128)(2,1)S(1)} %get-tuple-element.14), channel_id=1, source_target_pairs={{4,8},{5,9},{6,10},{7,11},{8,4},{9,5},{10,6},{11,7},{12,16},{13,17... | collective-permute-start | bytes 122888 | tf_op jit(solution)/shard_map/ppermute | solution.py:52

commit v3 on v2

v3 whole, which is shorter than its diff:
```python
import functools
import math

import jax
import jax.numpy as jnp
from jax import lax
from jax.experimental import pallas as pl
from jax.experimental.pallas import tpu as pltpu
from jax.sharding import PartitionSpec as P

HEAD_DIM = 128
TILE = 128
SPAN = 2
STAT_ROWS = 16
SCALE = 1.0 / math.sqrt(HEAD_DIM)
SCALE_LOG2 = SCALE * math.log2(math.e)
BOTH = ("ctx", "head")
NT = (((1,), (1,)), ((), ()))
TN = (((0,), (0,)), ((), ()))
NN = (((1,), (0,)), ((), ()))
VMEM_LIMIT = 16 * 1024 * 1024
VMEM_ALONE = 32 * 1024 * 1024
VMEM = pl.BlockSpec(memory_space=pltpu.VMEM)
SMEM = pl.BlockSpec(memory_space=pltpu.SMEM)
ANY = pl.BlockSpec(memory_space=pl.ANY)


def dot(a, b, dims):
    return lax.dot_general(a, b, dims, preferred_element_type=jnp.float32)


def kernel_call(kernel, out_shape, operands, flops, transcendentals=0):
    moved = sum(x.size * x.dtype.itemsize for x in operands)
    return pl.pallas_call(
        kernel,
        in_specs=[SMEM if x.dtype == jnp.int32 else VMEM for x in operands],
        out_specs=jax.tree.map(lambda _: VMEM, out_shape),
        out_shape=out_shape,
        compiler_params=pltpu.CompilerParams(vmem_limit_bytes=VMEM_LIMIT),
        cost_estimate=pl.CostEstimate(
            flops=flops, bytes_accessed=moved, transcendentals=transcendentals
        ),
    )(*operands)


def send(array, rule):
    n_ctx, n_head = lax.axis_size("ctx"), lax.axis_size("head")
    pairs = []
    for c in range(n_ctx):
        for h in range(n_head):
            to = rule(c, h)
            if 0 <= to[0] < n_ctx:
                pairs.append((c * n_head + h, to[0] * n_head + to[1]))
    return lax.ppermute(array, BOTH, pairs)


def in_pair(c, h):
    return (c ^ 1, h)


def even_chain(c, h):
    return (c ^ 2, h)


def odd_chain(c, h):
    return (c + 2, h) if c & 2 else (c - 2, h)


def across(c, h):
    return (c + 1, h) if c & 1 else (c - 1, h)


def forward(c, h):
    if h & 1:
        return (c ^ 1, h)
    return (c - 2, h) if c & 1 else (c + 2, h)


def offsets(pos):
    pair = 1 - 2 * lax.rem(pos, 2)
    chain = 2 - 4 * lax.rem(pos // 2, 2)
    return pair, chain, -chain, -pair


def after(value, *others):
    return lax.optimization_barrier((value,) + others)[0]


def pack_kernel(k_ref, v_ref, out_ref, sems):
    rows = k_ref.shape[0]
    copies = [
        pltpu.make_async_copy(k_ref, out_ref.at[:rows], sems.at[0]),
        pltpu.make_async_copy(v_ref, out_ref.at[rows:], sems.at[1]),
    ]
    for copy in copies:
        copy.start()
    for copy in copies:
        copy.wait()


def pack(keys, values):
    rows, feat = keys.shape
    return pl.pallas_call(
        pack_kernel,
        in_specs=[ANY] * 2,
        out_specs=VMEM,
        out_shape=jax.ShapeDtypeStruct((2 * rows, feat), keys.dtype),
        scratch_shapes=[pltpu.SemaphoreType.DMA((2,))],
        compiler_params=pltpu.CompilerParams(vmem_limit_bytes=VMEM_LIMIT),
        cost_estimate=pl.CostEstimate(
            flops=0, bytes_accessed=60_000_000, transcendentals=0
        ),
    )(keys, values)


def begin_kernel(order_ref, w_ref, g_a, g_b, out_ref, kept_ref, used, sems):
    cols = g_a.shape[1]
    copies = []
    for n in range(4):
        start = pl.multiple_of(order_ref[n] * cols, cols)
        to = used.at[n] if n < 2 else kept_ref.at[:, (n - 2) * cols:(n - 1) * cols]
        copies.append(pltpu.make_async_copy(w_ref.at[:, pl.ds(start, cols)], to, sems.at[n]))
        copies[-1].start()
    copies[0].wait()
    total = dot(used[0], g_a[...], NT)
    copies[1].wait()
    out_ref[...] = total + dot(used[1], g_b[...], NT)
    copies[2].wait()
    copies[3].wait()


def begin_project(order, out_weight, g_a, g_b):
    rows, cols = g_a.shape
    feat = out_weight.shape[0]
    return pl.pallas_call(
        begin_kernel,
        in_specs=[SMEM, ANY, VMEM, VMEM],
        out_specs=[VMEM, VMEM],
        out_shape=[
            jax.ShapeDtypeStruct((feat, rows), jnp.float32),
            jax.ShapeDtypeStruct((feat, 2 * cols), out_weight.dtype),
        ],
        scratch_shapes=[
            pltpu.VMEM((2, feat, cols), out_weight.dtype),
            pltpu.SemaphoreType.DMA((4,)),
        ],
        compiler_params=pltpu.CompilerParams(vmem_limit_bytes=VMEM_ALONE),
        cost_estimate=pl.CostEstimate(
            flops=4 * rows * cols * feat, bytes_accessed=8 * feat * cols, transcendentals=0
        ),
    )(order, out_weight, g_a, g_b)


def end_kernel(w_ref, g_a, g_b, begun, out_ref):
    cols = g_a.shape[1]
    total = begun[...] + dot(w_ref[:, :cols], g_a[...], NT)
    out_ref[...] = (total + dot(w_ref[:, cols:], g_b[...], NT)).astype(out_ref.dtype)


def end_project(weight, g_a, g_b, begun):
    rows, cols = g_a.shape
    feat = weight.shape[0]
    return kernel_call(
        end_kernel,
        jax.ShapeDtypeStruct((feat, rows), jnp.bfloat16),
        [weight, g_a, g_b, begun],
        4 * rows * cols * feat,
    )


def columns(head):
    return slice(head * HEAD_DIM, (head + 1) * HEAD_DIM)


def stat_slice(head, start=0):
    return slice(start + head * STAT_ROWS, start + (head + 1) * STAT_ROWS)


def bias_row(live_flags):
    parts = [
        jnp.full((1, TILE), jnp.where(flag, 0.0, -jnp.inf).astype(jnp.float32))
        for flag in live_flags
    ]
    return jnp.concatenate(parts, axis=1)


def window_bias(mask_ref, pos, tiles, which):
    offs = (0,) + offsets(pos)
    return [
        [
            bias_row(
                [
                    mask_ref[pos * tiles + a, (offs[n] + SPAN) * tiles + b] > 0
                    for a in range(tiles)
                ]
            )
            for b in range(tiles)
        ]
        for n in which
    ]


def source_bias(mask_ref, pos, tiles, which):
    total_tiles = mask_ref.shape[0]
    offs = (0,) + offsets(pos)
    rows = []
    for n in which:
        rows.append([])
        for b in range(tiles):
            flags = []
            for a in range(tiles):
                tile = (pos + offs[n]) * tiles + a
                inside = (tile >= 0) & (tile < total_tiles)
                column = (SPAN - offs[n]) * tiles + b
                flags.append(inside & (mask_ref[jnp.clip(tile, 0, total_tiles - 1), column] > 0))
            rows[-1].append(bias_row(flags))
    return rows


def over_keys(reduce, values):
    return reduce(values.reshape(TILE // 8, 8, values.shape[1]), axis=0)


def softmax_part(scores, biases):
    shifted = []
    top = None
    for block, rows in zip(scores, biases):
        shifted.append([])
        for b, row in enumerate(rows):
            value = block[b * TILE:(b + 1) * TILE] * SCALE_LOG2 + row
            shifted[-1].append(value)
            peak = over_keys(jnp.max, value)
            top = peak if top is None else jnp.maximum(top, peak)
    return shifted, jnp.max(top, axis=0, keepdims=True)


def weighted_values(shifted, top, values_of):
    totals = out = None
    for n, parts in enumerate(shifted):
        weights = []
        for value in parts:
            weight = jnp.exp2(value - top)
            weights.append(weight)
            part = over_keys(jnp.sum, weight)
            totals = part if totals is None else totals + part
        part = dot(values_of(n), jnp.concatenate(weights, axis=0).astype(jnp.bfloat16), TN)
        out = part if out is None else out + part
    return jnp.sum(totals, axis=0, keepdims=True), out


def in_order(steps, ahead_of, finish):
    ahead = ahead_of(*steps[0])
    for at, step in enumerate(steps):
        now = ahead
        if at + 1 < len(steps):
            ahead = ahead_of(*steps[at + 1])
        finish(*step, now)


def forward_kernel(which, pos_ref, mask_ref, q_ref, *rest):
    windows, (out_ref, run_ref) = rest[:len(which)], rest[len(which):]
    pos = pos_ref[0]
    rows, feat = q_ref.shape
    biases = window_bias(mask_ref, pos, rows // TILE, which)

    def scores_of(head):
        cols = columns(head)
        q = q_ref[:, cols]
        return [dot(w[:rows, cols], q, NT) for w in windows]

    def finish(head, scores):
        cols = columns(head)

        def values_of(n):
            return windows[n][rows:, cols]

        shifted, top = softmax_part(scores, biases)
        totals, out = weighted_values(shifted, top, values_of)
        out_ref[cols, :] = out
        at = head * STAT_ROWS
        run_ref[at:at + 8, :] = jnp.broadcast_to(top, (8, rows))
        run_ref[at + 8:at + 16, :] = jnp.broadcast_to(totals, (8, rows))

    in_order([(head,) for head in range(feat // HEAD_DIM)], scores_of, finish)


def forward_part(pos, tile_mask, queries, which, windows):
    rows, feat = queries.shape
    heads = feat // HEAD_DIM
    return kernel_call(
        functools.partial(forward_kernel, which),
        [
            jax.ShapeDtypeStruct((feat, rows), jnp.float32),
            jax.ShapeDtypeStruct((heads * STAT_ROWS, rows), jnp.float32),
        ],
        [pos, tile_mask, queries, *windows],
        4 * len(which) * rows * rows * feat,
        len(which) * rows * rows * heads,
    )


def statistics_kernel(
    which, pos_ref, mask_ref, q_ref, w_ref, out_in, run_in, d_ref, stats_ref, packed_ref
):
    pos = pos_ref[0]
    rows, feat = q_ref.shape
    biases = window_bias(mask_ref, pos, rows // TILE, [which])

    def scores_of(head):
        cols = columns(head)
        return [dot(w_ref[:rows, cols], q_ref[:, cols], NT)]

    def finish(head, scores):
        cols = columns(head)

        def values_of(n):
            return w_ref[rows:, cols]

        at = head * STAT_ROWS
        top_before, totals_before = run_in[at:at + 1, :], run_in[at + 8:at + 9, :]
        shifted, top = softmax_part(scores, biases)
        top = jnp.maximum(top, top_before)
        totals, out = weighted_values(shifted, top, values_of)
        shrink = jnp.exp2(top_before - top)
        totals = totals + totals_before * shrink
        out = out + out_in[cols, :] * shrink
        attn_out = (out / totals).astype(jnp.bfloat16).astype(jnp.float32)
        delta = jnp.sum(d_ref[cols, :].astype(jnp.float32) * attn_out, axis=0, keepdims=True)
        row = lax.broadcasted_iota(jnp.int32, (STAT_ROWS, rows), 0)
        stats = jnp.zeros((STAT_ROWS, rows), jnp.float32)
        place = 0
        for stat in (top + jnp.log2(totals), delta):
            for _ in range(3):
                piece = stat.astype(jnp.bfloat16).astype(jnp.float32)
                stats = jnp.where(row == place, piece, stats)
                stat = stat - piece
                place += 1
        stats_ref[stat_slice(head), :] = stats.astype(jnp.bfloat16)
        packed_ref[cols, :] = d_ref[cols, :]
        packed_ref[stat_slice(head, feat), :] = stats.astype(jnp.bfloat16)

    in_order([(head,) for head in range(feat // HEAD_DIM)], scores_of, finish)


def statistics(pos, tile_mask, queries, which, window, out, run, d_out_t):
    rows, feat = queries.shape
    heads = feat // HEAD_DIM
    return kernel_call(
        functools.partial(statistics_kernel, which),
        [
            jax.ShapeDtypeStruct((heads * STAT_ROWS, rows), jnp.bfloat16),
            jax.ShapeDtypeStruct((feat + heads * STAT_ROWS, rows), jnp.bfloat16),
        ],
        [pos, tile_mask, queries, window, out, run, d_out_t],
        4 * rows * rows * feat,
        rows * rows * heads,
    )


def block_grads(scores, dprobs, bias_rows, stats):
    stats = stats.astype(jnp.float32)
    lse = stats[0:1] + stats[1:2] + stats[2:3]
    delta = stats[3:4] + stats[4:5] + stats[5:6]
    probs = jnp.concatenate(
        [
            jnp.exp2(scores[b * TILE:(b + 1) * TILE] * SCALE_LOG2 + (row - lse))
            for b, row in enumerate(bias_rows)
        ],
        axis=0,
    )
    dscores = probs * (dprobs - delta)
    return probs.astype(jnp.bfloat16), dscores.astype(jnp.bfloat16)


def query_kernel(which, pos_ref, mask_ref, q_ref, *rest):
    count = len(which)
    windows = rest[:count]
    d_ref, s_ref, dq_ref, dk_ref, dv_ref = rest[count:]
    rows, feat = q_ref.shape
    biases = window_bias(mask_ref, pos_ref[0], rows // TILE, which)
    sums = [None]

    def keys_of(n, cols):
        return windows[n][:rows, cols]

    def values_of(n, cols):
        return windows[n][rows:, cols]

    def products(head, n):
        cols = columns(head)
        return (
            dot(keys_of(n, cols), q_ref[:, cols], NT),
            dot(values_of(n, cols), d_ref[cols, :], NN),
        )

    def finish(head, n, now):
        cols = columns(head)
        probs, dscores = block_grads(*now, biases[n], s_ref[stat_slice(head), :])
        part = dot(keys_of(n, cols), dscores, TN)
        if n == 0:
            sums[0] = part
            dk_ref[:, cols] = dot(dscores, q_ref[:, cols], NN)
            dv_ref[:, cols] = dot(probs, d_ref[cols, :], NT)
        else:
            sums[0] = sums[0] + part
        if n == count - 1:
            dq_ref[:, cols] = jnp.transpose(sums[0] * SCALE).astype(dq_ref.dtype)

    steps = [(head, n) for head in range(feat // HEAD_DIM) for n in range(count)]
    in_order(steps, products, finish)


def query_side(pos, tile_mask, queries, which, windows, d_out_t, stats):
    rows, feat = queries.shape
    total = jax.ShapeDtypeStruct((rows, feat), jnp.float32)
    return kernel_call(
        functools.partial(query_kernel, which),
        [jax.ShapeDtypeStruct((rows, feat), jnp.bfloat16), total, total],
        [pos, tile_mask, queries, *windows, d_out_t, stats],
        34 * rows * rows * feat,
        5 * rows * rows * feat // HEAD_DIM,
    )


def key_kernel(which, final, pos_ref, mask_ref, kv_ref, *rest):
    count = len(which)
    sources = [rest[3 * n:3 * n + 3] for n in range(count)]
    dk_in, dv_in, dk_ref, dv_ref = rest[3 * count:]
    rows, feat = dk_in.shape
    biases = source_bias(mask_ref, pos_ref[0], rows // TILE, which)
    sums = [None, None]

    def products(head, n):
        cols = columns(head)
        q_ref, d_ref, _ = sources[n]
        return (
            dot(kv_ref[:rows, cols], q_ref[:, cols], NT),
            dot(kv_ref[rows:, cols], d_ref[cols, :], NN),
        )

    def finish(head, n, now):
        cols = columns(head)
        q_ref, d_ref, s_ref = sources[n]
        start = feat if s_ref.shape[0] > feat else 0
        probs, dscores = block_grads(*now, biases[n], s_ref[stat_slice(head, start), :])
        before = (dk_in[:, cols], dv_in[:, cols]) if n == 0 else sums
        sums[:] = [
            before[0] + dot(dscores, q_ref[:, cols], NN),
            before[1] + dot(probs, d_ref[cols, :], NT),
        ]
        if n == count - 1:
            dk, dv = sums
            dk_ref[:, cols] = (dk * SCALE if final else dk).astype(dk_ref.dtype)
            dv_ref[:, cols] = dv.astype(dv_ref.dtype)

    steps = [(head, n) for head in range(feat // HEAD_DIM) for n in range(count)]
    in_order(steps, products, finish)


def key_side(pos, tile_mask, kv, sources, begun, final):
    rows, feat = begun[0].shape
    operands = [pos, tile_mask, kv]
    for _, q, d, s in sources:
        operands += [q, d, s]
    which = [source[0] for source in sources]
    dtype = jnp.bfloat16 if final else jnp.float32
    return kernel_call(
        functools.partial(key_kernel, which, final),
        [jax.ShapeDtypeStruct((rows, feat), dtype)] * 2,
        operands + list(begun),
        8 * len(which) * rows * rows * feat,
        len(which) * rows * rows * feat // HEAD_DIM,
    )


def local(queries, keys, values, out_weight, reward_grad, tile_mask):
    ctx = lax.axis_index("ctx").astype(jnp.int32)
    head = lax.axis_index("head").astype(jnp.int32)
    pos = ctx.reshape(1)

    def second_step(x, a, b):
        a_is_held = (ctx % 2 == 0) == (ctx // 2 % 2 == 0)
        return jnp.where(head % 2 == 1, jnp.where(a_is_held, a, b), x)

    far = send(reward_grad, lambda c, h: (c, h ^ 2))
    kv = pack(keys, values)
    kv_b = send(kv, odd_chain)
    kv_a = send(kv, even_chain)
    kv_x = send(kv, in_pair)
    near = send(after(reward_grad, kv), lambda c, h: (c, h ^ 1))
    order = jnp.stack([head, head ^ 1, head ^ 2, head ^ 3])
    begun, kept = begin_project(order, out_weight, reward_grad, near)
    far = after(far, begun)
    far_near = send(far, lambda c, h: (c, h ^ 1))
    kv_g = send(second_step(kv_x, kv_a, kv_b), forward)
    d_out_t = end_project(kept, far, far_near, begun)
    out, run = forward_part(
        pos, tile_mask, after(queries, d_out_t), [0, 1, 2, 3], [kv, kv_x, kv_a, kv_b]
    )
    late_queries = after(queries, out)
    q_b = send(late_queries, odd_chain)
    q_a = send(late_queries, even_chain)
    q_x = send(late_queries, in_pair)
    stats, packed = statistics(pos, tile_mask, queries, 4, kv_g, out, run, d_out_t)
    p_b = send(packed, odd_chain)
    p_a = send(packed, even_chain)
    p_x = send(packed, in_pair)
    q_g = send(second_step(q_x, q_a, q_b), forward)
    grad_queries, *begun_keys = query_side(
        pos, tile_mask, queries, [0, 1, 2, 3, 4], [kv, kv_x, kv_a, kv_b, kv_g], d_out_t, stats
    )
    p_g = send(second_step(*after((p_x, p_a, p_b), grad_queries)), forward)
    begun_keys = key_side(
        pos,
        tile_mask,
        kv,
        [(1, q_x, p_x, p_x), (2, q_a, p_a, p_a), (3, q_b, p_b, p_b)],
        begun_keys,
        False,
    )
    grad_keys, grad_values = key_side(
        pos, tile_mask, kv, [(4, q_g, p_g, p_g)], begun_keys, True
    )
    return (grad_queries, grad_keys, grad_values)


def solution(mesh):
    placed = (
        P("ctx", "head"),
        P("ctx", "head"),
        P("ctx", "head"),
        P("head", None),
        P("ctx", "head"),
        P(),
    )
    return jax.shard_map(
        local,
        mesh=mesh,
        in_specs=placed,
        out_specs=(P("ctx", "head"), P("ctx", "head"), P("ctx", "head")),
        check_vma=False,
    )
```

time: 72.6 us -> 70 us (0.964)
  waiting for transfers between devices: 10.7 us -> 16.8 us
  local copies, waits for them, and re-layouts: 10.3 us -> 5.89 us
  starting transfers between devices: 30.5 us -> 26.5 us
  other arithmetic: 2.42 us -> 0.32 us
  Pallas kernels: 17.1 us -> 18.6 us
    ppermute x16 -> x15, waiting for transfers between devices: 10.7 us -> 16.8 us  [send(): return lax.ppermute(array, BOTH, pairs)]
    ppermute x16 -> x15, starting transfers between devices: 30.5 us -> 26.5 us  [send(): return lax.ppermute(array, BOTH, pairs)]
    pallas_call x0 -> x2, Pallas kernels: none -> 3.46 us  [the longest x1 3.24 us: begin_project(): pl.pallas_call(begin_kernel, in_specs=[SMEM, ANY, VMEM, VMEM], out_specs=...]
    unnamed x15 -> x12, local copies, waits for them, and re-layouts: 8.55 us -> 5.89 us
    select_n x2 -> x3, other arithmetic: 2.27 us -> 0.24 us  [second_step(): return jnp.where(head % 2 == 1, jnp.where(a_is_held, a, b), x)]
    pallas_call x5 -> x6, Pallas kernels: 17.1 us -> 15.2 us  [kernel_call(): pl.pallas_call(kernel, in_specs=[SMEM if x.dtype == jnp.int32 else VMEM f...]
    concatenate x1 -> x0, local copies, waits for them, and re-layouts: 1.73 us -> none  [local(): kv = jnp.concatenate([keys, values], axis=0)]
  transfers between devices with their start and end apart: 16 -> 15, of which waited for: 6 -> 8; matrix products, arithmetic and copies ran while one was open for 8% -> 0% of each run, Pallas kernels for 19% -> 21%
where the time goes in v3:
time: 70 us; the launch traced here: 69.1 us
  starting transfers between devices  26.5 us (38%)
  Pallas kernels  18.6 us (27%)
  waiting for transfers between devices  16.8 us (24%)
  local copies, waits for them, and re-layouts  5.89 us (8%)
  between operations  0.84 us (1%)
    ppermute x15, starting transfers between devices, send(): return lax.ppermute(array, BOTH, pairs)  26.5 us
    ppermute x15, waiting for transfers between devices, send(): return lax.ppermute(array, BOTH, pairs)  16.8 us
    pallas_call x6, Pallas kernels, kernel_call(): pl.pallas_call(kernel, in_specs=[SMEM if x.dtype == jnp.int32 else VMEM f...  15.2 us
    unnamed x12, local copies, waits for them, and re-layouts  5.89 us
    pallas_call x1, Pallas kernels, begin_project(): pl.pallas_call(begin_kernel, in_specs=[SMEM, ANY, VMEM, VMEM], out_specs=...  3.24 us
  transfers between devices with their start and end apart: 15, of which 8 were waited for; matrix products, arithmetic and copies ran while one was open for 0% of the time, Pallas kernels for 21%

profile of v3, /device:TPU:8, one launch (start us, length us, event | category | flops | bytes accessed | tf_op | source)
XLA Modules:
  0.0 69.1 jit_solution(12086270591814853889)
XLA Ops:
  2.9 1.6 %collective-permute-start.5 = (bf16[256,1280]{1,0:T(8,128)(2,1)}, bf16[256,1280]{1,0:T(8,128)(2,1)S(1)}, u32[]{:S(2)}, u32[]{:S(2)}) collective-permute-start(bf16[256,1280]{1,0:T(8,128)(2,1)} %g_a.1), channel_id=1, source_target_pairs={{0,2},{1,3},{2,0},{3,1},{4,6},{5,7},{6,4},{7,5},{8,10},{9,11},{10,... | collective-permute-start | bytes 1966088 | tf_op jit(solution)/shard_map/ppermute | solution.py:54
  4.5 1.5 %collective-permute-start = (bf16[512,640]{1,0:T(8,128)(2,1)S(1)}, bf16[512,640]{1,0:T(8,128)(2,1)S(1)}, u32[]{:S(2)}, u32[]{:S(2)}) collective-permute-start(bf16[512,640]{1,0:T(8,128)(2,1)S(1)} %shard_map.85.rest_0_.kv_ref), channel_id=1, source_target_pairs={{0,4},{1,5},{2,6},{3,7},{4,0},{5,1},{6,2},{7,3},{8,12},{9,13},{10,... | collective-permute-start | bytes 1966088 | tf_op jit(solution)/shard_map/ppermute | solution.py:54
  6.4 4.6 %collective-permute-start.2 = (bf16[512,640]{1,0:T(8,128)(2,1)S(1)}, bf16[512,640]{1,0:T(8,128)(2,1)S(1)}, u32[]{:S(2)}, u32[]{:S(2)}) collective-permute-start(bf16[512,640]{1,0:T(8,128)(2,1)S(1)} %shard_map.85.rest_0_.kv_ref), channel_id=1, source_target_pairs={{8,16},{9,17},{10,18},{11,19},{12,20},{13,21},{14,22},{15,23},{16,... | collective-permute-start | bytes 1966088 | tf_op jit(solution)/shard_map/ppermute | solution.py:54
  11.2 2.9 %copy-done = bf16[640,5120]{1,0:T(8,128)(2,1)S(1)} copy-done((bf16[640,5120]{1,0:T(8,128)(2,1)S(1)}, bf16[640,5120]{1,0:T(8,128)(2,1)}, u32[]{:S(2)}) %copy-start) | copy-done | bytes 6553624
  14.0 1.1 %copy-done.2 = bf16[256,1280]{1,0:T(8,128)(2,1)S(1)} copy-done((bf16[256,1280]{1,0:T(8,128)(2,1)S(1)}, bf16[256,1280]{1,0:T(8,128)(2,1)}, u32[]{:S(2)}) %copy-start.2) | copy-done | bytes 655384
  15.1 3.2 %shard_map.86 = (f32[640,256]{1,0:T(8,128)S(1)}, bf16[640,2560]{1,0:T(8,128)(2,1)S(1)}) custom-call(s32[4]{0:T(128)S(1)} %pad_add_fusion.order_ref, bf16[640,5120]{1,0:T(8,128)(2,1)S(1)} %copy-done, bf16[256,1280]{1,0:T(8,128)(2,1)S(1)} %copy-done.2, bf16[256,1280]{1,0:T(8,128)(2,1)} %collective-permute-done.4.g_b), custom_call_target="tpu_custom_call" | custom-call | flops 838860800 | bytes 6553600 | tf_op jit(solution)/shard_map/pallas_call | solution.py:135
  18.4 1.9 %collective-permute-done.5.g_a = bf16[256,1280]{1,0:T(8,128)(2,1)S(1)} collective-permute-done((bf16[256,1280]{1,0:T(8,128)(2,1)}, bf16[256,1280]{1,0:T(8,128)(2,1)S(1)}, u32[]{:S(2)}, u32[]{:S(2)}) %collective-permute-start.5) | collective-permute-done | bytes 655392 | tf_op jit(solution)/shard_map/ppermute | solution.py:54
  20.2 1.0 %collective-permute-done.rest_1_ = bf16[512,640]{1,0:T(8,128)(2,1)S(1)} collective-permute-done((bf16[512,640]{1,0:T(8,128)(2,1)S(1)}, bf16[512,640]{1,0:T(8,128)(2,1)S(1)}, u32[]{:S(2)}, u32[]{:S(2)}) %collective-permute-start) | collective-permute-done | bytes 655392 | tf_op jit(solution)/shard_map/ppermute | solution.py:54
  21.3 1.2 %collective-permute-done.1.rest_2_ = bf16[512,640]{1,0:T(8,128)(2,1)S(1)} collective-permute-done((bf16[512,640]{1,0:T(8,128)(2,1)S(1)}, bf16[512,640]{1,0:T(8,128)(2,1)S(1)}, u32[]{:S(2)}, u32[]{:S(2)}) %collective-permute-start.1) | collective-permute-done | bytes 655392 | tf_op jit(solution)/shard_map/ppermute | solution.py:54
  22.5 3.0 %collective-permute-done.2.rest_3_ = bf16[512,640]{1,0:T(8,128)(2,1)S(1)} collective-permute-done((bf16[512,640]{1,0:T(8,128)(2,1)S(1)}, bf16[512,640]{1,0:T(8,128)(2,1)S(1)}, u32[]{:S(2)}, u32[]{:S(2)}) %collective-permute-start.2) | collective-permute-done | bytes 655392 | tf_op jit(solution)/shard_map/ppermute | solution.py:54
  25.6 3.6 %collective-permute-start.3 = (bf16[512,640]{1,0:T(8,128)(2,1)S(1)}, bf16[512,640]{1,0:T(8,128)(2,1)S(1)}, u32[]{:S(2)}, u32[]{:S(2)}) collective-permute-start(bf16[512,640]{1,0:T(8,128)(2,1)S(1)} %select_select_fusion), channel_id=1, source_target_pairs={{0,8},{1,5},{2,10},{3,7},{5,1},{7,3},{8,16},{9,13},{10,18},{11,15}... | collective-permute-start | bytes 1966088 | tf_op jit(solution)/shard_map/ppermute | solution.py:54
  29.3 1.0 %shard_map.87.d_ref.rest_5_ = bf16[640,256]{1,0:T(8,128)(2,1)S(1)} custom-call(bf16[640,2560]{1,0:T(8,128)(2,1)S(1)} %get-tuple-element.24.w_ref, bf16[256,1280]{1,0:T(8,128)(2,1)S(1)} %collective-permute-done.5.g_a, bf16[256,1280]{1,0:T(8,128)(2,1)S(1)} %collective-permute-done.6.g_b, f32[640,256]{1,0:T(8,128)S(1)} %get-tuple-element.25.begun), custom_call_target="tpu_custom_call" | custom-call | flops 838860800 | bytes 5242880 | tf_op jit(solution)/shard_map/pallas_call | solution.py:34
  30.3 2.6 %shard_map.88 = (f32[640,256]{1,0:T(8,128)S(1)}, f32[80,256]{1,0:T(8,128)S(1)}) custom-call(s32[1]{0:T(128)} %bitcast.pos_ref, s32[16,10]{1,0:T(8,128)S(1)} %copy-done.5, bf16[256,640]{1,0:T(8,128)(2,1)S(1)} %copy-done.1, bf16[512,640]{1,0:T(8,128)(2,1)S(1)} %shard_map.85.rest_0_.kv_ref, bf16[512,640]{1,0:T(8,128)(2,1)S(1)} %collective-permute-done.rest_1_, ...), custom_call_target="tpu_custom_call" | custom-call | flops 671088640 | bytes 2949764 | tf_op jit(solution)/shard_map/pallas_call | solution.py:34
  32.9 5.1 %collective-permute-done.3.w_ref.rest_4_ = bf16[512,640]{1,0:T(8,128)(2,1)S(1)} collective-permute-done((bf16[512,640]{1,0:T(8,128)(2,1)S(1)}, bf16[512,640]{1,0:T(8,128)(2,1)S(1)}, u32[]{:S(2)}, u32[]{:S(2)}) %collective-permute-start.3) | collective-permute-done | bytes 655392 | tf_op jit(solution)/shard_map/ppermute | solution.py:54
  38.1 1.6 %shard_map.89 = (bf16[80,256]{1,0:T(8,128)(2,1)S(1)}, bf16[720,256]{1,0:T(8,128)(2,1)S(1)}) custom-call(s32[1]{0:T(128)} %bitcast.pos_ref, s32[16,10]{1,0:T(8,128)S(1)} %copy-done.5, bf16[256,640]{1,0:T(8,128)(2,1)S(1)} %copy-done.1, bf16[512,640]{1,0:T(8,128)(2,1)S(1)} %collective-permute-done.3.w_ref.rest_4_, f32[640,256]{1,0:T(8,128)S(1)} %get-tuple-element.28.out_in, ...), custom_call_target="tpu_custom_call" | custom-call | flops 167772160 | bytes 2048644 | tf_op jit(solution)/shard_map/pallas_call | solution.py:34
  40.3 3.6 %collective-permute-start.13 = (bf16[720,256]{1,0:T(8,128)(2,1)S(1)}, bf16[720,256]{1,0:T(8,128)(2,1)S(1)}, u32[]{:S(2)}, u32[]{:S(2)}) collective-permute-start(bf16[720,256]{1,0:T(8,128)(2,1)S(1)} %get-tuple-element.33), channel_id=1, source_target_pairs={{8,16},{9,17},{10,18},{11,19},{12,20},{13,21},{14,22},{15,23},{16,... | collective-permute-start | bytes 1105928 | tf_op jit(solution)/shard_map/ppermute | solution.py:54
  44.0 2.7 %collective-permute-start.8 = (bf16[256,640]{1,0:T(8,128)(2,1)S(1)}, bf16[256,640]{1,0:T(8,128)(2,1)S(1)}, u32[]{:S(2)}, u32[]{:S(2)}) collective-permute-start(bf16[256,640]{1,0:T(8,128)(2,1)S(1)} %copy-done.1), channel_id=1, source_target_pairs={{8,16},{9,17},{10,18},{11,19},{12,20},{13,21},{14,22},{15,23},{16,... | collective-permute-start | bytes 983048 | tf_op jit(solution)/shard_map/ppermute | solution.py:54
  46.7 1.8 %collective-permute-done.11.rest_1_.rest_2_ = bf16[720,256]{1,0:T(8,128)(2,1)S(1)} collective-permute-done((bf16[720,256]{1,0:T(8,128)(2,1)S(1)}, bf16[720,256]{1,0:T(8,128)(2,1)S(1)}, u32[]{:S(2)}, u32[]{:S(2)}) %collective-permute-start.11) | collective-permute-done | bytes 368672 | tf_op jit(solution)/shard_map/ppermute | solution.py:54
  49.0 4.6 %shard_map.90 = (bf16[256,640]{1,0:T(8,128)(2,1)}, f32[256,640]{1,0:T(8,128)S(1)}, f32[256,640]{1,0:T(8,128)S(1)}) custom-call(s32[1]{0:T(128)} %bitcast.pos_ref, s32[16,10]{1,0:T(8,128)S(1)} %copy-done.5, bf16[256,640]{1,0:T(8,128)(2,1)S(1)} %copy-done.1, bf16[512,640]{1,0:T(8,128)(2,1)S(1)} %shard_map.85.rest_0_.kv_ref, ...), custom_call_target="tpu_custom_call" | custom-call | flops 1426063360 | bytes 3973764 | tf_op jit(solution)/shard_map/pallas_call | solution.py:34
  53.8 3.6 %collective-permute-start.14 = (bf16[720,256]{1,0:T(8,128)(2,1)S(1)}, bf16[720,256]{1,0:T(8,128)(2,1)S(1)}, u32[]{:S(2)}, u32[]{:S(2)}) collective-permute-start(bf16[720,256]{1,0:T(8,128)(2,1)S(1)} %select_select_fusion.1), channel_id=1, source_target_pairs={{0,8},{1,5},{2,10},{3,7},{5,1},{7,3},{8,16},{9,13},{10,18},{11,15}... | collective-permute-start | bytes 1105928 | tf_op jit(solution)/shard_map/ppermute | solution.py:54
  57.6 3.5 %collective-permute-start.10 = (bf16[256,640]{1,0:T(8,128)(2,1)S(1)}, bf16[256,640]{1,0:T(8,128)(2,1)S(1)}, u32[]{:S(2)}, u32[]{:S(2)}) collective-permute-start(bf16[256,640]{1,0:T(8,128)(2,1)S(1)} %select_select_fusion.2), channel_id=1, source_target_pairs={{0,8},{1,5},{2,10},{3,7},{5,1},{7,3},{8,16},{9,13},{10,18},{11,15}... | collective-permute-start | bytes 983048 | tf_op jit(solution)/shard_map/ppermute | solution.py:54
  61.1 3.0 %shard_map.91 = (f32[256,640]{1,0:T(8,128)S(1)}, f32[256,640]{1,0:T(8,128)S(1)}) custom-call(s32[1]{0:T(128)} %bitcast.pos_ref, s32[16,10]{1,0:T(8,128)S(1)} %copy-done.5, bf16[512,640]{1,0:T(8,128)(2,1)S(1)} %shard_map.85.rest_0_.kv_ref, bf16[256,640]{1,0:T(8,128)(2,1)S(1)} %collective-permute-done.9.rest_0_, ...), custom_call_target="tpu_custom_call" | custom-call | flops 1006632960 | bytes 5161604 | tf_op jit(solution)/shard_map/pallas_call | solution.py:34
  64.1 2.6 %collective-permute-done.10.rest_0_ = bf16[256,640]{1,0:T(8,128)(2,1)S(1)} collective-permute-done((bf16[256,640]{1,0:T(8,128)(2,1)S(1)}, bf16[256,640]{1,0:T(8,128)(2,1)S(1)}, u32[]{:S(2)}, u32[]{:S(2)}) %collective-permute-start.10) | collective-permute-done | bytes 327712 | tf_op jit(solution)/shard_map/ppermute | solution.py:54
  66.7 2.4 %shard_map.92 = (bf16[256,640]{1,0:T(8,128)(2,1)}, bf16[256,640]{1,0:T(8,128)(2,1)}) custom-call(s32[1]{0:T(128)} %bitcast.pos_ref, s32[16,10]{1,0:T(8,128)S(1)} %copy-done.5, bf16[512,640]{1,0:T(8,128)(2,1)S(1)} %shard_map.85.rest_0_.kv_ref, bf16[256,640]{1,0:T(8,128)(2,1)S(1)} %collective-permute-done.10.rest_0_, ...), custom_call_target="tpu_custom_call" | custom-call | flops 335544320 | bytes 3031684 | tf_op jit(solution)/shard_map/pallas_call | solution.py:34
  (30 shorter events, 4.4 us)
Async XLA Ops:
  0.6 1.0 %copy-start.3 = (bf16[256,640]{1,0:T(8,128)(2,1)S(1)}, bf16[256,640]{1,0:T(8,128)(2,1)}, u32[]{:S(2)}) copy-start(bf16[256,640]{1,0:T(8,128)(2,1)} %k_ref.1) | copy-start | bytes 983044
  1.6 1.0 %copy-start.4 = (bf16[256,640]{1,0:T(8,128)(2,1)S(1)}, bf16[256,640]{1,0:T(8,128)(2,1)}, u32[]{:S(2)}) copy-start(bf16[256,640]{1,0:T(8,128)(2,1)} %v_ref.1) | copy-start | bytes 983044
  2.8 8.3 %collective-permute-start.4 = (bf16[256,1280]{1,0:T(8,128)(2,1)}, bf16[256,1280]{1,0:T(8,128)(2,1)}, u32[]{:S(2)}, u32[]{:S(2)}) collective-permute-start(bf16[256,1280]{1,0:T(8,128)(2,1)} %g_a.1), channel_id=1, source_target_pairs={{0,1},{1,0},{2,3},{3,2},{4,5},{5,4},{6,7},{7,6},{8,9},{9,8},{10,11... | collective-permute-start | bytes 1966088 | tf_op jit(solution)/shard_map/ppermute | solution.py:54
  2.9 17.4 %collective-permute-start.5 = (bf16[256,1280]{1,0:T(8,128)(2,1)}, bf16[256,1280]{1,0:T(8,128)(2,1)S(1)}, u32[]{:S(2)}, u32[]{:S(2)}) collective-permute-start(bf16[256,1280]{1,0:T(8,128)(2,1)} %g_a.1), channel_id=1, source_target_pairs={{0,2},{1,3},{2,0},{3,1},{4,6},{5,7},{6,4},{7,5},{8,10},{9,11},{10,... | collective-permute-start | bytes 1966088 | tf_op jit(solution)/shard_map/ppermute | solution.py:54
  4.5 16.8 %collective-permute-start = (bf16[512,640]{1,0:T(8,128)(2,1)S(1)}, bf16[512,640]{1,0:T(8,128)(2,1)S(1)}, u32[]{:S(2)}, u32[]{:S(2)}) collective-permute-start(bf16[512,640]{1,0:T(8,128)(2,1)S(1)} %shard_map.85.rest_0_.kv_ref), channel_id=1, source_target_pairs={{0,4},{1,5},{2,6},{3,7},{4,0},{5,1},{6,2},{7,3},{8,12},{9,13},{10,... | collective-permute-start | bytes 1966088 | tf_op jit(solution)/shard_map/ppermute | solution.py:54
  6.0 16.5 %collective-permute-start.1 = (bf16[512,640]{1,0:T(8,128)(2,1)S(1)}, bf16[512,640]{1,0:T(8,128)(2,1)S(1)}, u32[]{:S(2)}, u32[]{:S(2)}) collective-permute-start(bf16[512,640]{1,0:T(8,128)(2,1)S(1)} %shard_map.85.rest_0_.kv_ref), channel_id=1, source_target_pairs={{0,8},{1,9},{2,10},{3,11},{4,12},{5,13},{6,14},{7,15},{8,0},{9,1},... | collective-permute-start | bytes 1966088 | tf_op jit(solution)/shard_map/ppermute | solution.py:54
  6.4 19.1 %collective-permute-start.2 = (bf16[512,640]{1,0:T(8,128)(2,1)S(1)}, bf16[512,640]{1,0:T(8,128)(2,1)S(1)}, u32[]{:S(2)}, u32[]{:S(2)}) collective-permute-start(bf16[512,640]{1,0:T(8,128)(2,1)S(1)} %shard_map.85.rest_0_.kv_ref), channel_id=1, source_target_pairs={{8,16},{9,17},{10,18},{11,19},{12,20},{13,21},{14,22},{15,23},{16,... | collective-permute-start | bytes 1966088 | tf_op jit(solution)/shard_map/ppermute | solution.py:54
  11.2 2.9 %copy-start = (bf16[640,5120]{1,0:T(8,128)(2,1)S(1)}, bf16[640,5120]{1,0:T(8,128)(2,1)}, u32[]{:S(2)}) copy-start(bf16[640,5120]{1,0:T(8,128)(2,1)} %w_ref.1) | copy-start | bytes 19660804
  14.0 1.1 %copy-start.2 = (bf16[256,1280]{1,0:T(8,128)(2,1)S(1)}, bf16[256,1280]{1,0:T(8,128)(2,1)}, u32[]{:S(2)}) copy-start(bf16[256,1280]{1,0:T(8,128)(2,1)} %g_a.1) | copy-start | bytes 1966084
  15.1 15.2 %copy-start.1 = (bf16[256,640]{1,0:T(8,128)(2,1)S(1)}, bf16[256,640]{1,0:T(8,128)(2,1)}, u32[]{:S(2)}) copy-start(bf16[256,640]{1,0:T(8,128)(2,1)} %q_ref.4) | copy-start | bytes 983044
  15.1 15.2 %copy-start.5 = (s32[16,10]{1,0:T(8,128)S(1)}, s32[16,10]{1,0:T(8,128)}, u32[]{:S(2)}) copy-start(s32[16,10]{1,0:T(8,128)} %mask_ref.9) | copy-start | bytes 1924
  20.2 9.0 %collective-permute-start.6 = (bf16[256,1280]{1,0:T(8,128)(2,1)S(1)}, bf16[256,1280]{1,0:T(8,128)(2,1)S(1)}, u32[]{:S(2)}, u32[]{:S(2)}) collective-permute-start(bf16[256,1280]{1,0:T(8,128)(2,1)S(1)} %collective-permute-done.5.g_a), channel_id=1, source_target_pairs={{0,1},{1,0},{2,3},{3,2},{4,5},{5,4},{6,7},{7,6},{8,9},{9,8},{10,11... | collective-permute-start | bytes 1966088 | tf_op jit(solution)/shard_map/ppermute | solution.py:54
  25.6 12.5 %collective-permute-start.3 = (bf16[512,640]{1,0:T(8,128)(2,1)S(1)}, bf16[512,640]{1,0:T(8,128)(2,1)S(1)}, u32[]{:S(2)}, u32[]{:S(2)}) collective-permute-start(bf16[512,640]{1,0:T(8,128)(2,1)S(1)} %select_select_fusion), channel_id=1, source_target_pairs={{0,8},{1,5},{2,10},{3,7},{5,1},{7,3},{8,16},{9,13},{10,18},{11,15}... | collective-permute-start | bytes 1966088 | tf_op jit(solution)/shard_map/ppermute | solution.py:54
  39.7 8.8 %collective-permute-start.11 = (bf16[720,256]{1,0:T(8,128)(2,1)S(1)}, bf16[720,256]{1,0:T(8,128)(2,1)S(1)}, u32[]{:S(2)}, u32[]{:S(2)}) collective-permute-start(bf16[720,256]{1,0:T(8,128)(2,1)S(1)} %get-tuple-element.33), channel_id=1, source_target_pairs={{0,4},{1,5},{2,6},{3,7},{4,0},{5,1},{6,2},{7,3},{8,12},{9,13},{10,... | collective-permute-start | bytes 1105928 | tf_op jit(solution)/shard_map/ppermute | solution.py:54
  40.3 13.4 %collective-permute-start.12 = (bf16[720,256]{1,0:T(8,128)(2,1)S(1)}, bf16[720,256]{1,0:T(8,128)(2,1)S(1)}, u32[]{:S(2)}, u32[]{:S(2)}) collective-permute-start(bf16[720,256]{1,0:T(8,128)(2,1)S(1)} %get-tuple-element.33), channel_id=1, source_target_pairs={{0,8},{1,9},{2,10},{3,11},{4,12},{5,13},{6,14},{7,15},{8,0},{9,1},... | collective-permute-start | bytes 1105928 | tf_op jit(solution)/shard_map/ppermute | solution.py:54
  40.3 13.4 %collective-permute-start.13 = (bf16[720,256]{1,0:T(8,128)(2,1)S(1)}, bf16[720,256]{1,0:T(8,128)(2,1)S(1)}, u32[]{:S(2)}, u32[]{:S(2)}) collective-permute-start(bf16[720,256]{1,0:T(8,128)(2,1)S(1)} %get-tuple-element.33), channel_id=1, source_target_pairs={{8,16},{9,17},{10,18},{11,19},{12,20},{13,21},{14,22},{15,23},{16,... | collective-permute-start | bytes 1105928 | tf_op jit(solution)/shard_map/ppermute | solution.py:54
  43.9 13.5 %collective-permute-start.7 = (bf16[256,640]{1,0:T(8,128)(2,1)S(1)}, bf16[256,640]{1,0:T(8,128)(2,1)S(1)}, u32[]{:S(2)}, u32[]{:S(2)}) collective-permute-start(bf16[256,640]{1,0:T(8,128)(2,1)S(1)} %copy-done.1), channel_id=1, source_target_pairs={{0,8},{1,9},{2,10},{3,11},{4,12},{5,13},{6,14},{7,15},{8,0},{9,1},... | collective-permute-start | bytes 983048 | tf_op jit(solution)/shard_map/ppermute | solution.py:54
  44.0 13.6 %collective-permute-start.8 = (bf16[256,640]{1,0:T(8,128)(2,1)S(1)}, bf16[256,640]{1,0:T(8,128)(2,1)S(1)}, u32[]{:S(2)}, u32[]{:S(2)}) collective-permute-start(bf16[256,640]{1,0:T(8,128)(2,1)S(1)} %copy-done.1), channel_id=1, source_target_pairs={{8,16},{9,17},{10,18},{11,19},{12,20},{13,21},{14,22},{15,23},{16,... | collective-permute-start | bytes 983048 | tf_op jit(solution)/shard_map/ppermute | solution.py:54
  48.5 9.1 %collective-permute-start.9 = (bf16[256,640]{1,0:T(8,128)(2,1)S(1)}, bf16[256,640]{1,0:T(8,128)(2,1)S(1)}, u32[]{:S(2)}, u32[]{:S(2)}) collective-permute-start(bf16[256,640]{1,0:T(8,128)(2,1)S(1)} %copy-done.1), channel_id=1, source_target_pairs={{0,4},{1,5},{2,6},{3,7},{4,0},{5,1},{6,2},{7,3},{8,12},{9,13},{10,... | collective-permute-start | bytes 983048 | tf_op jit(solution)/shard_map/ppermute | solution.py:54
  53.8 12.9 %collective-permute-start.14 = (bf16[720,256]{1,0:T(8,128)(2,1)S(1)}, bf16[720,256]{1,0:T(8,128)(2,1)S(1)}, u32[]{:S(2)}, u32[]{:S(2)}) collective-permute-start(bf16[720,256]{1,0:T(8,128)(2,1)S(1)} %select_select_fusion.1), channel_id=1, source_target_pairs={{0,8},{1,5},{2,10},{3,7},{5,1},{7,3},{8,16},{9,13},{10,18},{11,15}... | collective-permute-start | bytes 1105928 | tf_op jit(solution)/shard_map/ppermute | solution.py:54
  57.6 9.1 %collective-permute-start.10 = (bf16[256,640]{1,0:T(8,128)(2,1)S(1)}, bf16[256,640]{1,0:T(8,128)(2,1)S(1)}, u32[]{:S(2)}, u32[]{:S(2)}) collective-permute-start(bf16[256,640]{1,0:T(8,128)(2,1)S(1)} %select_select_fusion.2), channel_id=1, source_target_pairs={{0,8},{1,5},{2,10},{3,7},{5,1},{7,3},{8,16},{9,13},{10,18},{11,15}... | collective-permute-start | bytes 983048 | tf_op jit(solution)/shard_map/ppermute | solution.py:54

commit v4 on v3

--- a/solution.py
+++ b/solution.py
@@ -11,7 +11,9 @@
 HEAD_DIM = 128
 TILE = 128
 SPAN = 2
-STAT_ROWS = 16
+RUN_ROWS = 16
+STATS = 6
+STAT_TILE = 16
 SCALE = 1.0 / math.sqrt(HEAD_DIM)
 SCALE_LOG2 = SCALE * math.log2(math.e)
 BOTH = ("ctx", "head")
@@ -19,6 +21,7 @@
 TN = (((0,), (0,)), ((), ()))
 NN = (((1,), (0,)), ((), ()))
 VMEM_LIMIT = 16 * 1024 * 1024
+VMEM_PACK = 60 * 1024 * 1024
 VMEM_ALONE = 32 * 1024 * 1024
 VMEM = pl.BlockSpec(memory_space=pltpu.VMEM)
 SMEM = pl.BlockSpec(memory_space=pltpu.SMEM)
@@ -86,11 +89,12 @@
     return lax.optimization_barrier((value,) + others)[0]
 
 
-def pack_kernel(k_ref, v_ref, out_ref, sems):
-    rows = k_ref.shape[0]
+def pack_kernel(*refs):
+    arrays, out_ref, sems = refs[:-2], refs[-2], refs[-1]
+    rows = arrays[0].shape[0]
     copies = [
-        pltpu.make_async_copy(k_ref, out_ref.at[:rows], sems.at[0]),
-        pltpu.make_async_copy(v_ref, out_ref.at[rows:], sems.at[1]),
+        pltpu.make_async_copy(ref, out_ref.at[n * rows:(n + 1) * rows], sems.at[n])
+        for n, ref in enumerate(arrays)
     ]
     for copy in copies:
         copy.start()
@@ -98,19 +102,20 @@
         copy.wait()
 
 
-def pack(keys, values):
-    rows, feat = keys.shape
+def pack(*arrays):
+    rows, feat = arrays[0].shape
+    count = len(arrays)
     return pl.pallas_call(
         pack_kernel,
-        in_specs=[ANY] * 2,
+        in_specs=[ANY] * count,
         out_specs=VMEM,
-        out_shape=jax.ShapeDtypeStruct((2 * rows, feat), keys.dtype),
-        scratch_shapes=[pltpu.SemaphoreType.DMA((2,))],
-        compiler_params=pltpu.CompilerParams(vmem_limit_bytes=VMEM_LIMIT),
+        out_shape=jax.ShapeDtypeStruct((count * rows, feat), arrays[0].dtype),
+        scratch_shapes=[pltpu.SemaphoreType.DMA((count,))],
+        compiler_params=pltpu.CompilerParams(vmem_limit_bytes=VMEM_PACK),
         cost_estimate=pl.CostEstimate(
-            flops=0, bytes_accessed=60_000_000, transcendentals=0
+            flops=0, bytes_accessed=4 * count * rows * feat, transcendentals=0
         ),
-    )(keys, values)
+    )(*arrays)
 
 
 def begin_kernel(order_ref, w_ref, g_a, g_b, out_ref, kept_ref, used, sems):
@@ -172,8 +177,8 @@
     return slice(head * HEAD_DIM, (head + 1) * HEAD_DIM)
 
 
-def stat_slice(head, start=0):
-    return slice(start + head * STAT_ROWS, start + (head + 1) * STAT_ROWS)
+def stat_rows(heads):
+    return -(-heads * STATS // STAT_TILE) * STAT_TILE
 
 
 def bias_row(live_flags):
@@ -257,58 +262,58 @@
         finish(*step, now)
 
 
-def forward_kernel(which, pos_ref, mask_ref, q_ref, *rest):
+def forward_kernel(which, pos_ref, mask_ref, *rest):
     windows, (out_ref, run_ref) = rest[:len(which)], rest[len(which):]
     pos = pos_ref[0]
-    rows, feat = q_ref.shape
+    feat, rows = out_ref.shape
     biases = window_bias(mask_ref, pos, rows // TILE, which)
 
     def scores_of(head):
         cols = columns(head)
-        q = q_ref[:, cols]
+        q = windows[0][2 * rows:, cols]
         return [dot(w[:rows, cols], q, NT) for w in windows]
 
     def finish(head, scores):
         cols = columns(head)
 
         def values_of(n):
-            return windows[n][rows:, cols]
+            return windows[n][rows:2 * rows, cols]
 
         shifted, top = softmax_part(scores, biases)
         totals, out = weighted_values(shifted, top, values_of)
         out_ref[cols, :] = out
-        at = head * STAT_ROWS
+        at = head * RUN_ROWS
         run_ref[at:at + 8, :] = jnp.broadcast_to(top, (8, rows))
         run_ref[at + 8:at + 16, :] = jnp.broadcast_to(totals, (8, rows))
 
     in_order([(head,) for head in range(feat // HEAD_DIM)], scores_of, finish)
 
 
-def forward_part(pos, tile_mask, queries, which, windows):
-    rows, feat = queries.shape
+def forward_part(pos, tile_mask, own, which, windows):
+    rows, feat = own.shape[0] // 3, own.shape[1]
     heads = feat // HEAD_DIM
     return kernel_call(
         functools.partial(forward_kernel, which),
         [
             jax.ShapeDtypeStruct((feat, rows), jnp.float32),
-            jax.ShapeDtypeStruct((heads * STAT_ROWS, rows), jnp.float32),
+            jax.ShapeDtypeStruct((heads * RUN_ROWS, rows), jnp.float32),
         ],
-        [pos, tile_mask, queries, *windows],
+        [pos, tile_mask, own, *windows],
         4 * len(which) * rows * rows * feat,
         len(which) * rows * rows * heads,
     )
 
 
 def statistics_kernel(
-    which, pos_ref, mask_ref, q_ref, w_ref, out_in, run_in, d_ref, stats_ref, packed_ref
+    which, pos_ref, mask_ref, own_ref, w_ref, out_in, run_in, d_ref, stats_ref, packed_ref
 ):
     pos = pos_ref[0]
-    rows, feat = q_ref.shape
+    feat, rows = d_ref.shape
     biases = window_bias(mask_ref, pos, rows // TILE, [which])
 
     def scores_of(head):
         cols = columns(head)
-        return [dot(w_ref[:rows, cols], q_ref[:, cols], NT)]
+        return [dot(w_ref[:rows, cols], own_ref[2 * rows:, cols], NT)]
 
     def finish(head, scores):
         cols = columns(head)
@@ -316,7 +321,7 @@
         def values_of(n):
             return w_ref[rows:, cols]
 
-        at = head * STAT_ROWS
+        at = head * RUN_ROWS
         top_before, totals_before = run_in[at:at + 1, :], run_in[at + 8:at + 9, :]
         shifted, top = softmax_part(scores, biases)
         top = jnp.maximum(top, top_before)
@@ -326,41 +331,44 @@
         out = out + out_in[cols, :] * shrink
         attn_out = (out / totals).astype(jnp.bfloat16).astype(jnp.float32)
         delta = jnp.sum(d_ref[cols, :].astype(jnp.float32) * attn_out, axis=0, keepdims=True)
-        row = lax.broadcasted_iota(jnp.int32, (STAT_ROWS, rows), 0)
-        stats = jnp.zeros((STAT_ROWS, rows), jnp.float32)
-        place = 0
+        place = head * STATS
         for stat in (top + jnp.log2(totals), delta):
             for _ in range(3):
                 piece = stat.astype(jnp.bfloat16).astype(jnp.float32)
-                stats = jnp.where(row == place, piece, stats)
+                all_stats[0] = jnp.where(row == place, piece, all_stats[0])
                 stat = stat - piece
                 place += 1
-        stats_ref[stat_slice(head), :] = stats.astype(jnp.bfloat16)
         packed_ref[cols, :] = d_ref[cols, :]
-        packed_ref[stat_slice(head, feat), :] = stats.astype(jnp.bfloat16)
-
+
+    row = lax.broadcasted_iota(jnp.int32, stats_ref.shape, 0)
+    all_stats = [jnp.zeros(stats_ref.shape, jnp.float32)]
     in_order([(head,) for head in range(feat // HEAD_DIM)], scores_of, finish)
-
-
-def statistics(pos, tile_mask, queries, which, window, out, run, d_out_t):
-    rows, feat = queries.shape
+    stats_ref[...] = all_stats[0].astype(jnp.bfloat16)
+    packed_ref[feat:, :] = all_stats[0].astype(jnp.bfloat16)
+
+
+def statistics(pos, tile_mask, own, which, window, out, run, d_out_t):
+    feat, rows = d_out_t.shape
     heads = feat // HEAD_DIM
     return kernel_call(
         functools.partial(statistics_kernel, which),
         [
-            jax.ShapeDtypeStruct((heads * STAT_ROWS, rows), jnp.bfloat16),
-            jax.ShapeDtypeStruct((feat + heads * STAT_ROWS, rows), jnp.bfloat16),
+            jax.ShapeDtypeStruct((stat_rows(heads), rows), jnp.bfloat16),
+            jax.ShapeDtypeStruct((feat + stat_rows(heads), rows), jnp.bfloat16),
         ],
-        [pos, tile_mask, queries, window, out, run, d_out_t],
+        [pos, tile_mask, own, window, out, run, d_out_t],
         4 * rows * rows * feat,
         rows * rows * heads,
     )
 
 
-def block_grads(scores, dprobs, bias_rows, stats):
-    stats = stats.astype(jnp.float32)
-    lse = stats[0:1] + stats[1:2] + stats[2:3]
-    delta = stats[3:4] + stats[4:5] + stats[5:6]
+def statistics_of(ref, start, head):
+    stats = ref[start:, :].astype(jnp.float32)
+    rows = [stats[head * STATS + n:head * STATS + n + 1] for n in range(STATS)]
+    return rows[0] + rows[1] + rows[2], rows[3] + rows[4] + rows[5]
+
+
+def block_grads(scores, dprobs, bias_rows, lse, delta):
     probs = jnp.concatenate(
         [
             jnp.exp2(scores[b * TILE:(b + 1) * TILE] * SCALE_LOG2 + (row - lse))
@@ -372,11 +380,11 @@
     return probs.astype(jnp.bfloat16), dscores.astype(jnp.bfloat16)
 
 
-def query_kernel(which, pos_ref, mask_ref, q_ref, *rest):
+def query_kernel(which, pos_ref, mask_ref, *rest):
     count = len(which)
     windows = rest[:count]
     d_ref, s_ref, dq_ref, dk_ref, dv_ref = rest[count:]
-    rows, feat = q_ref.shape
+    rows, feat = dq_ref.shape
     biases = window_bias(mask_ref, pos_ref[0], rows // TILE, which)
     sums = [None]
 
@@ -384,22 +392,25 @@
         return windows[n][:rows, cols]
 
     def values_of(n, cols):
-        return windows[n][rows:, cols]
+        return windows[n][rows:2 * rows, cols]
+
+    def queries_of(cols):
+        return windows[0][2 * rows:, cols]
 
     def products(head, n):
         cols = columns(head)
         return (
-            dot(keys_of(n, cols), q_ref[:, cols], NT),
+            dot(keys_of(n, cols), queries_of(cols), NT),
             dot(values_of(n, cols), d_ref[cols, :], NN),
         )
 
     def finish(head, n, now):
         cols = columns(head)
-        probs, dscores = block_grads(*now, biases[n], s_ref[stat_slice(head), :])
+        probs, dscores = block_grads(*now, biases[n], *statistics_of(s_ref, 0, head))
         part = dot(keys_of(n, cols), dscores, TN)
         if n == 0:
             sums[0] = part
-            dk_ref[:, cols] = dot(dscores, q_ref[:, cols], NN)
+            dk_ref[:, cols] = dot(dscores, queries_of(cols), NN)
             dv_ref[:, cols] = dot(probs, d_ref[cols, :], NT)
         else:
             sums[0] = sums[0] + part
@@ -410,19 +421,19 @@
     in_order(steps, products, finish)
 
 
-def query_side(pos, tile_mask, queries, which, windows, d_out_t, stats):
-    rows, feat = queries.shape
+def query_side(pos, tile_mask, own, which, windows, d_out_t, stats):
+    feat, rows = d_out_t.shape
     total = jax.ShapeDtypeStruct((rows, feat), jnp.float32)
     return kernel_call(
         functools.partial(query_kernel, which),
         [jax.ShapeDtypeStruct((rows, feat), jnp.bfloat16), total, total],
-        [pos, tile_mask, queries, *windows, d_out_t, stats],
+        [pos, tile_mask, own, *windows, d_out_t, stats],
         34 * rows * rows * feat,
         5 * rows * rows * feat // HEAD_DIM,
     )
 
 
-def key_kernel(which, final, pos_ref, mask_ref, kv_ref, *rest):
+def key_kernel(which, final, pos_ref, mask_ref, own_ref, *rest):
     count = len(which)
     sources = [rest[3 * n:3 * n + 3] for n in range(count)]
     dk_in, dv_in, dk_ref, dv_ref = rest[3 * count:]
@@ -434,18 +445,18 @@
         cols = columns(head)
         q_ref, d_ref, _ = sources[n]
         return (
-            dot(kv_ref[:rows, cols], q_ref[:, cols], NT),
-            dot(kv_ref[rows:, cols], d_ref[cols, :], NN),
+            dot(own_ref[:rows, cols], q_ref[q_ref.shape[0] - rows:, cols], NT),
+            dot(own_ref[rows:2 * rows, cols], d_ref[cols, :], NN),
         )
 
     def finish(head, n, now):
         cols = columns(head)
         q_ref, d_ref, s_ref = sources[n]
         start = feat if s_ref.shape[0] > feat else 0
-        probs, dscores = block_grads(*now, biases[n], s_ref[stat_slice(head, start), :])
+        probs, dscores = block_grads(*now, biases[n], *statistics_of(s_ref, start, head))
         before = (dk_in[:, cols], dv_in[:, cols]) if n == 0 else sums
         sums[:] = [
-            before[0] + dot(dscores, q_ref[:, cols], NN),
+            before[0] + dot(dscores, q_ref[q_ref.shape[0] - rows:, cols], NN),
             before[1] + dot(probs, d_ref[cols, :], NT),
         ]
         if n == count - 1:
@@ -457,9 +468,9 @@
     in_order(steps, products, finish)
 
 
-def key_side(pos, tile_mask, kv, sources, begun, final):
+def key_side(pos, tile_mask, own, sources, begun, final):
     rows, feat = begun[0].shape
-    operands = [pos, tile_mask, kv]
+    operands = [pos, tile_mask, own]
     for _, q, d, s in sources:
         operands += [q, d, s]
     which = [source[0] for source in sources]
@@ -474,6 +485,7 @@
 
 
 def local(queries, keys, values, out_weight, reward_grad, tile_mask):
+    rows = queries.shape[0]
     ctx = lax.axis_index("ctx").astype(jnp.int32)
     head = lax.axis_index("head").astype(jnp.int32)
     pos = ctx.reshape(1)
@@ -483,43 +495,44 @@
         return jnp.where(head % 2 == 1, jnp.where(a_is_held, a, b), x)
 
     far = send(reward_grad, lambda c, h: (c, h ^ 2))
-    kv = pack(keys, values)
-    kv_b = send(kv, odd_chain)
-    kv_a = send(kv, even_chain)
-    kv_x = send(kv, in_pair)
-    near = send(after(reward_grad, kv), lambda c, h: (c, h ^ 1))
+    kvq = pack(keys, values, queries)
+    kvq_b = send(kvq, odd_chain)
+    kvq_a = send(kvq, even_chain)
+    kvq_x = send(kvq, in_pair)
+    near = send(after(reward_grad, kvq), lambda c, h: (c, h ^ 1))
     order = jnp.stack([head, head ^ 1, head ^ 2, head ^ 3])
     begun, kept = begin_project(order, out_weight, reward_grad, near)
     far = after(far, begun)
     far_near = send(far, lambda c, h: (c, h ^ 1))
-    kv_g = send(second_step(kv_x, kv_a, kv_b), forward)
-    d_out_t = end_project(kept, far, far_near, begun)
+    second = second_step(kvq_x, kvq_a, kvq_b)
+    kv_g = send(second[:2 * rows], forward)
+    d_out_t = end_project(kept, far, far_near, after(begun, second))
     out, run = forward_part(
-        pos, tile_mask, after(queries, d_out_t), [0, 1, 2, 3], [kv, kv_x, kv_a, kv_b]
-    )
-    late_queries = after(queries, out)
-    q_b = send(late_queries, odd_chain)
-    q_a = send(late_queries, even_chain)
-    q_x = send(late_queries, in_pair)
-    stats, packed = statistics(pos, tile_mask, queries, 4, kv_g, out, run, d_out_t)
+        pos, tile_mask, after(kvq, d_out_t), [0, 1, 2, 3], [kvq_x, kvq_a, kvq_b]
+    )
+    stats, packed = statistics(pos, tile_mask, kvq, 4, kv_g, out, run, d_out_t)
+    q_g = send(after(second[2 * rows:], out), forward)
+    d_g = send(d_out_t, across)
     p_b = send(packed, odd_chain)
     p_a = send(packed, even_chain)
     p_x = send(packed, in_pair)
-    q_g = send(second_step(q_x, q_a, q_b), forward)
+    s_g = send(stats, across)
     grad_queries, *begun_keys = query_side(
-        pos, tile_mask, queries, [0, 1, 2, 3, 4], [kv, kv_x, kv_a, kv_b, kv_g], d_out_t, stats
-    )
-    p_g = send(second_step(*after((p_x, p_a, p_b), grad_queries)), forward)
-    begun_keys = key_side(
+        pos, tile_mask, kvq, [0, 1, 2, 3, 4], [kvq_x, kvq_a, kvq_b, kv_g], d_out_t,
+        after(stats, q_g, d_g),
+    )
+    grad_keys, grad_values = key_side(
         pos,
         tile_mask,
-        kv,
-        [(1, q_x, p_x, p_x), (2, q_a, p_a, p_a), (3, q_b, p_b, p_b)],
+        kvq,
+        [
+            (4, q_g, d_g, s_g),
+            (1, kvq_x, p_x, p_x),
+            (2, kvq_a, p_a, p_a),
+            (3, kvq_b, p_b, p_b),
+        ],
         begun_keys,
-        False,
-    )
-    grad_keys, grad_values = key_side(
-        pos, tile_mask, kv, [(4, q_g, p_g, p_g)], begun_keys, True
+        True,
     )
     return (grad_queries, grad_keys, grad_values)
 

time: 70 us -> 65 us (0.929)
  starting transfers between devices: 26.5 us -> 23 us
  Pallas kernels: 18.6 us -> 20.8 us
  local copies, waits for them, and re-layouts: 5.89 us -> 4.04 us
  waiting for transfers between devices: 16.8 us -> 15.6 us
    ppermute x15 -> x13, starting transfers between devices: 26.5 us -> 23 us  [send(): return lax.ppermute(array, BOTH, pairs)]
    pallas_call x1, Pallas kernels: 0.22 us -> 2.16 us  [pack(): pl.pallas_call(pack_kernel, in_specs=[ANY] * count, out_specs=VMEM, out_s...]
    unnamed x12 -> x8, local copies, waits for them, and re-layouts: 5.89 us -> 3.96 us
    ppermute x15 -> x13, waiting for transfers between devices: 16.8 us -> 15.6 us  [send(): return lax.ppermute(array, BOTH, pairs)]
    pallas_call x6 -> x5, Pallas kernels: 15.2 us -> 15.4 us  [kernel_call(): pl.pallas_call(kernel, in_specs=[SMEM if x.dtype == jnp.int32 else VMEM f...]
  transfers between devices with their start and end apart: 15 -> 13, of which waited for: 8 -> 7; matrix products, arithmetic and copies ran while one was open for 0% -> 0% of each run, Pallas kernels for 21% -> 22%
where the time goes in v4:
time: 65 us; the launch traced here: 64.4 us
  starting transfers between devices  23 us (35%)
  Pallas kernels  20.8 us (32%)
  waiting for transfers between devices  15.6 us (24%)
  local copies, waits for them, and re-layouts  4.04 us (6%)
  between operations  0.8 us (1%)
    ppermute x13, starting transfers between devices, send(): return lax.ppermute(array, BOTH, pairs)  23 us
    ppermute x13, waiting for transfers between devices, send(): return lax.ppermute(array, BOTH, pairs)  15.6 us
    pallas_call x5, Pallas kernels, kernel_call(): pl.pallas_call(kernel, in_specs=[SMEM if x.dtype == jnp.int32 else VMEM f...  15.4 us
    unnamed x8, local copies, waits for them, and re-layouts  3.96 us
    pallas_call x1, Pallas kernels, begin_project(): pl.pallas_call(begin_kernel, in_specs=[SMEM, ANY, VMEM, VMEM], out_specs=...  3.2 us
    pallas_call x1, Pallas kernels, pack(): pl.pallas_call(pack_kernel, in_specs=[ANY] * count, out_specs=VMEM, out_s...  2.16 us
  transfers between devices with their start and end apart: 13, of which 7 were waited for; matrix products, arithmetic and copies ran while one was open for 0% of the time, Pallas kernels for 22%

profile of v4, /device:TPU:8, one launch (start us, length us, event | category | flops | bytes accessed | tf_op | source)
XLA Modules:
  0.0 64.4 jit_solution(15407548070290792248)
XLA Ops:
  0.6 2.2 %shard_map.85.rest_0_.own_ref = bf16[768,640]{1,0:T(8,128)(2,1)} custom-call(bf16[256,640]{1,0:T(8,128)(2,1)} %refs_0_.1, bf16[256,640]{1,0:T(8,128)(2,1)} %refs_1_.1, bf16[256,640]{1,0:T(8,128)(2,1)} %refs_2_.1), custom_call_target="tpu_custom_call" | custom-call | bytes 1966080 | tf_op jit(solution)/shard_map/pallas_call | solution.py:108
  2.8 1.6 %collective-permute-start = (bf16[768,640]{1,0:T(8,128)(2,1)}, bf16[768,640]{1,0:T(8,128)(2,1)S(1)}, u32[]{:S(2)}, u32[]{:S(2)}) collective-permute-start(bf16[768,640]{1,0:T(8,128)(2,1)} %shard_map.85.rest_0_.own_ref), channel_id=1, source_target_pairs={{0,4},{1,5},{2,6},{3,7},{4,0},{5,1},{6,2},{7,3},{8,12},{9,13},{10,... | collective-permute-start | bytes 2949128 | tf_op jit(solution)/shard_map/ppermute | solution.py:57
  4.8 4.6 %collective-permute-start.2 = (bf16[768,640]{1,0:T(8,128)(2,1)}, bf16[768,640]{1,0:T(8,128)(2,1)S(1)}, u32[]{:S(2)}, u32[]{:S(2)}) collective-permute-start(bf16[768,640]{1,0:T(8,128)(2,1)} %shard_map.85.rest_0_.own_ref), channel_id=1, source_target_pairs={{8,16},{9,17},{10,18},{11,19},{12,20},{13,21},{14,22},{15,23},{16,... | collective-permute-start | bytes 2949128 | tf_op jit(solution)/shard_map/ppermute | solution.py:57
  9.5 1.6 %collective-permute-start.5 = (bf16[256,1280]{1,0:T(8,128)(2,1)}, bf16[256,1280]{1,0:T(8,128)(2,1)}, u32[]{:S(2)}, u32[]{:S(2)}) collective-permute-start(bf16[256,1280]{1,0:T(8,128)(2,1)} %g_a.1), channel_id=1, source_target_pairs={{0,2},{1,3},{2,0},{3,1},{4,6},{5,7},{6,4},{7,5},{8,10},{9,11},{10,... | collective-permute-start | bytes 1966088 | tf_op jit(solution)/shard_map/ppermute | solution.py:57
  11.2 0.8 %collective-permute-done.4.g_b = bf16[256,1280]{1,0:T(8,128)(2,1)} collective-permute-done((bf16[256,1280]{1,0:T(8,128)(2,1)}, bf16[256,1280]{1,0:T(8,128)(2,1)}, u32[]{:S(2)}, u32[]{:S(2)}) %collective-permute-start.4) | collective-permute-done | bytes 655392 | tf_op jit(solution)/shard_map/ppermute | solution.py:57
  11.9 2.9 %copy-done.1 = bf16[640,5120]{1,0:T(8,128)(2,1)S(1)} copy-done((bf16[640,5120]{1,0:T(8,128)(2,1)S(1)}, bf16[640,5120]{1,0:T(8,128)(2,1)}, u32[]{:S(2)}) %copy-start.1) | copy-done | bytes 6553624
  14.8 1.1 %copy-done.2 = bf16[256,1280]{1,0:T(8,128)(2,1)S(1)} copy-done((bf16[256,1280]{1,0:T(8,128)(2,1)S(1)}, bf16[256,1280]{1,0:T(8,128)(2,1)}, u32[]{:S(2)}) %copy-start.2) | copy-done | bytes 655384
  15.9 3.2 %shard_map.86 = (f32[640,256]{1,0:T(8,128)S(1)}, bf16[640,2560]{1,0:T(8,128)(2,1)S(1)}) custom-call(s32[4]{0:T(128)S(1)} %pad_add_fusion.order_ref, bf16[640,5120]{1,0:T(8,128)(2,1)S(1)} %copy-done.1, bf16[256,1280]{1,0:T(8,128)(2,1)S(1)} %copy-done.2, bf16[256,1280]{1,0:T(8,128)(2,1)} %collective-permute-done.4.g_b), custom_call_target="tpu_custom_call" | custom-call | flops 838860800 | bytes 6553600 | tf_op jit(solution)/shard_map/pallas_call | solution.py:140
  19.1 7.9 %collective-permute-done.5.g_a = bf16[256,1280]{1,0:T(8,128)(2,1)} collective-permute-done((bf16[256,1280]{1,0:T(8,128)(2,1)}, bf16[256,1280]{1,0:T(8,128)(2,1)}, u32[]{:S(2)}, u32[]{:S(2)}) %collective-permute-start.5) | collective-permute-done | bytes 655392 | tf_op jit(solution)/shard_map/ppermute | solution.py:57
  27.0 0.8 %collective-permute-done.1.rest_2_.rest_6_ = bf16[768,640]{1,0:T(8,128)(2,1)S(1)} collective-permute-done((bf16[768,640]{1,0:T(8,128)(2,1)}, bf16[768,640]{1,0:T(8,128)(2,1)S(1)}, u32[]{:S(2)}, u32[]{:S(2)}) %collective-permute-start.1) | collective-permute-done | bytes 983072 | tf_op jit(solution)/shard_map/ppermute | solution.py:57
  27.8 3.0 %collective-permute-done.2.rest_3_.rest_9_ = bf16[768,640]{1,0:T(8,128)(2,1)S(1)} collective-permute-done((bf16[768,640]{1,0:T(8,128)(2,1)}, bf16[768,640]{1,0:T(8,128)(2,1)S(1)}, u32[]{:S(2)}, u32[]{:S(2)}) %collective-permute-start.2) | collective-permute-done | bytes 983072 | tf_op jit(solution)/shard_map/ppermute | solution.py:57
  31.0 3.6 %collective-permute-start.3 = (bf16[512,640]{1,0:T(8,128)(2,1)S(1)}, bf16[512,640]{1,0:T(8,128)(2,1)S(1)}, u32[]{:S(2)}, u32[]{:S(2)}) collective-permute-start(bf16[512,640]{1,0:T(8,128)(2,1)S(1)} %slice.8), channel_id=1, source_target_pairs={{0,8},{1,5},{2,10},{3,7},{5,1},{7,3},{8,16},{9,13},{10,18},{11,15}... | collective-permute-start | bytes 1966088 | tf_op jit(solution)/shard_map/ppermute | solution.py:57
  34.7 2.1 %shard_map.87.d_ref.rest_5_ = bf16[640,256]{1,0:T(8,128)(2,1)S(1)} custom-call(bf16[640,2560]{1,0:T(8,128)(2,1)S(1)} %get-tuple-element.21.w_ref, bf16[256,1280]{1,0:T(8,128)(2,1)} %collective-permute-done.5.g_a, bf16[256,1280]{1,0:T(8,128)(2,1)S(1)} %collective-permute-done.6.g_b, f32[640,256]{1,0:T(8,128)S(1)} %get-tuple-element.24.begun), custom_call_target="tpu_custom_call" | custom-call | flops 838860800 | bytes 5242880 | tf_op jit(solution)/shard_map/pallas_call | solution.py:37
  36.9 2.6 %shard_map.88 = (f32[640,256]{1,0:T(8,128)S(1)}, f32[80,256]{1,0:T(8,128)S(1)}) custom-call(s32[1]{0:T(128)} %bitcast.pos_ref, s32[16,10]{1,0:T(8,128)S(1)} %copy-done.3, bf16[768,640]{1,0:T(8,128)(2,1)S(1)} %copy-done, bf16[768,640]{1,0:T(8,128)(2,1)S(1)} %collective-permute-done.rest_1_.rest_3_, ...), custom_call_target="tpu_custom_call" | custom-call | flops 671088640 | bytes 3932804 | tf_op jit(solution)/shard_map/pallas_call | solution.py:37
  39.5 1.9 %collective-permute-start.7 = (bf16[256,640]{1,0:T(8,128)(2,1)S(1)}, bf16[256,640]{1,0:T(8,128)(2,1)S(1)}, u32[]{:S(2)}, u32[]{:S(2)}) collective-permute-start(bf16[256,640]{1,0:T(8,128)(2,1)S(1)} %slice.9), channel_id=1, source_target_pairs={{0,8},{1,5},{2,10},{3,7},{5,1},{7,3},{8,16},{9,13},{10,18},{11,15}... | collective-permute-start | bytes 983048 | tf_op jit(solution)/shard_map/ppermute | solution.py:57
  41.4 1.9 %collective-permute-start.8 = (bf16[640,256]{1,0:T(8,128)(2,1)S(1)}, bf16[640,256]{1,0:T(8,128)(2,1)S(1)}, u32[]{:S(2)}, u32[]{:S(2)}) collective-permute-start(bf16[640,256]{1,0:T(8,128)(2,1)S(1)} %shard_map.87.d_ref.rest_5_), channel_id=1, source_target_pairs={{4,8},{5,9},{6,10},{7,11},{8,4},{9,5},{10,6},{11,7},{12,16},{13,17... | collective-permute-start | bytes 983048 | tf_op jit(solution)/shard_map/ppermute | solution.py:57
  43.5 1.6 %shard_map.89 = (bf16[32,256]{1,0:T(8,128)(2,1)S(1)}, bf16[672,256]{1,0:T(8,128)(2,1)S(1)}) custom-call(s32[1]{0:T(128)} %bitcast.pos_ref, s32[16,10]{1,0:T(8,128)S(1)} %copy-done.3, bf16[768,640]{1,0:T(8,128)(2,1)S(1)} %copy-done, bf16[512,640]{1,0:T(8,128)(2,1)S(1)} %collective-permute-done.3.w_ref.rest_4_, f32[640,256]{1,0:T(8,128)S(1)} %get-tuple-element.26.out_in, ...), custom_call_target="tpu_custom_call" | custom-call | flops 167772160 | bytes 2704004 | tf_op jit(solution)/shard_map/pallas_call | solution.py:37
  45.1 1.4 %collective-permute-start.10 = (bf16[672,256]{1,0:T(8,128)(2,1)S(1)}, bf16[672,256]{1,0:T(8,128)(2,1)S(1)}, u32[]{:S(2)}, u32[]{:S(2)}) collective-permute-start(bf16[672,256]{1,0:T(8,128)(2,1)S(1)} %get-tuple-element.32), channel_id=1, source_target_pairs={{0,4},{1,5},{2,6},{3,7},{4,0},{5,1},{6,2},{7,3},{8,12},{9,13},{10,... | collective-permute-start | bytes 1032200 | tf_op jit(solution)/shard_map/ppermute | solution.py:57
  46.4 2.0 %collective-permute-start.11 = (bf16[672,256]{1,0:T(8,128)(2,1)S(1)}, bf16[672,256]{1,0:T(8,128)(2,1)S(1)}, u32[]{:S(2)}, u32[]{:S(2)}) collective-permute-start(bf16[672,256]{1,0:T(8,128)(2,1)S(1)} %get-tuple-element.32), channel_id=1, source_target_pairs={{0,8},{1,9},{2,10},{3,11},{4,12},{5,13},{6,14},{7,15},{8,0},{9,1},... | collective-permute-start | bytes 1032200 | tf_op jit(solution)/shard_map/ppermute | solution.py:57
  48.5 1.9 %collective-permute-start.12 = (bf16[672,256]{1,0:T(8,128)(2,1)S(1)}, bf16[672,256]{1,0:T(8,128)(2,1)S(1)}, u32[]{:S(2)}, u32[]{:S(2)}) collective-permute-start(bf16[672,256]{1,0:T(8,128)(2,1)S(1)} %get-tuple-element.32), channel_id=1, source_target_pairs={{8,16},{9,17},{10,18},{11,19},{12,20},{13,21},{14,22},{15,23},{16,... | collective-permute-start | bytes 1032200 | tf_op jit(solution)/shard_map/ppermute | solution.py:57
  50.4 1.9 %collective-permute-start.9 = (bf16[32,256]{1,0:T(8,128)(2,1)S(1)}, bf16[32,256]{1,0:T(8,128)(2,1)S(1)}, u32[]{:S(2)}, u32[]{:S(2)}) collective-permute-start(bf16[32,256]{1,0:T(8,128)(2,1)S(1)} %get-tuple-element.30.rest_6_), channel_id=1, source_target_pairs={{4,8},{5,9},{6,10},{7,11},{8,4},{9,5},{10,6},{11,7},{12,16},{13,17... | collective-permute-start | bytes 49160 | tf_op jit(solution)/shard_map/ppermute | solution.py:57
  52.3 2.6 %collective-permute-done.8.rest_1_ = bf16[640,256]{1,0:T(8,128)(2,1)S(1)} collective-permute-done((bf16[640,256]{1,0:T(8,128)(2,1)S(1)}, bf16[640,256]{1,0:T(8,128)(2,1)S(1)}, u32[]{:S(2)}, u32[]{:S(2)}) %collective-permute-start.8) | collective-permute-done | bytes 327712 | tf_op jit(solution)/shard_map/ppermute | solution.py:57
  54.9 4.6 %shard_map.90 = (bf16[256,640]{1,0:T(8,128)(2,1)}, f32[256,640]{1,0:T(8,128)S(1)}, f32[256,640]{1,0:T(8,128)S(1)}) custom-call(s32[1]{0:T(128)} %bitcast.pos_ref, s32[16,10]{1,0:T(8,128)S(1)} %copy-done.3, bf16[768,640]{1,0:T(8,128)(2,1)S(1)} %copy-done, bf16[768,640]{1,0:T(8,128)(2,1)S(1)} %collective-permute-done.rest_1_.rest_3_, ...), custom_call_target="tpu_custom_call" | custom-call | flops 1426063360 | bytes 4932228 | tf_op jit(solution)/shard_map/pallas_call | solution.py:37
  60.0 4.5 %shard_map.91 = (bf16[256,640]{1,0:T(8,128)(2,1)}, bf16[256,640]{1,0:T(8,128)(2,1)}) custom-call(s32[1]{0:T(128)} %bitcast.pos_ref, s32[16,10]{1,0:T(8,128)S(1)} %copy-done.3, bf16[768,640]{1,0:T(8,128)(2,1)S(1)} %copy-done, bf16[256,640]{1,0:T(8,128)(2,1)S(1)} %collective-permute-done.7.rest_0_, bf16[640,256]{1,0:T(8,128)(2,1)S(1)} %collective-permute-done.8.rest_1_, ...), custom_call_target="tpu_custom_call" | custom-call | flops 1342177280 | bytes 7979652 | tf_op jit(solution)/shard_map/pallas_call | solution.py:37
  (21 shorter events, 1.4 us)
Async XLA Ops:
  2.8 24.2 %collective-permute-start = (bf16[768,640]{1,0:T(8,128)(2,1)}, bf16[768,640]{1,0:T(8,128)(2,1)S(1)}, u32[]{:S(2)}, u32[]{:S(2)}) collective-permute-start(bf16[768,640]{1,0:T(8,128)(2,1)} %shard_map.85.rest_0_.own_ref), channel_id=1, source_target_pairs={{0,4},{1,5},{2,6},{3,7},{4,0},{5,1},{6,2},{7,3},{8,12},{9,13},{10,... | collective-permute-start | bytes 2949128 | tf_op jit(solution)/shard_map/ppermute | solution.py:57
  4.4 23.4 %collective-permute-start.1 = (bf16[768,640]{1,0:T(8,128)(2,1)}, bf16[768,640]{1,0:T(8,128)(2,1)S(1)}, u32[]{:S(2)}, u32[]{:S(2)}) collective-permute-start(bf16[768,640]{1,0:T(8,128)(2,1)} %shard_map.85.rest_0_.own_ref), channel_id=1, source_target_pairs={{0,8},{1,9},{2,10},{3,11},{4,12},{5,13},{6,14},{7,15},{8,0},{9,1},... | collective-permute-start | bytes 2949128 | tf_op jit(solution)/shard_map/ppermute | solution.py:57
  4.8 26.0 %collective-permute-start.2 = (bf16[768,640]{1,0:T(8,128)(2,1)}, bf16[768,640]{1,0:T(8,128)(2,1)S(1)}, u32[]{:S(2)}, u32[]{:S(2)}) collective-permute-start(bf16[768,640]{1,0:T(8,128)(2,1)} %shard_map.85.rest_0_.own_ref), channel_id=1, source_target_pairs={{8,16},{9,17},{10,18},{11,19},{12,20},{13,21},{14,22},{15,23},{16,... | collective-permute-start | bytes 2949128 | tf_op jit(solution)/shard_map/ppermute | solution.py:57
  9.4 2.5 %collective-permute-start.4 = (bf16[256,1280]{1,0:T(8,128)(2,1)}, bf16[256,1280]{1,0:T(8,128)(2,1)}, u32[]{:S(2)}, u32[]{:S(2)}) collective-permute-start(bf16[256,1280]{1,0:T(8,128)(2,1)} %g_a.1), channel_id=1, source_target_pairs={{0,1},{1,0},{2,3},{3,2},{4,5},{5,4},{6,7},{7,6},{8,9},{9,8},{10,11... | collective-permute-start | bytes 1966088 | tf_op jit(solution)/shard_map/ppermute | solution.py:57
  9.5 17.5 %collective-permute-start.5 = (bf16[256,1280]{1,0:T(8,128)(2,1)}, bf16[256,1280]{1,0:T(8,128)(2,1)}, u32[]{:S(2)}, u32[]{:S(2)}) collective-permute-start(bf16[256,1280]{1,0:T(8,128)(2,1)} %g_a.1), channel_id=1, source_target_pairs={{0,2},{1,3},{2,0},{3,1},{4,6},{5,7},{6,4},{7,5},{8,10},{9,11},{10,... | collective-permute-start | bytes 1966088 | tf_op jit(solution)/shard_map/ppermute | solution.py:57
  11.9 2.9 %copy-start.1 = (bf16[640,5120]{1,0:T(8,128)(2,1)S(1)}, bf16[640,5120]{1,0:T(8,128)(2,1)}, u32[]{:S(2)}) copy-start(bf16[640,5120]{1,0:T(8,128)(2,1)} %w_ref.1) | copy-start | bytes 19660804
  14.8 1.1 %copy-start.2 = (bf16[256,1280]{1,0:T(8,128)(2,1)S(1)}, bf16[256,1280]{1,0:T(8,128)(2,1)}, u32[]{:S(2)}) copy-start(bf16[256,1280]{1,0:T(8,128)(2,1)} %g_a.1) | copy-start | bytes 1966084
  19.1 17.8 %copy-start = (bf16[768,640]{1,0:T(8,128)(2,1)S(1)}, bf16[768,640]{1,0:T(8,128)(2,1)}, u32[]{:S(2)}) copy-start(bf16[768,640]{1,0:T(8,128)(2,1)} %shard_map.85.rest_0_.own_ref) | copy-start | bytes 2949124
  19.1 17.8 %copy-start.3 = (s32[16,10]{1,0:T(8,128)S(1)}, s32[16,10]{1,0:T(8,128)}, u32[]{:S(2)}) copy-start(s32[16,10]{1,0:T(8,128)} %mask_ref.7) | copy-start | bytes 1924
  27.0 7.8 %collective-permute-start.6 = (bf16[256,1280]{1,0:T(8,128)(2,1)}, bf16[256,1280]{1,0:T(8,128)(2,1)S(1)}, u32[]{:S(2)}, u32[]{:S(2)}) collective-permute-start(bf16[256,1280]{1,0:T(8,128)(2,1)} %collective-permute-done.5.g_a), channel_id=1, source_target_pairs={{0,1},{1,0},{2,3},{3,2},{4,5},{5,4},{6,7},{7,6},{8,9},{9,8},{10,11... | collective-permute-start | bytes 1966088 | tf_op jit(solution)/shard_map/ppermute | solution.py:57
  31.0 12.5 %collective-permute-start.3 = (bf16[512,640]{1,0:T(8,128)(2,1)S(1)}, bf16[512,640]{1,0:T(8,128)(2,1)S(1)}, u32[]{:S(2)}, u32[]{:S(2)}) collective-permute-start(bf16[512,640]{1,0:T(8,128)(2,1)S(1)} %slice.8), channel_id=1, source_target_pairs={{0,8},{1,5},{2,10},{3,7},{5,1},{7,3},{8,16},{9,13},{10,18},{11,15}... | collective-permute-start | bytes 1966088 | tf_op jit(solution)/shard_map/ppermute | solution.py:57
  39.5 10.9 %collective-permute-start.7 = (bf16[256,640]{1,0:T(8,128)(2,1)S(1)}, bf16[256,640]{1,0:T(8,128)(2,1)S(1)}, u32[]{:S(2)}, u32[]{:S(2)}) collective-permute-start(bf16[256,640]{1,0:T(8,128)(2,1)S(1)} %slice.9), channel_id=1, source_target_pairs={{0,8},{1,5},{2,10},{3,7},{5,1},{7,3},{8,16},{9,13},{10,18},{11,15}... | collective-permute-start | bytes 983048 | tf_op jit(solution)/shard_map/ppermute | solution.py:57
  41.4 13.5 %collective-permute-start.8 = (bf16[640,256]{1,0:T(8,128)(2,1)S(1)}, bf16[640,256]{1,0:T(8,128)(2,1)S(1)}, u32[]{:S(2)}, u32[]{:S(2)}) collective-permute-start(bf16[640,256]{1,0:T(8,128)(2,1)S(1)} %shard_map.87.d_ref.rest_5_), channel_id=1, source_target_pairs={{4,8},{5,9},{6,10},{7,11},{8,4},{9,5},{10,6},{11,7},{12,16},{13,17... | collective-permute-start | bytes 983048 | tf_op jit(solution)/shard_map/ppermute | solution.py:57
  45.1 14.9 %collective-permute-start.10 = (bf16[672,256]{1,0:T(8,128)(2,1)S(1)}, bf16[672,256]{1,0:T(8,128)(2,1)S(1)}, u32[]{:S(2)}, u32[]{:S(2)}) collective-permute-start(bf16[672,256]{1,0:T(8,128)(2,1)S(1)} %get-tuple-element.32), channel_id=1, source_target_pairs={{0,4},{1,5},{2,6},{3,7},{4,0},{5,1},{6,2},{7,3},{8,12},{9,13},{10,... | collective-permute-start | bytes 1032200 | tf_op jit(solution)/shard_map/ppermute | solution.py:57
  46.4 13.5 %collective-permute-start.11 = (bf16[672,256]{1,0:T(8,128)(2,1)S(1)}, bf16[672,256]{1,0:T(8,128)(2,1)S(1)}, u32[]{:S(2)}, u32[]{:S(2)}) collective-permute-start(bf16[672,256]{1,0:T(8,128)(2,1)S(1)} %get-tuple-element.32), channel_id=1, source_target_pairs={{0,8},{1,9},{2,10},{3,11},{4,12},{5,13},{6,14},{7,15},{8,0},{9,1},... | collective-permute-start | bytes 1032200 | tf_op jit(solution)/shard_map/ppermute | solution.py:57
  48.5 11.5 %collective-permute-start.12 = (bf16[672,256]{1,0:T(8,128)(2,1)S(1)}, bf16[672,256]{1,0:T(8,128)(2,1)S(1)}, u32[]{:S(2)}, u32[]{:S(2)}) collective-permute-start(bf16[672,256]{1,0:T(8,128)(2,1)S(1)} %get-tuple-element.32), channel_id=1, source_target_pairs={{8,16},{9,17},{10,18},{11,19},{12,20},{13,21},{14,22},{15,23},{16,... | collective-permute-start | bytes 1032200 | tf_op jit(solution)/shard_map/ppermute | solution.py:57
  50.4 9.6 %collective-permute-start.9 = (bf16[32,256]{1,0:T(8,128)(2,1)S(1)}, bf16[32,256]{1,0:T(8,128)(2,1)S(1)}, u32[]{:S(2)}, u32[]{:S(2)}) collective-permute-start(bf16[32,256]{1,0:T(8,128)(2,1)S(1)} %get-tuple-element.30.rest_6_), channel_id=1, source_target_pairs={{4,8},{5,9},{6,10},{7,11},{8,4},{9,5},{10,6},{11,7},{12,16},{13,17... | collective-permute-start | bytes 49160 | tf_op jit(solution)/shard_map/ppermute | solution.py:57

commit v5 on v4

--- a/solution.py
+++ b/solution.py
@@ -14,13 +14,14 @@
 RUN_ROWS = 16
 STATS = 6
 STAT_TILE = 16
+BLOCKS = 4
 SCALE = 1.0 / math.sqrt(HEAD_DIM)
 SCALE_LOG2 = SCALE * math.log2(math.e)
 BOTH = ("ctx", "head")
 NT = (((1,), (1,)), ((), ()))
 TN = (((0,), (0,)), ((), ()))
 NN = (((1,), (0,)), ((), ()))
-VMEM_LIMIT = 16 * 1024 * 1024
+VMEM_LIMIT = 32 * 1024 * 1024
 VMEM_PACK = 60 * 1024 * 1024
 VMEM_ALONE = 32 * 1024 * 1024
 VMEM = pl.BlockSpec(memory_space=pltpu.VMEM)
@@ -179,6 +180,11 @@
 
 def stat_rows(heads):
     return -(-heads * STATS // STAT_TILE) * STAT_TILE
+
+
+def block_rows(n, head, rows):
+    at = (head * BLOCKS + n) * rows
+    return slice(at, at + rows)
 
 
 def bias_row(live_flags):
@@ -239,7 +245,7 @@
     return shifted, jnp.max(top, axis=0, keepdims=True)
 
 
-def weighted_values(shifted, top, values_of):
+def weighted_values(shifted, top, values_of, keep=None):
     totals = out = None
     for n, parts in enumerate(shifted):
         weights = []
@@ -248,7 +254,10 @@
             weights.append(weight)
             part = over_keys(jnp.sum, weight)
             totals = part if totals is None else totals + part
-        part = dot(values_of(n), jnp.concatenate(weights, axis=0).astype(jnp.bfloat16), TN)
+        weights = jnp.concatenate(weights, axis=0)
+        if keep is not None:
+            keep(n, weights)
+        part = dot(values_of(n), weights.astype(jnp.bfloat16), TN)
         out = part if out is None else out + part
     return jnp.sum(totals, axis=0, keepdims=True), out
 
@@ -263,7 +272,7 @@
 
 
 def forward_kernel(which, pos_ref, mask_ref, *rest):
-    windows, (out_ref, run_ref) = rest[:len(which)], rest[len(which):]
+    windows, (out_ref, run_ref, kept_ref) = rest[:len(which)], rest[len(which):]
     pos = pos_ref[0]
     feat, rows = out_ref.shape
     biases = window_bias(mask_ref, pos, rows // TILE, which)
@@ -279,8 +288,11 @@
         def values_of(n):
             return windows[n][rows:2 * rows, cols]
 
+        def keep(n, weights):
+            kept_ref[block_rows(n, head, rows), :] = weights
+
         shifted, top = softmax_part(scores, biases)
-        totals, out = weighted_values(shifted, top, values_of)
+        totals, out = weighted_values(shifted, top, values_of, keep)
         out_ref[cols, :] = out
         at = head * RUN_ROWS
         run_ref[at:at + 8, :] = jnp.broadcast_to(top, (8, rows))
@@ -297,6 +309,7 @@
         [
             jax.ShapeDtypeStruct((feat, rows), jnp.float32),
             jax.ShapeDtypeStruct((heads * RUN_ROWS, rows), jnp.float32),
+            jax.ShapeDtypeStruct((len(which) * feat // HEAD_DIM * rows, rows), jnp.float32),
         ],
         [pos, tile_mask, own, *windows],
         4 * len(which) * rows * rows * feat,
@@ -380,108 +393,139 @@
     return probs.astype(jnp.bfloat16), dscores.astype(jnp.bfloat16)
 
 
-def query_kernel(which, pos_ref, mask_ref, *rest):
-    count = len(which)
-    windows = rest[:count]
-    d_ref, s_ref, dq_ref, dk_ref, dv_ref = rest[count:]
+def query_kernel(which, pos_ref, mask_ref, own_ref, *rest):
+    windows, rest = (own_ref,) + rest[:BLOCKS], rest[BLOCKS:]
+    d_ref, s_ref, run_ref, kept_ref, q_last, d_last, *outs = rest
+    dq_ref, dk_ref, dv_ref, scores_ref, dprobs_ref = outs
     rows, feat = dq_ref.shape
-    biases = window_bias(mask_ref, pos_ref[0], rows // TILE, which)
+    last_bias = window_bias(mask_ref, pos_ref[0], rows // TILE, which[BLOCKS:])[0]
     sums = [None]
 
-    def keys_of(n, cols):
-        return windows[n][:rows, cols]
-
-    def values_of(n, cols):
-        return windows[n][rows:2 * rows, cols]
-
-    def queries_of(cols):
-        return windows[0][2 * rows:, cols]
-
     def products(head, n):
         cols = columns(head)
-        return (
-            dot(keys_of(n, cols), queries_of(cols), NT),
-            dot(values_of(n, cols), d_ref[cols, :], NN),
-        )
+        keys, values = own_ref[:rows, cols], own_ref[rows:2 * rows, cols]
+        queries = own_ref[2 * rows:, cols]
+        if n < BLOCKS:
+            others = q_last[:, cols] if n == BLOCKS - 1 else windows[n + 1][2 * rows:, cols]
+            scores_ref[block_rows(n, head, rows), :] = dot(keys, others, NT)
+            scores = None
+        else:
+            dprobs_ref[head * rows:(head + 1) * rows, :] = dot(values, d_last[cols, :], NN)
+            scores = dot(windows[n][:rows, cols], queries, NT)
+        return scores, dot(windows[n][rows:2 * rows, cols], d_ref[cols, :], NN)
 
     def finish(head, n, now):
         cols = columns(head)
-        probs, dscores = block_grads(*now, biases[n], *statistics_of(s_ref, 0, head))
-        part = dot(keys_of(n, cols), dscores, TN)
+        scores, dprobs = now
+        lse, delta = statistics_of(s_ref, 0, head)
+        if n < BLOCKS:
+            at = head * RUN_ROWS
+            factor = jnp.exp2(run_ref[at:at + 1, :] - lse)
+            probs = kept_ref[block_rows(n, head, rows), :] * factor
+            dscores = (probs * (dprobs - delta)).astype(jnp.bfloat16)
+        else:
+            _, dscores = block_grads(scores, dprobs, last_bias, lse, delta)
+        part = dot(windows[n][:rows, cols], dscores, TN)
         if n == 0:
             sums[0] = part
-            dk_ref[:, cols] = dot(dscores, queries_of(cols), NN)
-            dv_ref[:, cols] = dot(probs, d_ref[cols, :], NT)
+            dk_ref[:, cols] = dot(dscores, own_ref[2 * rows:, cols], NN)
+            dv_ref[:, cols] = dot(probs.astype(jnp.bfloat16), d_ref[cols, :], NT)
         else:
             sums[0] = sums[0] + part
-        if n == count - 1:
+        if n == BLOCKS:
             dq_ref[:, cols] = jnp.transpose(sums[0] * SCALE).astype(dq_ref.dtype)
 
-    steps = [(head, n) for head in range(feat // HEAD_DIM) for n in range(count)]
+    steps = [(head, n) for head in range(feat // HEAD_DIM) for n in range(BLOCKS + 1)]
     in_order(steps, products, finish)
 
 
-def query_side(pos, tile_mask, own, which, windows, d_out_t, stats):
+def query_side(pos, tile_mask, own, which, windows, d_out_t, stats, run, kept, q_last, d_last):
     feat, rows = d_out_t.shape
+    heads = feat // HEAD_DIM
     total = jax.ShapeDtypeStruct((rows, feat), jnp.float32)
     return kernel_call(
         functools.partial(query_kernel, which),
-        [jax.ShapeDtypeStruct((rows, feat), jnp.bfloat16), total, total],
-        [pos, tile_mask, own, *windows, d_out_t, stats],
-        34 * rows * rows * feat,
-        5 * rows * rows * feat // HEAD_DIM,
-    )
-
-
-def key_kernel(which, final, pos_ref, mask_ref, own_ref, *rest):
-    count = len(which)
-    sources = [rest[3 * n:3 * n + 3] for n in range(count)]
-    dk_in, dv_in, dk_ref, dv_ref = rest[3 * count:]
+        [
+            jax.ShapeDtypeStruct((rows, feat), jnp.bfloat16),
+            total,
+            total,
+            jax.ShapeDtypeStruct((heads * BLOCKS * rows, rows), jnp.float32),
+            jax.ShapeDtypeStruct((heads * rows, rows), jnp.float32),
+        ],
+        [pos, tile_mask, own, *windows, d_out_t, stats, run, kept, q_last, d_last],
+        36 * rows * rows * feat,
+        rows * rows * heads,
+    )
+
+
+def key_kernel(which, pos_ref, mask_ref, own_ref, *rest):
+    sources = [rest[3 * n:3 * n + 3] for n in range(BLOCKS)]
+    scores_ref, dprobs_ref, dk_in, dv_in, dk_out, dv_out, dk_ref, dv_ref, sems = rest[3 * BLOCKS:]
+    copies = []
     rows, feat = dk_in.shape
     biases = source_bias(mask_ref, pos_ref[0], rows // TILE, which)
     sums = [None, None]
 
     def products(head, n):
         cols = columns(head)
-        q_ref, d_ref, _ = sources[n]
-        return (
-            dot(own_ref[:rows, cols], q_ref[q_ref.shape[0] - rows:, cols], NT),
-            dot(own_ref[rows:2 * rows, cols], d_ref[cols, :], NN),
-        )
-
-    def finish(head, n, now):
+        if n == BLOCKS - 1:
+            return dprobs_ref[head * rows:(head + 1) * rows, :]
+        return dot(own_ref[rows:2 * rows, cols], sources[n][1][cols, :], NN)
+
+    def finish(head, n, dprobs):
         cols = columns(head)
         q_ref, d_ref, s_ref = sources[n]
         start = feat if s_ref.shape[0] > feat else 0
-        probs, dscores = block_grads(*now, biases[n], *statistics_of(s_ref, start, head))
+        scores = scores_ref[block_rows(n, head, rows), :]
+        probs, dscores = block_grads(
+            scores, dprobs, biases[n], *statistics_of(s_ref, start, head)
+        )
         before = (dk_in[:, cols], dv_in[:, cols]) if n == 0 else sums
         sums[:] = [
             before[0] + dot(dscores, q_ref[q_ref.shape[0] - rows:, cols], NN),
             before[1] + dot(probs, d_ref[cols, :], NT),
         ]
-        if n == count - 1:
+        if n == BLOCKS - 1:
             dk, dv = sums
-            dk_ref[:, cols] = (dk * SCALE if final else dk).astype(dk_ref.dtype)
+            dk_ref[:, cols] = (dk * SCALE).astype(dk_ref.dtype)
             dv_ref[:, cols] = dv.astype(dv_ref.dtype)
-
-    steps = [(head, n) for head in range(feat // HEAD_DIM) for n in range(count)]
+            for which_out, (from_ref, to_ref) in enumerate(((dk_ref, dk_out), (dv_ref, dv_out))):
+                copies.append(
+                    pltpu.make_async_copy(
+                        from_ref.at[:, cols], to_ref.at[:, cols], sems.at[2 * head + which_out]
+                    )
+                )
+                copies[-1].start()
+
+    steps = [(head, n) for head in range(feat // HEAD_DIM) for n in range(BLOCKS)]
     in_order(steps, products, finish)
-
-
-def key_side(pos, tile_mask, own, sources, begun, final):
+    for copy in copies:
+        copy.wait()
+
+
+def key_side(pos, tile_mask, own, sources, scores, dprobs, begun):
     rows, feat = begun[0].shape
     operands = [pos, tile_mask, own]
     for _, q, d, s in sources:
         operands += [q, d, s]
-    which = [source[0] for source in sources]
-    dtype = jnp.bfloat16 if final else jnp.float32
-    return kernel_call(
-        functools.partial(key_kernel, which, final),
-        [jax.ShapeDtypeStruct((rows, feat), dtype)] * 2,
-        operands + list(begun),
-        8 * len(which) * rows * rows * feat,
-        len(which) * rows * rows * feat // HEAD_DIM,
-    )
+    operands += [scores, dprobs, *begun]
+    return pl.pallas_call(
+        functools.partial(key_kernel, [source[0] for source in sources]),
+        in_specs=[SMEM if x.dtype == jnp.int32 else VMEM for x in operands],
+        out_specs=[ANY] * 2,
+        out_shape=[jax.ShapeDtypeStruct((rows, feat), jnp.bfloat16)] * 2,
+        scratch_shapes=[
+            pltpu.VMEM((rows, feat), jnp.bfloat16),
+            pltpu.VMEM((rows, feat), jnp.bfloat16),
+            pltpu.SemaphoreType.DMA((2 * feat // HEAD_DIM,)),
+        ],
+        compiler_params=pltpu.CompilerParams(vmem_limit_bytes=VMEM_LIMIT),
+        cost_estimate=pl.CostEstimate(
+            flops=26 * rows * rows * feat,
+            bytes_accessed=sum(x.size * x.dtype.itemsize for x in operands),
+            transcendentals=BLOCKS * rows * rows * feat // HEAD_DIM,
+        ),
+    )(*operands)
 
 
 def local(queries, keys, values, out_weight, reward_grad, tile_mask):
@@ -507,8 +551,8 @@
     second = second_step(kvq_x, kvq_a, kvq_b)
     kv_g = send(second[:2 * rows], forward)
     d_out_t = end_project(kept, far, far_near, after(begun, second))
-    out, run = forward_part(
-        pos, tile_mask, after(kvq, d_out_t), [0, 1, 2, 3], [kvq_x, kvq_a, kvq_b]
+    out, run, kept_weights = forward_part(
+        pos, tile_mask, after(kvq, d_out_t), [0, 2, 1, 3], [kvq_a, kvq_x, kvq_b]
     )
     stats, packed = statistics(pos, tile_mask, kvq, 4, kv_g, out, run, d_out_t)
     q_g = send(after(second[2 * rows:], out), forward)
@@ -517,22 +561,23 @@
     p_a = send(packed, even_chain)
     p_x = send(packed, in_pair)
     s_g = send(stats, across)
-    grad_queries, *begun_keys = query_side(
-        pos, tile_mask, kvq, [0, 1, 2, 3, 4], [kvq_x, kvq_a, kvq_b, kv_g], d_out_t,
-        after(stats, q_g, d_g),
+    grad_queries, *begun_keys, scores, dprobs = query_side(
+        pos, tile_mask, kvq, [0, 2, 1, 3, 4], [kvq_a, kvq_x, kvq_b, kv_g], d_out_t,
+        stats, run, kept_weights, q_g, d_g,
     )
     grad_keys, grad_values = key_side(
         pos,
         tile_mask,
         kvq,
         [
+            (2, kvq_a, p_a, p_a),
+            (1, kvq_x, p_x, p_x),
+            (3, kvq_b, p_b, p_b),
             (4, q_g, d_g, s_g),
-            (1, kvq_x, p_x, p_x),
-            (2, kvq_a, p_a, p_a),
-            (3, kvq_b, p_b, p_b),
-        ],
+        ],
+        scores,
+        dprobs,
         begun_keys,
-        True,
     )
     return (grad_queries, grad_keys, grad_values)
 

time: 65 us -> 64.3 us (0.989)
  waiting for transfers between devices: 15.6 us -> 13.7 us
  starting transfers between devices: 23 us -> 24.9 us
  Pallas kernels: 20.8 us -> 20 us
    pallas_call x5 -> x4, Pallas kernels: 15.4 us -> 11 us  [kernel_call(): pl.pallas_call(kernel, in_specs=[SMEM if x.dtype == jnp.int32 else VMEM f...]
    pallas_call x0 -> x1, Pallas kernels: none -> 3.71 us  [key_side(): pl.pallas_call(functools.partial(key_kernel, [source[0] for source in sou...]
    ppermute x13, waiting for transfers between devices: 15.6 us -> 13.7 us  [send(): return lax.ppermute(array, BOTH, pairs)]
    ppermute x13, starting transfers between devices: 23 us -> 24.9 us  [send(): return lax.ppermute(array, BOTH, pairs)]
  transfers between devices with their start and end apart: 13 -> 13, of which waited for: 7 -> 5; matrix products, arithmetic and copies ran while one was open for 0% -> 0% of each run, Pallas kernels for 22% -> 22%
where the time goes in v5:
time: 64.3 us; the launch traced here: 63.7 us
  starting transfers between devices  24.9 us (39%)
  Pallas kernels  20 us (31%)
  waiting for transfers between devices  13.7 us (21%)
  local copies, waits for them, and re-layouts  4.04 us (6%)
  between operations  0.82 us (1%)
    ppermute x13, starting transfers between devices, send(): return lax.ppermute(array, BOTH, pairs)  24.9 us
    ppermute x13, waiting for transfers between devices, send(): return lax.ppermute(array, BOTH, pairs)  13.7 us
    pallas_call x4, Pallas kernels, kernel_call(): pl.pallas_call(kernel, in_specs=[SMEM if x.dtype == jnp.int32 else VMEM f...  11 us
    unnamed x8, local copies, waits for them, and re-layouts  3.95 us
    pallas_call x1, Pallas kernels, key_side(): pl.pallas_call(functools.partial(key_kernel, [source[0] for source in sou...  3.71 us
    pallas_call x1, Pallas kernels, begin_project(): pl.pallas_call(begin_kernel, in_specs=[SMEM, ANY, VMEM, VMEM], out_specs=...  3.2 us
    pallas_call x1, Pallas kernels, pack(): pl.pallas_call(pack_kernel, in_specs=[ANY] * count, out_specs=VMEM, out_s...  2.16 us
  transfers between devices with their start and end apart: 13, of which 5 were waited for; matrix products, arithmetic and copies ran while one was open for 0% of the time, Pallas kernels for 22%

profile of v5, /device:TPU:8, one launch (start us, length us, event | category | flops | bytes accessed | tf_op | source)
XLA Modules:
  0.0 63.7 jit_solution(10470177948638697103)
XLA Ops:
  0.6 2.2 %shard_map.85.rest_0_.own_ref = bf16[768,640]{1,0:T(8,128)(2,1)} custom-call(bf16[256,640]{1,0:T(8,128)(2,1)} %refs_0_.1, bf16[256,640]{1,0:T(8,128)(2,1)} %refs_1_.1, bf16[256,640]{1,0:T(8,128)(2,1)} %refs_2_.1), custom_call_target="tpu_custom_call" | custom-call | bytes 1966080 | tf_op jit(solution)/shard_map/pallas_call | solution.py:109
  2.9 1.9 %collective-permute-start.1 = (bf16[768,640]{1,0:T(8,128)(2,1)}, bf16[768,640]{1,0:T(8,128)(2,1)S(1)}, u32[]{:S(2)}, u32[]{:S(2)}) collective-permute-start(bf16[768,640]{1,0:T(8,128)(2,1)} %shard_map.85.rest_0_.own_ref), channel_id=1, source_target_pairs={{0,4},{1,5},{2,6},{3,7},{4,0},{5,1},{6,2},{7,3},{8,12},{9,13},{10,... | collective-permute-start | bytes 2949128 | tf_op jit(solution)/shard_map/ppermute | solution.py:58
  4.8 4.6 %collective-permute-start.2 = (bf16[768,640]{1,0:T(8,128)(2,1)}, bf16[768,640]{1,0:T(8,128)(2,1)S(1)}, u32[]{:S(2)}, u32[]{:S(2)}) collective-permute-start(bf16[768,640]{1,0:T(8,128)(2,1)} %shard_map.85.rest_0_.own_ref), channel_id=1, source_target_pairs={{8,16},{9,17},{10,18},{11,19},{12,20},{13,21},{14,22},{15,23},{16,... | collective-permute-start | bytes 2949128 | tf_op jit(solution)/shard_map/ppermute | solution.py:58
  9.5 1.6 %collective-permute-start.5 = (bf16[256,1280]{1,0:T(8,128)(2,1)}, bf16[256,1280]{1,0:T(8,128)(2,1)}, u32[]{:S(2)}, u32[]{:S(2)}) collective-permute-start(bf16[256,1280]{1,0:T(8,128)(2,1)} %g_a.1), channel_id=1, source_target_pairs={{0,2},{1,3},{2,0},{3,1},{4,6},{5,7},{6,4},{7,5},{8,10},{9,11},{10,... | collective-permute-start | bytes 1966088 | tf_op jit(solution)/shard_map/ppermute | solution.py:58
  11.2 0.8 %collective-permute-done.4.g_b = bf16[256,1280]{1,0:T(8,128)(2,1)} collective-permute-done((bf16[256,1280]{1,0:T(8,128)(2,1)}, bf16[256,1280]{1,0:T(8,128)(2,1)}, u32[]{:S(2)}, u32[]{:S(2)}) %collective-permute-start.4) | collective-permute-done | bytes 655392 | tf_op jit(solution)/shard_map/ppermute | solution.py:58
  11.9 2.9 %copy-done.1 = bf16[640,5120]{1,0:T(8,128)(2,1)S(1)} copy-done((bf16[640,5120]{1,0:T(8,128)(2,1)S(1)}, bf16[640,5120]{1,0:T(8,128)(2,1)}, u32[]{:S(2)}) %copy-start.1) | copy-done | bytes 6553624
  14.8 1.1 %copy-done.2 = bf16[256,1280]{1,0:T(8,128)(2,1)S(1)} copy-done((bf16[256,1280]{1,0:T(8,128)(2,1)S(1)}, bf16[256,1280]{1,0:T(8,128)(2,1)}, u32[]{:S(2)}) %copy-start.2) | copy-done | bytes 655384
  15.9 3.2 %shard_map.86 = (f32[640,256]{1,0:T(8,128)S(1)}, bf16[640,2560]{1,0:T(8,128)(2,1)S(1)}) custom-call(s32[4]{0:T(128)S(1)} %pad_add_fusion.order_ref, bf16[640,5120]{1,0:T(8,128)(2,1)S(1)} %copy-done.1, bf16[256,1280]{1,0:T(8,128)(2,1)S(1)} %copy-done.2, bf16[256,1280]{1,0:T(8,128)(2,1)} %collective-permute-done.4.g_b), custom_call_target="tpu_custom_call" | custom-call | flops 838860800 | bytes 6553600 | tf_op jit(solution)/shard_map/pallas_call | solution.py:141
  19.1 7.9 %collective-permute-done.5.g_a = bf16[256,1280]{1,0:T(8,128)(2,1)} collective-permute-done((bf16[256,1280]{1,0:T(8,128)(2,1)}, bf16[256,1280]{1,0:T(8,128)(2,1)}, u32[]{:S(2)}, u32[]{:S(2)}) %collective-permute-start.5) | collective-permute-done | bytes 655392 | tf_op jit(solution)/shard_map/ppermute | solution.py:58
  27.0 3.8 %collective-permute-done.2.rest_3_.rest_2_.rest_6_ = bf16[768,640]{1,0:T(8,128)(2,1)S(1)} collective-permute-done((bf16[768,640]{1,0:T(8,128)(2,1)}, bf16[768,640]{1,0:T(8,128)(2,1)S(1)}, u32[]{:S(2)}, u32[]{:S(2)}) %collective-permute-start.2) | collective-permute-done | bytes 983072 | tf_op jit(solution)/shard_map/ppermute | solution.py:58
  30.8 0.1 select_select_fusion
  31.0 3.6 %collective-permute-start.3 = (bf16[512,640]{1,0:T(8,128)(2,1)S(1)}, bf16[512,640]{1,0:T(8,128)(2,1)S(1)}, u32[]{:S(2)}, u32[]{:S(2)}) collective-permute-start(bf16[512,640]{1,0:T(8,128)(2,1)S(1)} %slice.8), channel_id=1, source_target_pairs={{0,8},{1,5},{2,10},{3,7},{5,1},{7,3},{8,16},{9,13},{10,18},{11,15}... | collective-permute-start | bytes 1966088 | tf_op jit(solution)/shard_map/ppermute | solution.py:58
  34.7 2.1 %shard_map.87.d_ref.rest_4_ = bf16[640,256]{1,0:T(8,128)(2,1)S(1)} custom-call(bf16[640,2560]{1,0:T(8,128)(2,1)S(1)} %get-tuple-element.23.w_ref, bf16[256,1280]{1,0:T(8,128)(2,1)} %collective-permute-done.5.g_a, bf16[256,1280]{1,0:T(8,128)(2,1)S(1)} %collective-permute-done.6.g_b, f32[640,256]{1,0:T(8,128)S(1)} %get-tuple-element.26.begun), custom_call_target="tpu_custom_call" | custom-call | flops 838860800 | bytes 5242880 | tf_op jit(solution)/shard_map/pallas_call | solution.py:38
  36.9 2.6 %shard_map.88 = (f32[640,256]{1,0:T(8,128)S(1)}, f32[80,256]{1,0:T(8,128)S(1)}, f32[5120,256]{1,0:T(8,128)S(1)}) custom-call(s32[1]{0:T(128)} %bitcast.pos_ref, s32[16,10]{1,0:T(8,128)S(1)} %copy-done.3, bf16[768,640]{1,0:T(8,128)(2,1)S(1)} %copy-done, bf16[768,640]{1,0:T(8,128)(2,1)S(1)} %collective-permute-done.rest_1_.rest_0_, ...), custom_call_target="tpu_custom_call" | custom-call | flops 671088640 | bytes 3932804 | tf_op jit(solution)/shard_map/pallas_call | solution.py:38
  39.5 1.9 %collective-permute-start.7 = (bf16[256,640]{1,0:T(8,128)(2,1)S(1)}, bf16[256,640]{1,0:T(8,128)(2,1)S(1)}, u32[]{:S(2)}, u32[]{:S(2)}) collective-permute-start(bf16[256,640]{1,0:T(8,128)(2,1)S(1)} %slice.9), channel_id=1, source_target_pairs={{0,8},{1,5},{2,10},{3,7},{5,1},{7,3},{8,16},{9,13},{10,18},{11,15}... | collective-permute-start | bytes 983048 | tf_op jit(solution)/shard_map/ppermute | solution.py:58
  41.4 1.9 %collective-permute-start.8 = (bf16[640,256]{1,0:T(8,128)(2,1)S(1)}, bf16[640,256]{1,0:T(8,128)(2,1)S(1)}, u32[]{:S(2)}, u32[]{:S(2)}) collective-permute-start(bf16[640,256]{1,0:T(8,128)(2,1)S(1)} %shard_map.87.d_ref.rest_4_), channel_id=1, source_target_pairs={{4,8},{5,9},{6,10},{7,11},{8,4},{9,5},{10,6},{11,7},{12,16},{13,17... | collective-permute-start | bytes 983048 | tf_op jit(solution)/shard_map/ppermute | solution.py:58
  43.4 0.1 collective-permute-done.3.w_ref.rest_3_
  43.5 1.6 %shard_map.89 = (bf16[32,256]{1,0:T(8,128)(2,1)S(1)}, bf16[672,256]{1,0:T(8,128)(2,1)S(1)}) custom-call(s32[1]{0:T(128)} %bitcast.pos_ref, s32[16,10]{1,0:T(8,128)S(1)} %copy-done.3, bf16[768,640]{1,0:T(8,128)(2,1)S(1)} %copy-done, bf16[512,640]{1,0:T(8,128)(2,1)S(1)} %collective-permute-done.3.w_ref.rest_3_, f32[640,256]{1,0:T(8,128)S(1)} %get-tuple-element.28.out_in, ...), custom_call_target="tpu_custom_call" | custom-call | flops 167772160 | bytes 2704004 | tf_op jit(solution)/shard_map/pallas_call | solution.py:38
  45.1 1.4 %collective-permute-start.10 = (bf16[672,256]{1,0:T(8,128)(2,1)S(1)}, bf16[672,256]{1,0:T(8,128)(2,1)S(1)}, u32[]{:S(2)}, u32[]{:S(2)}) collective-permute-start(bf16[672,256]{1,0:T(8,128)(2,1)S(1)} %get-tuple-element.34), channel_id=1, source_target_pairs={{0,4},{1,5},{2,6},{3,7},{4,0},{5,1},{6,2},{7,3},{8,12},{9,13},{10,... | collective-permute-start | bytes 1032200 | tf_op jit(solution)/shard_map/ppermute | solution.py:58
  46.5 2.8 %collective-permute-start.11 = (bf16[672,256]{1,0:T(8,128)(2,1)S(1)}, bf16[672,256]{1,0:T(8,128)(2,1)S(1)}, u32[]{:S(2)}, u32[]{:S(2)}) collective-permute-start(bf16[672,256]{1,0:T(8,128)(2,1)S(1)} %get-tuple-element.34), channel_id=1, source_target_pairs={{8,16},{9,17},{10,18},{11,19},{12,20},{13,21},{14,22},{15,23},{16,... | collective-permute-start | bytes 1032200 | tf_op jit(solution)/shard_map/ppermute | solution.py:58
  49.4 4.8 %collective-permute-start.12 = (bf16[32,256]{1,0:T(8,128)(2,1)S(1)}, bf16[32,256]{1,0:T(8,128)(2,1)S(1)}, u32[]{:S(2)}, u32[]{:S(2)}) collective-permute-start(bf16[32,256]{1,0:T(8,128)(2,1)S(1)} %get-tuple-element.30.rest_5_), channel_id=1, source_target_pairs={{4,8},{5,9},{6,10},{7,11},{8,4},{9,5},{10,6},{11,7},{12,16},{13,17... | collective-permute-start | bytes 49160 | tf_op jit(solution)/shard_map/ppermute | solution.py:58
  54.2 4.6 %shard_map.90 = (bf16[256,640]{1,0:T(8,128)(2,1)}, f32[256,640]{1,0:T(8,128)S(1)}, f32[256,640]{1,0:T(8,128)S(1)}, f32[5120,256]{1,0:T(8,128)S(1)}, f32[1280,256]{1,0:T(8,128)S(1)}) custom-call(s32[1]{0:T(128)} %bitcast.pos_ref, s32[16,10]{1,0:T(8,128)S(1)} %copy-done.3, bf16[768,640]{1,0:T(8,128)(2,1)S(1)} %copy-done, ...), custom_call_target="tpu_custom_call" | custom-call | flops 1509949440 | bytes 10912388 | tf_op jit(solution)/shard_map/pallas_call | solution.py:38
  58.9 1.1 %collective-permute-done.12.rest_11_ = bf16[32,256]{1,0:T(8,128)(2,1)S(1)} collective-permute-done((bf16[32,256]{1,0:T(8,128)(2,1)S(1)}, bf16[32,256]{1,0:T(8,128)(2,1)S(1)}, u32[]{:S(2)}, u32[]{:S(2)}) %collective-permute-start.12) | collective-permute-done | bytes 16416 | tf_op jit(solution)/shard_map/ppermute | solution.py:58
  60.0 3.7 %shard_map.91 = (bf16[256,640]{1,0:T(8,128)(2,1)}, bf16[256,640]{1,0:T(8,128)(2,1)}) custom-call(s32[1]{0:T(128)} %bitcast.pos_ref, s32[16,10]{1,0:T(8,128)S(1)} %copy-done.3, bf16[768,640]{1,0:T(8,128)(2,1)S(1)} %copy-done, bf16[768,640]{1,0:T(8,128)(2,1)S(1)} %collective-permute-done.rest_1_.rest_0_, ...), custom_call_target="tpu_custom_call" | custom-call | flops 1090519040 | bytes 14533252 | tf_op jit(solution)/shard_map/pallas_call | solution.py:512
  (21 shorter events, 0.4 us)
Async XLA Ops:
  2.8 24.2 %collective-permute-start = (bf16[768,640]{1,0:T(8,128)(2,1)}, bf16[768,640]{1,0:T(8,128)(2,1)S(1)}, u32[]{:S(2)}, u32[]{:S(2)}) collective-permute-start(bf16[768,640]{1,0:T(8,128)(2,1)} %shard_map.85.rest_0_.own_ref), channel_id=1, source_target_pairs={{0,8},{1,9},{2,10},{3,11},{4,12},{5,13},{6,14},{7,15},{8,0},{9,1},... | collective-permute-start | bytes 2949128 | tf_op jit(solution)/shard_map/ppermute | solution.py:58
  2.9 24.1 %collective-permute-start.1 = (bf16[768,640]{1,0:T(8,128)(2,1)}, bf16[768,640]{1,0:T(8,128)(2,1)S(1)}, u32[]{:S(2)}, u32[]{:S(2)}) collective-permute-start(bf16[768,640]{1,0:T(8,128)(2,1)} %shard_map.85.rest_0_.own_ref), channel_id=1, source_target_pairs={{0,4},{1,5},{2,6},{3,7},{4,0},{5,1},{6,2},{7,3},{8,12},{9,13},{10,... | collective-permute-start | bytes 2949128 | tf_op jit(solution)/shard_map/ppermute | solution.py:58
  4.8 26.0 %collective-permute-start.2 = (bf16[768,640]{1,0:T(8,128)(2,1)}, bf16[768,640]{1,0:T(8,128)(2,1)S(1)}, u32[]{:S(2)}, u32[]{:S(2)}) collective-permute-start(bf16[768,640]{1,0:T(8,128)(2,1)} %shard_map.85.rest_0_.own_ref), channel_id=1, source_target_pairs={{8,16},{9,17},{10,18},{11,19},{12,20},{13,21},{14,22},{15,23},{16,... | collective-permute-start | bytes 2949128 | tf_op jit(solution)/shard_map/ppermute | solution.py:58
  9.4 2.5 %collective-permute-start.4 = (bf16[256,1280]{1,0:T(8,128)(2,1)}, bf16[256,1280]{1,0:T(8,128)(2,1)}, u32[]{:S(2)}, u32[]{:S(2)}) collective-permute-start(bf16[256,1280]{1,0:T(8,128)(2,1)} %g_a.1), channel_id=1, source_target_pairs={{0,1},{1,0},{2,3},{3,2},{4,5},{5,4},{6,7},{7,6},{8,9},{9,8},{10,11... | collective-permute-start | bytes 1966088 | tf_op jit(solution)/shard_map/ppermute | solution.py:58
  9.5 17.5 %collective-permute-start.5 = (bf16[256,1280]{1,0:T(8,128)(2,1)}, bf16[256,1280]{1,0:T(8,128)(2,1)}, u32[]{:S(2)}, u32[]{:S(2)}) collective-permute-start(bf16[256,1280]{1,0:T(8,128)(2,1)} %g_a.1), channel_id=1, source_target_pairs={{0,2},{1,3},{2,0},{3,1},{4,6},{5,7},{6,4},{7,5},{8,10},{9,11},{10,... | collective-permute-start | bytes 1966088 | tf_op jit(solution)/shard_map/ppermute | solution.py:58
  11.9 2.9 %copy-start.1 = (bf16[640,5120]{1,0:T(8,128)(2,1)S(1)}, bf16[640,5120]{1,0:T(8,128)(2,1)}, u32[]{:S(2)}) copy-start(bf16[640,5120]{1,0:T(8,128)(2,1)} %w_ref.1) | copy-start | bytes 19660804
  14.8 1.1 %copy-start.2 = (bf16[256,1280]{1,0:T(8,128)(2,1)S(1)}, bf16[256,1280]{1,0:T(8,128)(2,1)}, u32[]{:S(2)}) copy-start(bf16[256,1280]{1,0:T(8,128)(2,1)} %g_a.1) | copy-start | bytes 1966084
  27.0 9.9 %copy-start = (bf16[768,640]{1,0:T(8,128)(2,1)S(1)}, bf16[768,640]{1,0:T(8,128)(2,1)}, u32[]{:S(2)}) copy-start(bf16[768,640]{1,0:T(8,128)(2,1)} %shard_map.85.rest_0_.own_ref) | copy-start | bytes 2949124
  27.0 9.9 %copy-start.3 = (s32[16,10]{1,0:T(8,128)S(1)}, s32[16,10]{1,0:T(8,128)}, u32[]{:S(2)}) copy-start(s32[16,10]{1,0:T(8,128)} %mask_ref.7) | copy-start | bytes 1924
  27.0 7.7 %collective-permute-start.6 = (bf16[256,1280]{1,0:T(8,128)(2,1)}, bf16[256,1280]{1,0:T(8,128)(2,1)S(1)}, u32[]{:S(2)}, u32[]{:S(2)}) collective-permute-start(bf16[256,1280]{1,0:T(8,128)(2,1)} %collective-permute-done.5.g_a), channel_id=1, source_target_pairs={{0,1},{1,0},{2,3},{3,2},{4,5},{5,4},{6,7},{7,6},{8,9},{9,8},{10,11... | collective-permute-start | bytes 1966088 | tf_op jit(solution)/shard_map/ppermute | solution.py:58
  31.0 12.5 %collective-permute-start.3 = (bf16[512,640]{1,0:T(8,128)(2,1)S(1)}, bf16[512,640]{1,0:T(8,128)(2,1)S(1)}, u32[]{:S(2)}, u32[]{:S(2)}) collective-permute-start(bf16[512,640]{1,0:T(8,128)(2,1)S(1)} %slice.8), channel_id=1, source_target_pairs={{0,8},{1,5},{2,10},{3,7},{5,1},{7,3},{8,16},{9,13},{10,18},{11,15}... | collective-permute-start | bytes 1966088 | tf_op jit(solution)/shard_map/ppermute | solution.py:58
  39.5 9.9 %collective-permute-start.7 = (bf16[256,640]{1,0:T(8,128)(2,1)S(1)}, bf16[256,640]{1,0:T(8,128)(2,1)S(1)}, u32[]{:S(2)}, u32[]{:S(2)}) collective-permute-start(bf16[256,640]{1,0:T(8,128)(2,1)S(1)} %slice.9), channel_id=1, source_target_pairs={{0,8},{1,5},{2,10},{3,7},{5,1},{7,3},{8,16},{9,13},{10,18},{11,15}... | collective-permute-start | bytes 983048 | tf_op jit(solution)/shard_map/ppermute | solution.py:58
  41.4 12.8 %collective-permute-start.8 = (bf16[640,256]{1,0:T(8,128)(2,1)S(1)}, bf16[640,256]{1,0:T(8,128)(2,1)S(1)}, u32[]{:S(2)}, u32[]{:S(2)}) collective-permute-start(bf16[640,256]{1,0:T(8,128)(2,1)S(1)} %shard_map.87.d_ref.rest_4_), channel_id=1, source_target_pairs={{4,8},{5,9},{6,10},{7,11},{8,4},{9,5},{10,6},{11,7},{12,16},{13,17... | collective-permute-start | bytes 983048 | tf_op jit(solution)/shard_map/ppermute | solution.py:58
  45.1 14.9 %collective-permute-start.10 = (bf16[672,256]{1,0:T(8,128)(2,1)S(1)}, bf16[672,256]{1,0:T(8,128)(2,1)S(1)}, u32[]{:S(2)}, u32[]{:S(2)}) collective-permute-start(bf16[672,256]{1,0:T(8,128)(2,1)S(1)} %get-tuple-element.34), channel_id=1, source_target_pairs={{0,4},{1,5},{2,6},{3,7},{4,0},{5,1},{6,2},{7,3},{8,12},{9,13},{10,... | collective-permute-start | bytes 1032200 | tf_op jit(solution)/shard_map/ppermute | solution.py:58
  46.5 13.5 %collective-permute-start.11 = (bf16[672,256]{1,0:T(8,128)(2,1)S(1)}, bf16[672,256]{1,0:T(8,128)(2,1)S(1)}, u32[]{:S(2)}, u32[]{:S(2)}) collective-permute-start(bf16[672,256]{1,0:T(8,128)(2,1)S(1)} %get-tuple-element.34), channel_id=1, source_target_pairs={{8,16},{9,17},{10,18},{11,19},{12,20},{13,21},{14,22},{15,23},{16,... | collective-permute-start | bytes 1032200 | tf_op jit(solution)/shard_map/ppermute | solution.py:58
  49.3 10.7 %collective-permute-start.9 = (bf16[672,256]{1,0:T(8,128)(2,1)S(1)}, bf16[672,256]{1,0:T(8,128)(2,1)S(1)}, u32[]{:S(2)}, u32[]{:S(2)}) collective-permute-start(bf16[672,256]{1,0:T(8,128)(2,1)S(1)} %get-tuple-element.34), channel_id=1, source_target_pairs={{0,8},{1,9},{2,10},{3,11},{4,12},{5,13},{6,14},{7,15},{8,0},{9,1},... | collective-permute-start | bytes 1032200 | tf_op jit(solution)/shard_map/ppermute | solution.py:58
  49.4 10.6 %collective-permute-start.12 = (bf16[32,256]{1,0:T(8,128)(2,1)S(1)}, bf16[32,256]{1,0:T(8,128)(2,1)S(1)}, u32[]{:S(2)}, u32[]{:S(2)}) collective-permute-start(bf16[32,256]{1,0:T(8,128)(2,1)S(1)} %get-tuple-element.30.rest_5_), channel_id=1, source_target_pairs={{4,8},{5,9},{6,10},{7,11},{8,4},{9,5},{10,6},{11,7},{12,16},{13,17... | collective-permute-start | bytes 49160 | tf_op jit(solution)/shard_map/ppermute | solution.py:58

commit v6 on v5

--- a/solution.py
+++ b/solution.py
@@ -195,37 +195,38 @@
     return jnp.concatenate(parts, axis=1)
 
 
-def window_bias(mask_ref, pos, tiles, which):
-    offs = (0,) + offsets(pos)
-    return [
-        [
-            bias_row(
-                [
-                    mask_ref[pos * tiles + a, (offs[n] + SPAN) * tiles + b] > 0
-                    for a in range(tiles)
-                ]
+def bias_kernel(pos_ref, mask_ref, window_ref, source_ref):
+    pos = pos_ref[0]
+    rows = window_ref.shape[1]
+    tiles = rows // TILE
+    total_tiles = mask_ref.shape[0]
+    window_ref[...] = jnp.zeros_like(window_ref)
+    source_ref[...] = jnp.zeros_like(source_ref)
+    for n, off in enumerate((0,) + offsets(pos)):
+        for b in range(tiles):
+            at = slice(n * tiles + b, n * tiles + b + 1)
+            column = (off + SPAN) * tiles + b
+            window_ref[at, :] = bias_row(
+                [mask_ref[pos * tiles + a, column] > 0 for a in range(tiles)]
             )
-            for b in range(tiles)
-        ]
-        for n in which
-    ]
-
-
-def source_bias(mask_ref, pos, tiles, which):
-    total_tiles = mask_ref.shape[0]
-    offs = (0,) + offsets(pos)
-    rows = []
-    for n in which:
-        rows.append([])
-        for b in range(tiles):
             flags = []
             for a in range(tiles):
-                tile = (pos + offs[n]) * tiles + a
+                tile = (pos + off) * tiles + a
                 inside = (tile >= 0) & (tile < total_tiles)
-                column = (SPAN - offs[n]) * tiles + b
+                column = (SPAN - off) * tiles + b
                 flags.append(inside & (mask_ref[jnp.clip(tile, 0, total_tiles - 1), column] > 0))
-            rows[-1].append(bias_row(flags))
-    return rows
+            source_ref[at, :] = bias_row(flags)
+
+
+def biases_of(pos, tile_mask, rows):
+    count = -(-(2 * SPAN + 1) * (rows // TILE) // 8) * 8
+    shape = jax.ShapeDtypeStruct((count, rows), jnp.float32)
+    return kernel_call(bias_kernel, [shape, shape], [pos, tile_mask], 0)
+
+
+def bias_rows(ref, which):
+    tiles = ref.shape[1] // TILE
+    return [[ref[n * tiles + b:n * tiles + b + 1, :] for b in range(tiles)] for n in which]
 
 
 def over_keys(reduce, values):
@@ -246,7 +247,8 @@
 
 
 def weighted_values(shifted, top, values_of, keep=None):
-    totals = out = None
+    totals = None
+    blocks = []
     for n, parts in enumerate(shifted):
         weights = []
         for value in parts:
@@ -257,8 +259,9 @@
         weights = jnp.concatenate(weights, axis=0)
         if keep is not None:
             keep(n, weights)
-        part = dot(values_of(n), weights.astype(jnp.bfloat16), TN)
-        out = part if out is None else out + part
+        blocks.append(weights.astype(jnp.bfloat16))
+    values = jnp.concatenate([values_of(n) for n in range(len(blocks))], axis=0)
+    out = dot(values, jnp.concatenate(blocks, axis=0), TN)
     return jnp.sum(totals, axis=0, keepdims=True), out
 
 
@@ -271,11 +274,10 @@
         finish(*step, now)
 
 
-def forward_kernel(which, pos_ref, mask_ref, *rest):
+def forward_kernel(which, bias_ref, *rest):
     windows, (out_ref, run_ref, kept_ref) = rest[:len(which)], rest[len(which):]
-    pos = pos_ref[0]
     feat, rows = out_ref.shape
-    biases = window_bias(mask_ref, pos, rows // TILE, which)
+    biases = bias_rows(bias_ref, which)
 
     def scores_of(head):
         cols = columns(head)
@@ -301,7 +303,7 @@
     in_order([(head,) for head in range(feat // HEAD_DIM)], scores_of, finish)
 
 
-def forward_part(pos, tile_mask, own, which, windows):
+def forward_part(bias, own, which, windows):
     rows, feat = own.shape[0] // 3, own.shape[1]
     heads = feat // HEAD_DIM
     return kernel_call(
@@ -311,18 +313,17 @@
             jax.ShapeDtypeStruct((heads * RUN_ROWS, rows), jnp.float32),
             jax.ShapeDtypeStruct((len(which) * feat // HEAD_DIM * rows, rows), jnp.float32),
         ],
-        [pos, tile_mask, own, *windows],
+        [bias, own, *windows],
         4 * len(which) * rows * rows * feat,
         len(which) * rows * rows * heads,
     )
 
 
 def statistics_kernel(
-    which, pos_ref, mask_ref, own_ref, w_ref, out_in, run_in, d_ref, stats_ref, packed_ref
+    which, bias_ref, own_ref, w_ref, out_in, run_in, d_ref, stats_ref, packed_ref
 ):
-    pos = pos_ref[0]
     feat, rows = d_ref.shape
-    biases = window_bias(mask_ref, pos, rows // TILE, [which])
+    biases = bias_rows(bias_ref, [which])
 
     def scores_of(head):
         cols = columns(head)
@@ -360,7 +361,7 @@
     packed_ref[feat:, :] = all_stats[0].astype(jnp.bfloat16)
 
 
-def statistics(pos, tile_mask, own, which, window, out, run, d_out_t):
+def statistics(bias, own, which, window, out, run, d_out_t):
     feat, rows = d_out_t.shape
     heads = feat // HEAD_DIM
     return kernel_call(
@@ -369,7 +370,7 @@
             jax.ShapeDtypeStruct((stat_rows(heads), rows), jnp.bfloat16),
             jax.ShapeDtypeStruct((feat + stat_rows(heads), rows), jnp.bfloat16),
         ],
-        [pos, tile_mask, own, window, out, run, d_out_t],
+        [bias, own, window, out, run, d_out_t],
         4 * rows * rows * feat,
         rows * rows * heads,
     )
@@ -393,53 +394,46 @@
     return probs.astype(jnp.bfloat16), dscores.astype(jnp.bfloat16)
 
 
-def query_kernel(which, pos_ref, mask_ref, own_ref, *rest):
+def query_kernel(which, bias_ref, own_ref, *rest):
     windows, rest = (own_ref,) + rest[:BLOCKS], rest[BLOCKS:]
     d_ref, s_ref, run_ref, kept_ref, q_last, d_last, *outs = rest
     dq_ref, dk_ref, dv_ref, scores_ref, dprobs_ref = outs
     rows, feat = dq_ref.shape
-    last_bias = window_bias(mask_ref, pos_ref[0], rows // TILE, which[BLOCKS:])[0]
-    sums = [None]
-
-    def products(head, n):
+    last_bias = bias_rows(bias_ref, which[BLOCKS:])[0]
+
+    def products(head):
         cols = columns(head)
         keys, values = own_ref[:rows, cols], own_ref[rows:2 * rows, cols]
         queries = own_ref[2 * rows:, cols]
-        if n < BLOCKS:
+        for n in range(BLOCKS):
             others = q_last[:, cols] if n == BLOCKS - 1 else windows[n + 1][2 * rows:, cols]
             scores_ref[block_rows(n, head, rows), :] = dot(keys, others, NT)
-            scores = None
-        else:
-            dprobs_ref[head * rows:(head + 1) * rows, :] = dot(values, d_last[cols, :], NN)
-            scores = dot(windows[n][:rows, cols], queries, NT)
-        return scores, dot(windows[n][rows:2 * rows, cols], d_ref[cols, :], NN)
-
-    def finish(head, n, now):
+        dprobs_ref[head * rows:(head + 1) * rows, :] = dot(values, d_last[cols, :], NN)
+        scores = dot(windows[BLOCKS][:rows, cols], queries, NT)
+        return scores, [dot(w[rows:2 * rows, cols], d_ref[cols, :], NN) for w in windows]
+
+    def finish(head, now):
         cols = columns(head)
         scores, dprobs = now
         lse, delta = statistics_of(s_ref, 0, head)
-        if n < BLOCKS:
-            at = head * RUN_ROWS
-            factor = jnp.exp2(run_ref[at:at + 1, :] - lse)
+        at = head * RUN_ROWS
+        factor = jnp.exp2(run_ref[at:at + 1, :] - lse)
+        dscores = []
+        for n in range(BLOCKS):
             probs = kept_ref[block_rows(n, head, rows), :] * factor
-            dscores = (probs * (dprobs - delta)).astype(jnp.bfloat16)
-        else:
-            _, dscores = block_grads(scores, dprobs, last_bias, lse, delta)
-        part = dot(windows[n][:rows, cols], dscores, TN)
-        if n == 0:
-            sums[0] = part
-            dk_ref[:, cols] = dot(dscores, own_ref[2 * rows:, cols], NN)
-            dv_ref[:, cols] = dot(probs.astype(jnp.bfloat16), d_ref[cols, :], NT)
-        else:
-            sums[0] = sums[0] + part
-        if n == BLOCKS:
-            dq_ref[:, cols] = jnp.transpose(sums[0] * SCALE).astype(dq_ref.dtype)
-
-    steps = [(head, n) for head in range(feat // HEAD_DIM) for n in range(BLOCKS + 1)]
-    in_order(steps, products, finish)
-
-
-def query_side(pos, tile_mask, own, which, windows, d_out_t, stats, run, kept, q_last, d_last):
+            dscores.append((probs * (dprobs[n] - delta)).astype(jnp.bfloat16))
+            if n == 0:
+                dv_ref[:, cols] = dot(probs.astype(jnp.bfloat16), d_ref[cols, :], NT)
+        dk_ref[:, cols] = dot(dscores[0], own_ref[2 * rows:, cols], NN)
+        dscores.append(block_grads(scores, dprobs[BLOCKS], last_bias, lse, delta)[1])
+        keys = jnp.concatenate([w[:rows, cols] for w in windows], axis=0)
+        dq = dot(keys, jnp.concatenate(dscores, axis=0), TN)
+        dq_ref[:, cols] = jnp.transpose(dq * SCALE).astype(dq_ref.dtype)
+
+    in_order([(head,) for head in range(feat // HEAD_DIM)], products, finish)
+
+
+def query_side(bias, own, which, windows, d_out_t, stats, run, kept, q_last, d_last):
     feat, rows = d_out_t.shape
     heads = feat // HEAD_DIM
     total = jax.ShapeDtypeStruct((rows, feat), jnp.float32)
@@ -452,66 +446,63 @@
             jax.ShapeDtypeStruct((heads * BLOCKS * rows, rows), jnp.float32),
             jax.ShapeDtypeStruct((heads * rows, rows), jnp.float32),
         ],
-        [pos, tile_mask, own, *windows, d_out_t, stats, run, kept, q_last, d_last],
+        [bias, own, *windows, d_out_t, stats, run, kept, q_last, d_last],
         36 * rows * rows * feat,
         rows * rows * heads,
     )
 
 
-def key_kernel(which, pos_ref, mask_ref, own_ref, *rest):
+def key_kernel(which, bias_ref, own_ref, *rest):
     sources = [rest[3 * n:3 * n + 3] for n in range(BLOCKS)]
     scores_ref, dprobs_ref, dk_in, dv_in, dk_out, dv_out, dk_ref, dv_ref, sems = rest[3 * BLOCKS:]
     copies = []
     rows, feat = dk_in.shape
-    biases = source_bias(mask_ref, pos_ref[0], rows // TILE, which)
-    sums = [None, None]
-
-    def products(head, n):
-        cols = columns(head)
-        if n == BLOCKS - 1:
-            return dprobs_ref[head * rows:(head + 1) * rows, :]
-        return dot(own_ref[rows:2 * rows, cols], sources[n][1][cols, :], NN)
-
-    def finish(head, n, dprobs):
-        cols = columns(head)
-        q_ref, d_ref, s_ref = sources[n]
-        start = feat if s_ref.shape[0] > feat else 0
-        scores = scores_ref[block_rows(n, head, rows), :]
-        probs, dscores = block_grads(
-            scores, dprobs, biases[n], *statistics_of(s_ref, start, head)
-        )
-        before = (dk_in[:, cols], dv_in[:, cols]) if n == 0 else sums
-        sums[:] = [
-            before[0] + dot(dscores, q_ref[q_ref.shape[0] - rows:, cols], NN),
-            before[1] + dot(probs, d_ref[cols, :], NT),
-        ]
-        if n == BLOCKS - 1:
-            dk, dv = sums
-            dk_ref[:, cols] = (dk * SCALE).astype(dk_ref.dtype)
-            dv_ref[:, cols] = dv.astype(dv_ref.dtype)
-            for which_out, (from_ref, to_ref) in enumerate(((dk_ref, dk_out), (dv_ref, dv_out))):
-                copies.append(
-                    pltpu.make_async_copy(
-                        from_ref.at[:, cols], to_ref.at[:, cols], sems.at[2 * head + which_out]
-                    )
+    biases = bias_rows(bias_ref, which)
+
+    def products(head):
+        cols = columns(head)
+        values = own_ref[rows:2 * rows, cols]
+        dprobs = [dot(values, sources[n][1][cols, :], NN) for n in range(BLOCKS - 1)]
+        return dprobs + [dprobs_ref[head * rows:(head + 1) * rows, :]]
+
+    def finish(head, dprobs):
+        cols = columns(head)
+        blocks = []
+        for n, (_, _, s_ref) in enumerate(sources):
+            start = feat if s_ref.shape[0] > feat else 0
+            scores = scores_ref[block_rows(n, head, rows), :]
+            blocks.append(
+                block_grads(scores, dprobs[n], biases[n], *statistics_of(s_ref, start, head))
+            )
+        probs, dscores = (jnp.concatenate(parts, axis=1) for parts in zip(*blocks))
+        queries = jnp.concatenate([q[q.shape[0] - rows:, cols] for q, _, _ in sources], axis=0)
+        grads = jnp.concatenate([d[cols, :] for _, d, _ in sources], axis=1)
+        dk = dk_in[:, cols] + dot(dscores, queries, NN)
+        dv = dv_in[:, cols] + dot(probs, grads, NT)
+        dk_ref[:, cols] = (dk * SCALE).astype(dk_ref.dtype)
+        dv_ref[:, cols] = dv.astype(dv_ref.dtype)
+        for which_out, (from_ref, to_ref) in enumerate(((dk_ref, dk_out), (dv_ref, dv_out))):
+            copies.append(
+                pltpu.make_async_copy(
+                    from_ref.at[:, cols], to_ref.at[:, cols], sems.at[2 * head + which_out]
                 )
-                copies[-1].start()
-
-    steps = [(head, n) for head in range(feat // HEAD_DIM) for n in range(BLOCKS)]
-    in_order(steps, products, finish)
+            )
+            copies[-1].start()
+
+    in_order([(head,) for head in range(feat // HEAD_DIM)], products, finish)
     for copy in copies:
         copy.wait()
 
 
-def key_side(pos, tile_mask, own, sources, scores, dprobs, begun):
+def key_side(bias, own, sources, scores, dprobs, begun):
     rows, feat = begun[0].shape
-    operands = [pos, tile_mask, own]
+    operands = [bias, own]
     for _, q, d, s in sources:
         operands += [q, d, s]
     operands += [scores, dprobs, *begun]
     return pl.pallas_call(
         functools.partial(key_kernel, [source[0] for source in sources]),
-        in_specs=[SMEM if x.dtype == jnp.int32 else VMEM for x in operands],
+        in_specs=[VMEM] * len(operands),
         out_specs=[ANY] * 2,
         out_shape=[jax.ShapeDtypeStruct((rows, feat), jnp.bfloat16)] * 2,
         scratch_shapes=[
@@ -545,6 +536,8 @@
     kvq_x = send(kvq, in_pair)
     near = send(after(reward_grad, kvq), lambda c, h: (c, h ^ 1))
     order = jnp.stack([head, head ^ 1, head ^ 2, head ^ 3])
+    own_bias, other_bias = biases_of(pos, tile_mask, rows)
+    near = after(near, own_bias, other_bias)
     begun, kept = begin_project(order, out_weight, reward_grad, near)
     far = after(far, begun)
     far_near = send(far, lambda c, h: (c, h ^ 1))
@@ -552,9 +545,9 @@
     kv_g = send(second[:2 * rows], forward)
     d_out_t = end_project(kept, far, far_near, after(begun, second))
     out, run, kept_weights = forward_part(
-        pos, tile_mask, after(kvq, d_out_t), [0, 2, 1, 3], [kvq_a, kvq_x, kvq_b]
-    )
-    stats, packed = statistics(pos, tile_mask, kvq, 4, kv_g, out, run, d_out_t)
+        own_bias, after(kvq, d_out_t), [0, 2, 1, 3], [kvq_a, kvq_x, kvq_b]
+    )
+    stats, packed = statistics(own_bias, kvq, 4, kv_g, out, run, d_out_t)
     q_g = send(after(second[2 * rows:], out), forward)
     d_g = send(d_out_t, across)
     p_b = send(packed, odd_chain)
@@ -562,12 +555,11 @@
     p_x = send(packed, in_pair)
     s_g = send(stats, across)
     grad_queries, *begun_keys, scores, dprobs = query_side(
-        pos, tile_mask, kvq, [0, 2, 1, 3, 4], [kvq_a, kvq_x, kvq_b, kv_g], d_out_t,
+        own_bias, kvq, [0, 2, 1, 3, 4], [kvq_a, kvq_x, kvq_b, kv_g], d_out_t,
         stats, run, kept_weights, q_g, d_g,
     )
     grad_keys, grad_values = key_side(
-        pos,
-        tile_mask,
+        other_bias,
         kvq,
         [
             (2, kvq_a, p_a, p_a),

time: 64.3 us -> 63.2 us (0.983)
  Pallas kernels: 20 us -> 17.8 us
  local copies, waits for them, and re-layouts: 4.04 us -> 4.74 us
    pallas_call x4 -> x5, Pallas kernels: 11 us -> 9.43 us  [kernel_call(): pl.pallas_call(kernel, in_specs=[SMEM if x.dtype == jnp.int32 else VMEM f...]
    unnamed x8, local copies, waits for them, and re-layouts: 3.95 us -> 4.65 us
    pallas_call x1, Pallas kernels: 3.71 us -> 3.03 us  [key_side(): pl.pallas_call(functools.partial(key_kernel, [source[0] for source in sou...]
  transfers between devices with their start and end apart: 13 -> 13, of which waited for: 5 -> 5; matrix products, arithmetic and copies ran while one was open for 0% -> 1% of each run, Pallas kernels for 22% -> 20%
where the time goes in v6:
time: 63.2 us; the launch traced here: 62.5 us
  starting transfers between devices  24.9 us (39%)
  Pallas kernels  17.8 us (28%)
  waiting for transfers between devices  14 us (22%)
  local copies, waits for them, and re-layouts  4.74 us (8%)
  between operations  0.8 us (1%)
    ppermute x13, starting transfers between devices, send(): return lax.ppermute(array, BOTH, pairs)  24.9 us
    ppermute x13, waiting for transfers between devices, send(): return lax.ppermute(array, BOTH, pairs)  14 us
    pallas_call x5, Pallas kernels, kernel_call(): pl.pallas_call(kernel, in_specs=[SMEM if x.dtype == jnp.int32 else VMEM f...  9.43 us
    unnamed x8, local copies, waits for them, and re-layouts  4.65 us
    pallas_call x1, Pallas kernels, begin_project(): pl.pallas_call(begin_kernel, in_specs=[SMEM, ANY, VMEM, VMEM], out_specs=...  3.2 us
    pallas_call x1, Pallas kernels, key_side(): pl.pallas_call(functools.partial(key_kernel, [source[0] for source in sou...  3.03 us
    pallas_call x1, Pallas kernels, pack(): pl.pallas_call(pack_kernel, in_specs=[ANY] * count, out_specs=VMEM, out_s...  2.16 us
  transfers between devices with their start and end apart: 13, of which 5 were waited for; matrix products, arithmetic and copies ran while one was open for 1% of the time, Pallas kernels for 20%

profile of v6, /device:TPU:8, one launch (start us, length us, event | category | flops | bytes accessed | tf_op | source)
XLA Modules:
  0.0 62.5 jit_solution(14616064342427623280)
XLA Ops:
  0.6 2.2 %shard_map.86.rest_0_.own_ref = bf16[768,640]{1,0:T(8,128)(2,1)} custom-call(bf16[256,640]{1,0:T(8,128)(2,1)} %refs_0_.1, bf16[256,640]{1,0:T(8,128)(2,1)} %refs_1_.1, bf16[256,640]{1,0:T(8,128)(2,1)} %refs_2_.1), custom_call_target="tpu_custom_call" | custom-call | bytes 1966080 | tf_op jit(solution)/shard_map/pallas_call | solution.py:109
  2.9 1.9 %collective-permute-start.1 = (bf16[768,640]{1,0:T(8,128)(2,1)}, bf16[768,640]{1,0:T(8,128)(2,1)S(1)}, u32[]{:S(2)}, u32[]{:S(2)}) collective-permute-start(bf16[768,640]{1,0:T(8,128)(2,1)} %shard_map.86.rest_0_.own_ref), channel_id=1, source_target_pairs={{0,4},{1,5},{2,6},{3,7},{4,0},{5,1},{6,2},{7,3},{8,12},{9,13},{10,... | collective-permute-start | bytes 2949128 | tf_op jit(solution)/shard_map/ppermute | solution.py:58
  4.8 4.6 %collective-permute-start.2 = (bf16[768,640]{1,0:T(8,128)(2,1)}, bf16[768,640]{1,0:T(8,128)(2,1)S(1)}, u32[]{:S(2)}, u32[]{:S(2)}) collective-permute-start(bf16[768,640]{1,0:T(8,128)(2,1)} %shard_map.86.rest_0_.own_ref), channel_id=1, source_target_pairs={{8,16},{9,17},{10,18},{11,19},{12,20},{13,21},{14,22},{15,23},{16,... | collective-permute-start | bytes 2949128 | tf_op jit(solution)/shard_map/ppermute | solution.py:58
  9.5 1.6 %collective-permute-start.5 = (bf16[256,1280]{1,0:T(8,128)(2,1)}, bf16[256,1280]{1,0:T(8,128)(2,1)}, u32[]{:S(2)}, u32[]{:S(2)}) collective-permute-start(bf16[256,1280]{1,0:T(8,128)(2,1)} %g_a.1), channel_id=1, source_target_pairs={{0,2},{1,3},{2,0},{3,1},{4,6},{5,7},{6,4},{7,5},{8,10},{9,11},{10,... | collective-permute-start | bytes 1966088 | tf_op jit(solution)/shard_map/ppermute | solution.py:58
  11.1 0.7 %copy-done.3 = s32[16,10]{1,0:T(8,128)S(1)} copy-done((s32[16,10]{1,0:T(8,128)S(1)}, s32[16,10]{1,0:T(8,128)}, u32[]{:S(2)}) %copy-start.3) | copy-done | bytes 664
  11.8 0.8 %shard_map.85 = (f32[16,256]{1,0:T(8,128)S(1)}, f32[16,256]{1,0:T(8,128)S(1)}) custom-call(s32[1]{0:T(128)} %bitcast.pos_ref, s32[16,10]{1,0:T(8,128)S(1)} %copy-done.3), custom_call_target="tpu_custom_call" | custom-call | bytes 644 | tf_op jit(solution)/shard_map/pallas_call | solution.py:38
  12.7 2.9 %copy-done.1 = bf16[640,5120]{1,0:T(8,128)(2,1)S(1)} copy-done((bf16[640,5120]{1,0:T(8,128)(2,1)S(1)}, bf16[640,5120]{1,0:T(8,128)(2,1)}, u32[]{:S(2)}) %copy-start.1) | copy-done | bytes 6553624
  15.5 1.1 %copy-done.2 = bf16[256,1280]{1,0:T(8,128)(2,1)S(1)} copy-done((bf16[256,1280]{1,0:T(8,128)(2,1)S(1)}, bf16[256,1280]{1,0:T(8,128)(2,1)}, u32[]{:S(2)}) %copy-start.2) | copy-done | bytes 655384
  16.6 3.2 %shard_map.87 = (f32[640,256]{1,0:T(8,128)S(1)}, bf16[640,2560]{1,0:T(8,128)(2,1)S(1)}) custom-call(s32[4]{0:T(128)S(1)} %pad_add_fusion.order_ref, bf16[640,5120]{1,0:T(8,128)(2,1)S(1)} %copy-done.1, bf16[256,1280]{1,0:T(8,128)(2,1)S(1)} %copy-done.2, bf16[256,1280]{1,0:T(8,128)(2,1)} %collective-permute-done.4.g_b), custom_call_target="tpu_custom_call" | custom-call | flops 838860800 | bytes 6553600 | tf_op jit(solution)/shard_map/pallas_call | solution.py:141
  19.8 7.1 %collective-permute-done.5.g_a = bf16[256,1280]{1,0:T(8,128)(2,1)} collective-permute-done((bf16[256,1280]{1,0:T(8,128)(2,1)}, bf16[256,1280]{1,0:T(8,128)(2,1)}, u32[]{:S(2)}, u32[]{:S(2)}) %collective-permute-start.5) | collective-permute-done | bytes 655392 | tf_op jit(solution)/shard_map/ppermute | solution.py:58
  27.0 3.8 %collective-permute-done.2.rest_3_.rest_2_.rest_6_ = bf16[768,640]{1,0:T(8,128)(2,1)S(1)} collective-permute-done((bf16[768,640]{1,0:T(8,128)(2,1)}, bf16[768,640]{1,0:T(8,128)(2,1)S(1)}, u32[]{:S(2)}, u32[]{:S(2)}) %collective-permute-start.2) | collective-permute-done | bytes 983072 | tf_op jit(solution)/shard_map/ppermute | solution.py:58
  31.0 3.6 %collective-permute-start.3 = (bf16[512,640]{1,0:T(8,128)(2,1)S(1)}, bf16[512,640]{1,0:T(8,128)(2,1)S(1)}, u32[]{:S(2)}, u32[]{:S(2)}) collective-permute-start(bf16[512,640]{1,0:T(8,128)(2,1)S(1)} %slice.8), channel_id=1, source_target_pairs={{0,8},{1,5},{2,10},{3,7},{5,1},{7,3},{8,16},{9,13},{10,18},{11,15}... | collective-permute-start | bytes 1966088 | tf_op jit(solution)/shard_map/ppermute | solution.py:58
  34.7 2.1 %shard_map.88.d_ref.rest_4_ = bf16[640,256]{1,0:T(8,128)(2,1)S(1)} custom-call(bf16[640,2560]{1,0:T(8,128)(2,1)S(1)} %get-tuple-element.29.w_ref, bf16[256,1280]{1,0:T(8,128)(2,1)} %collective-permute-done.5.g_a, bf16[256,1280]{1,0:T(8,128)(2,1)S(1)} %collective-permute-done.6.g_b, f32[640,256]{1,0:T(8,128)S(1)} %get-tuple-element.32.begun), custom_call_target="tpu_custom_call" | custom-call | flops 838860800 | bytes 5242880 | tf_op jit(solution)/shard_map/pallas_call | solution.py:38
  36.9 2.0 %shard_map.89 = (f32[640,256]{1,0:T(8,128)S(1)}, f32[80,256]{1,0:T(8,128)S(1)}, f32[5120,256]{1,0:T(8,128)S(1)}) custom-call(f32[16,256]{1,0:T(8,128)S(1)} %get-tuple-element.25.bias_ref, bf16[768,640]{1,0:T(8,128)(2,1)S(1)} %copy-done, bf16[768,640]{1,0:T(8,128)(2,1)S(1)} %collective-permute-done.rest_1_.rest_0_, ...), custom_call_target="tpu_custom_call" | custom-call | flops 671088640 | bytes 3948544 | tf_op jit(solution)/shard_map/pallas_call | solution.py:38
  38.8 1.9 %collective-permute-start.7 = (bf16[256,640]{1,0:T(8,128)(2,1)S(1)}, bf16[256,640]{1,0:T(8,128)(2,1)S(1)}, u32[]{:S(2)}, u32[]{:S(2)}) collective-permute-start(bf16[256,640]{1,0:T(8,128)(2,1)S(1)} %slice.9), channel_id=1, source_target_pairs={{0,8},{1,5},{2,10},{3,7},{5,1},{7,3},{8,16},{9,13},{10,18},{11,15}... | collective-permute-start | bytes 983048 | tf_op jit(solution)/shard_map/ppermute | solution.py:58
  40.8 1.9 %collective-permute-start.8 = (bf16[640,256]{1,0:T(8,128)(2,1)S(1)}, bf16[640,256]{1,0:T(8,128)(2,1)S(1)}, u32[]{:S(2)}, u32[]{:S(2)}) collective-permute-start(bf16[640,256]{1,0:T(8,128)(2,1)S(1)} %shard_map.88.d_ref.rest_4_), channel_id=1, source_target_pairs={{4,8},{5,9},{6,10},{7,11},{8,4},{9,5},{10,6},{11,7},{12,16},{13,17... | collective-permute-start | bytes 983048 | tf_op jit(solution)/shard_map/ppermute | solution.py:58
  42.7 0.8 %collective-permute-done.3.w_ref.rest_3_ = bf16[512,640]{1,0:T(8,128)(2,1)S(1)} collective-permute-done((bf16[512,640]{1,0:T(8,128)(2,1)S(1)}, bf16[512,640]{1,0:T(8,128)(2,1)S(1)}, u32[]{:S(2)}, u32[]{:S(2)}) %collective-permute-start.3) | collective-permute-done | bytes 655392 | tf_op jit(solution)/shard_map/ppermute | solution.py:58
  43.5 0.9 %shard_map.90 = (bf16[32,256]{1,0:T(8,128)(2,1)S(1)}, bf16[672,256]{1,0:T(8,128)(2,1)S(1)}) custom-call(f32[16,256]{1,0:T(8,128)S(1)} %get-tuple-element.25.bias_ref, bf16[768,640]{1,0:T(8,128)(2,1)S(1)} %copy-done, bf16[512,640]{1,0:T(8,128)(2,1)S(1)} %collective-permute-done.3.w_ref.rest_3_, f32[640,256]{1,0:T(8,128)S(1)} %get-tuple-element.34.out_in, ...), custom_call_target="tpu_custom_call" | custom-call | flops 167772160 | bytes 2719744 | tf_op jit(solution)/shard_map/pallas_call | solution.py:38
  44.4 0.7 %collective-permute-start.10 = (bf16[672,256]{1,0:T(8,128)(2,1)S(1)}, bf16[672,256]{1,0:T(8,128)(2,1)S(1)}, u32[]{:S(2)}, u32[]{:S(2)}) collective-permute-start(bf16[672,256]{1,0:T(8,128)(2,1)S(1)} %get-tuple-element.40), channel_id=1, source_target_pairs={{0,4},{1,5},{2,6},{3,7},{4,0},{5,1},{6,2},{7,3},{8,12},{9,13},{10,... | collective-permute-start | bytes 1032200 | tf_op jit(solution)/shard_map/ppermute | solution.py:58
  45.1 3.5 %collective-permute-start.11 = (bf16[672,256]{1,0:T(8,128)(2,1)S(1)}, bf16[672,256]{1,0:T(8,128)(2,1)S(1)}, u32[]{:S(2)}, u32[]{:S(2)}) collective-permute-start(bf16[672,256]{1,0:T(8,128)(2,1)S(1)} %get-tuple-element.40), channel_id=1, source_target_pairs={{8,16},{9,17},{10,18},{11,19},{12,20},{13,21},{14,22},{15,23},{16,... | collective-permute-start | bytes 1032200 | tf_op jit(solution)/shard_map/ppermute | solution.py:58
  48.7 4.8 %collective-permute-start.12 = (bf16[32,256]{1,0:T(8,128)(2,1)S(1)}, bf16[32,256]{1,0:T(8,128)(2,1)S(1)}, u32[]{:S(2)}, u32[]{:S(2)}) collective-permute-start(bf16[32,256]{1,0:T(8,128)(2,1)S(1)} %get-tuple-element.36.rest_5_), channel_id=1, source_target_pairs={{4,8},{5,9},{6,10},{7,11},{8,4},{9,5},{10,6},{11,7},{12,16},{13,17... | collective-permute-start | bytes 49160 | tf_op jit(solution)/shard_map/ppermute | solution.py:58
  53.9 3.6 %shard_map.91 = (bf16[256,640]{1,0:T(8,128)(2,1)}, f32[256,640]{1,0:T(8,128)S(1)}, f32[256,640]{1,0:T(8,128)S(1)}, f32[5120,256]{1,0:T(8,128)S(1)}, f32[1280,256]{1,0:T(8,128)S(1)}) custom-call(f32[16,256]{1,0:T(8,128)S(1)} %get-tuple-element.25.bias_ref, bf16[768,640]{1,0:T(8,128)(2,1)S(1)} %copy-done, ...), custom_call_target="tpu_custom_call" | custom-call | flops 1509949440 | bytes 10928128 | tf_op jit(solution)/shard_map/pallas_call | solution.py:38
  57.5 1.9 %collective-permute-done.12.rest_11_ = bf16[32,256]{1,0:T(8,128)(2,1)S(1)} collective-permute-done((bf16[32,256]{1,0:T(8,128)(2,1)S(1)}, bf16[32,256]{1,0:T(8,128)(2,1)S(1)}, u32[]{:S(2)}, u32[]{:S(2)}) %collective-permute-start.12) | collective-permute-done | bytes 16416 | tf_op jit(solution)/shard_map/ppermute | solution.py:58
  59.4 3.0 %shard_map.92 = (bf16[256,640]{1,0:T(8,128)(2,1)}, bf16[256,640]{1,0:T(8,128)(2,1)}) custom-call(f32[16,256]{1,0:T(8,128)S(1)} %get-tuple-element.27.bias_ref, bf16[768,640]{1,0:T(8,128)(2,1)S(1)} %copy-done, bf16[768,640]{1,0:T(8,128)(2,1)S(1)} %collective-permute-done.rest_1_.rest_0_, bf16[672,256]{1,0:T(8,128)(2,1)S(1)} %collective-permute-done.9.rest_1_.rest_2_, ...), custom_call_target="tpu_custom_call" | custom-call | flops 1090519040 | bytes 14548992 | tf_op jit(solution)/shard_map/pallas_call | solution.py:503
  (22 shorter events, 0.9 us)
Async XLA Ops:
  2.8 24.2 %collective-permute-start = (bf16[768,640]{1,0:T(8,128)(2,1)}, bf16[768,640]{1,0:T(8,128)(2,1)S(1)}, u32[]{:S(2)}, u32[]{:S(2)}) collective-permute-start(bf16[768,640]{1,0:T(8,128)(2,1)} %shard_map.86.rest_0_.own_ref), channel_id=1, source_target_pairs={{0,8},{1,9},{2,10},{3,11},{4,12},{5,13},{6,14},{7,15},{8,0},{9,1},... | collective-permute-start | bytes 2949128 | tf_op jit(solution)/shard_map/ppermute | solution.py:58
  2.9 24.1 %collective-permute-start.1 = (bf16[768,640]{1,0:T(8,128)(2,1)}, bf16[768,640]{1,0:T(8,128)(2,1)S(1)}, u32[]{:S(2)}, u32[]{:S(2)}) collective-permute-start(bf16[768,640]{1,0:T(8,128)(2,1)} %shard_map.86.rest_0_.own_ref), channel_id=1, source_target_pairs={{0,4},{1,5},{2,6},{3,7},{4,0},{5,1},{6,2},{7,3},{8,12},{9,13},{10,... | collective-permute-start | bytes 2949128 | tf_op jit(solution)/shard_map/ppermute | solution.py:58
  4.8 26.0 %collective-permute-start.2 = (bf16[768,640]{1,0:T(8,128)(2,1)}, bf16[768,640]{1,0:T(8,128)(2,1)S(1)}, u32[]{:S(2)}, u32[]{:S(2)}) collective-permute-start(bf16[768,640]{1,0:T(8,128)(2,1)} %shard_map.86.rest_0_.own_ref), channel_id=1, source_target_pairs={{8,16},{9,17},{10,18},{11,19},{12,20},{13,21},{14,22},{15,23},{16,... | collective-permute-start | bytes 2949128 | tf_op jit(solution)/shard_map/ppermute | solution.py:58
  9.4 3.2 %collective-permute-start.4 = (bf16[256,1280]{1,0:T(8,128)(2,1)}, bf16[256,1280]{1,0:T(8,128)(2,1)}, u32[]{:S(2)}, u32[]{:S(2)}) collective-permute-start(bf16[256,1280]{1,0:T(8,128)(2,1)} %g_a.1), channel_id=1, source_target_pairs={{0,1},{1,0},{2,3},{3,2},{4,5},{5,4},{6,7},{7,6},{8,9},{9,8},{10,11... | collective-permute-start | bytes 1966088 | tf_op jit(solution)/shard_map/ppermute | solution.py:58
  9.5 17.5 %collective-permute-start.5 = (bf16[256,1280]{1,0:T(8,128)(2,1)}, bf16[256,1280]{1,0:T(8,128)(2,1)}, u32[]{:S(2)}, u32[]{:S(2)}) collective-permute-start(bf16[256,1280]{1,0:T(8,128)(2,1)} %g_a.1), channel_id=1, source_target_pairs={{0,2},{1,3},{2,0},{3,1},{4,6},{5,7},{6,4},{7,5},{8,10},{9,11},{10,... | collective-permute-start | bytes 1966088 | tf_op jit(solution)/shard_map/ppermute | solution.py:58
  11.1 0.7 %copy-start.3 = (s32[16,10]{1,0:T(8,128)S(1)}, s32[16,10]{1,0:T(8,128)}, u32[]{:S(2)}) copy-start(s32[16,10]{1,0:T(8,128)} %mask_ref.1) | copy-start | bytes 1924
  12.7 2.9 %copy-start.1 = (bf16[640,5120]{1,0:T(8,128)(2,1)S(1)}, bf16[640,5120]{1,0:T(8,128)(2,1)}, u32[]{:S(2)}) copy-start(bf16[640,5120]{1,0:T(8,128)(2,1)} %w_ref.1) | copy-start | bytes 19660804
  15.5 1.1 %copy-start.2 = (bf16[256,1280]{1,0:T(8,128)(2,1)S(1)}, bf16[256,1280]{1,0:T(8,128)(2,1)}, u32[]{:S(2)}) copy-start(bf16[256,1280]{1,0:T(8,128)(2,1)} %g_a.1) | copy-start | bytes 1966084
  27.0 9.9 %copy-start = (bf16[768,640]{1,0:T(8,128)(2,1)S(1)}, bf16[768,640]{1,0:T(8,128)(2,1)}, u32[]{:S(2)}) copy-start(bf16[768,640]{1,0:T(8,128)(2,1)} %shard_map.86.rest_0_.own_ref) | copy-start | bytes 2949124
  27.0 7.7 %collective-permute-start.6 = (bf16[256,1280]{1,0:T(8,128)(2,1)}, bf16[256,1280]{1,0:T(8,128)(2,1)S(1)}, u32[]{:S(2)}, u32[]{:S(2)}) collective-permute-start(bf16[256,1280]{1,0:T(8,128)(2,1)} %collective-permute-done.5.g_a), channel_id=1, source_target_pairs={{0,1},{1,0},{2,3},{3,2},{4,5},{5,4},{6,7},{7,6},{8,9},{9,8},{10,11... | collective-permute-start | bytes 1966088 | tf_op jit(solution)/shard_map/ppermute | solution.py:58
  31.0 12.5 %collective-permute-start.3 = (bf16[512,640]{1,0:T(8,128)(2,1)S(1)}, bf16[512,640]{1,0:T(8,128)(2,1)S(1)}, u32[]{:S(2)}, u32[]{:S(2)}) collective-permute-start(bf16[512,640]{1,0:T(8,128)(2,1)S(1)} %slice.8), channel_id=1, source_target_pairs={{0,8},{1,5},{2,10},{3,7},{5,1},{7,3},{8,16},{9,13},{10,18},{11,15}... | collective-permute-start | bytes 1966088 | tf_op jit(solution)/shard_map/ppermute | solution.py:58
  38.8 9.9 %collective-permute-start.7 = (bf16[256,640]{1,0:T(8,128)(2,1)S(1)}, bf16[256,640]{1,0:T(8,128)(2,1)S(1)}, u32[]{:S(2)}, u32[]{:S(2)}) collective-permute-start(bf16[256,640]{1,0:T(8,128)(2,1)S(1)} %slice.9), channel_id=1, source_target_pairs={{0,8},{1,5},{2,10},{3,7},{5,1},{7,3},{8,16},{9,13},{10,18},{11,15}... | collective-permute-start | bytes 983048 | tf_op jit(solution)/shard_map/ppermute | solution.py:58
  40.8 13.1 %collective-permute-start.8 = (bf16[640,256]{1,0:T(8,128)(2,1)S(1)}, bf16[640,256]{1,0:T(8,128)(2,1)S(1)}, u32[]{:S(2)}, u32[]{:S(2)}) collective-permute-start(bf16[640,256]{1,0:T(8,128)(2,1)S(1)} %shard_map.88.d_ref.rest_4_), channel_id=1, source_target_pairs={{4,8},{5,9},{6,10},{7,11},{8,4},{9,5},{10,6},{11,7},{12,16},{13,17... | collective-permute-start | bytes 983048 | tf_op jit(solution)/shard_map/ppermute | solution.py:58
  44.4 15.0 %collective-permute-start.10 = (bf16[672,256]{1,0:T(8,128)(2,1)S(1)}, bf16[672,256]{1,0:T(8,128)(2,1)S(1)}, u32[]{:S(2)}, u32[]{:S(2)}) collective-permute-start(bf16[672,256]{1,0:T(8,128)(2,1)S(1)} %get-tuple-element.40), channel_id=1, source_target_pairs={{0,4},{1,5},{2,6},{3,7},{4,0},{5,1},{6,2},{7,3},{8,12},{9,13},{10,... | collective-permute-start | bytes 1032200 | tf_op jit(solution)/shard_map/ppermute | solution.py:58
  45.1 14.3 %collective-permute-start.11 = (bf16[672,256]{1,0:T(8,128)(2,1)S(1)}, bf16[672,256]{1,0:T(8,128)(2,1)S(1)}, u32[]{:S(2)}, u32[]{:S(2)}) collective-permute-start(bf16[672,256]{1,0:T(8,128)(2,1)S(1)} %get-tuple-element.40), channel_id=1, source_target_pairs={{8,16},{9,17},{10,18},{11,19},{12,20},{13,21},{14,22},{15,23},{16,... | collective-permute-start | bytes 1032200 | tf_op jit(solution)/shard_map/ppermute | solution.py:58
  48.6 10.8 %collective-permute-start.9 = (bf16[672,256]{1,0:T(8,128)(2,1)S(1)}, bf16[672,256]{1,0:T(8,128)(2,1)S(1)}, u32[]{:S(2)}, u32[]{:S(2)}) collective-permute-start(bf16[672,256]{1,0:T(8,128)(2,1)S(1)} %get-tuple-element.40), channel_id=1, source_target_pairs={{0,8},{1,9},{2,10},{3,11},{4,12},{5,13},{6,14},{7,15},{8,0},{9,1},... | collective-permute-start | bytes 1032200 | tf_op jit(solution)/shard_map/ppermute | solution.py:58
  48.7 10.7 %collective-permute-start.12 = (bf16[32,256]{1,0:T(8,128)(2,1)S(1)}, bf16[32,256]{1,0:T(8,128)(2,1)S(1)}, u32[]{:S(2)}, u32[]{:S(2)}) collective-permute-start(bf16[32,256]{1,0:T(8,128)(2,1)S(1)} %get-tuple-element.36.rest_5_), channel_id=1, source_target_pairs={{4,8},{5,9},{6,10},{7,11},{8,4},{9,5},{10,6},{11,7},{12,16},{13,17... | collective-permute-start | bytes 49160 | tf_op jit(solution)/shard_map/ppermute | solution.py:58

commit v7 on v6

--- a/solution.py
+++ b/solution.py
@@ -545,7 +545,7 @@
     kv_g = send(second[:2 * rows], forward)
     d_out_t = end_project(kept, far, far_near, after(begun, second))
     out, run, kept_weights = forward_part(
-        own_bias, after(kvq, d_out_t), [0, 2, 1, 3], [kvq_a, kvq_x, kvq_b]
+        own_bias, after(kvq, d_out_t), [0, 1, 2, 3], [kvq_x, kvq_a, kvq_b]
     )
     stats, packed = statistics(own_bias, kvq, 4, kv_g, out, run, d_out_t)
     q_g = send(after(second[2 * rows:], out), forward)
@@ -555,15 +555,15 @@
     p_x = send(packed, in_pair)
     s_g = send(stats, across)
     grad_queries, *begun_keys, scores, dprobs = query_side(
-        own_bias, kvq, [0, 2, 1, 3, 4], [kvq_a, kvq_x, kvq_b, kv_g], d_out_t,
+        own_bias, kvq, [0, 1, 2, 3, 4], [kvq_x, kvq_a, kvq_b, kv_g], d_out_t,
         stats, run, kept_weights, q_g, d_g,
     )
     grad_keys, grad_values = key_side(
         other_bias,
         kvq,
         [
+            (1, kvq_x, p_x, p_x),
             (2, kvq_a, p_a, p_a),
-            (1, kvq_x, p_x, p_x),
             (3, kvq_b, p_b, p_b),
             (4, q_g, d_g, s_g),
         ],

time: 63.2 us -> 63 us (level)
  starting transfers between devices: 24.9 us -> 22.4 us
  waiting for transfers between devices: 14 us -> 16.5 us
    ppermute x13, waiting for transfers between devices: 14 us -> 16.5 us  [send(): return lax.ppermute(array, BOTH, pairs)]
    ppermute x13, starting transfers between devices: 24.9 us -> 22.4 us  [send(): return lax.ppermute(array, BOTH, pairs)]
  transfers between devices with their start and end apart: 13 -> 13, of which waited for: 5 -> 7; matrix products, arithmetic and copies ran while one was open for 1% -> 1% of each run, Pallas kernels for 20% -> 20%
where the time goes in v7:
time: 63 us; the launch traced here: 62.4 us
  starting transfers between devices  22.4 us (36%)
  Pallas kernels  17.8 us (28%)
  waiting for transfers between devices  16.5 us (26%)
  local copies, waits for them, and re-layouts  4.74 us (8%)
  between operations  0.78 us (1%)
    ppermute x13, starting transfers between devices, send(): return lax.ppermute(array, BOTH, pairs)  22.4 us
    ppermute x13, waiting for transfers between devices, send(): return lax.ppermute(array, BOTH, pairs)  16.5 us
    pallas_call x5, Pallas kernels, kernel_call(): pl.pallas_call(kernel, in_specs=[SMEM if x.dtype == jnp.int32 else VMEM f...  9.42 us
    unnamed x8, local copies, waits for them, and re-layouts  4.65 us
    pallas_call x1, Pallas kernels, begin_project(): pl.pallas_call(begin_kernel, in_specs=[SMEM, ANY, VMEM, VMEM], out_specs=...  3.2 us
    pallas_call x1, Pallas kernels, key_side(): pl.pallas_call(functools.partial(key_kernel, [source[0] for source in sou...  3.02 us
    pallas_call x1, Pallas kernels, pack(): pl.pallas_call(pack_kernel, in_specs=[ANY] * count, out_specs=VMEM, out_s...  2.16 us
  transfers between devices with their start and end apart: 13, of which 7 were waited for; matrix products, arithmetic and copies ran while one was open for 1% of the time, Pallas kernels for 20%

profile of v7, /device:TPU:8, one launch (start us, length us, event | category | flops | bytes accessed | tf_op | source)
XLA Modules:
  0.0 62.4 jit_solution(17589287125764119604)
XLA Ops:
  0.6 2.2 %shard_map.86.rest_0_.own_ref = bf16[768,640]{1,0:T(8,128)(2,1)} custom-call(bf16[256,640]{1,0:T(8,128)(2,1)} %refs_0_.1, bf16[256,640]{1,0:T(8,128)(2,1)} %refs_1_.1, bf16[256,640]{1,0:T(8,128)(2,1)} %refs_2_.1), custom_call_target="tpu_custom_call" | custom-call | bytes 1966080 | tf_op jit(solution)/shard_map/pallas_call | solution.py:109
  2.8 1.6 %collective-permute-start = (bf16[768,640]{1,0:T(8,128)(2,1)}, bf16[768,640]{1,0:T(8,128)(2,1)S(1)}, u32[]{:S(2)}, u32[]{:S(2)}) collective-permute-start(bf16[768,640]{1,0:T(8,128)(2,1)} %shard_map.86.rest_0_.own_ref), channel_id=1, source_target_pairs={{0,4},{1,5},{2,6},{3,7},{4,0},{5,1},{6,2},{7,3},{8,12},{9,13},{10,... | collective-permute-start | bytes 2949128 | tf_op jit(solution)/shard_map/ppermute | solution.py:58
  4.8 4.6 %collective-permute-start.2 = (bf16[768,640]{1,0:T(8,128)(2,1)}, bf16[768,640]{1,0:T(8,128)(2,1)S(1)}, u32[]{:S(2)}, u32[]{:S(2)}) collective-permute-start(bf16[768,640]{1,0:T(8,128)(2,1)} %shard_map.86.rest_0_.own_ref), channel_id=1, source_target_pairs={{8,16},{9,17},{10,18},{11,19},{12,20},{13,21},{14,22},{15,23},{16,... | collective-permute-start | bytes 2949128 | tf_op jit(solution)/shard_map/ppermute | solution.py:58
  9.5 1.6 %collective-permute-start.5 = (bf16[256,1280]{1,0:T(8,128)(2,1)}, bf16[256,1280]{1,0:T(8,128)(2,1)}, u32[]{:S(2)}, u32[]{:S(2)}) collective-permute-start(bf16[256,1280]{1,0:T(8,128)(2,1)} %g_a.1), channel_id=1, source_target_pairs={{0,2},{1,3},{2,0},{3,1},{4,6},{5,7},{6,4},{7,5},{8,10},{9,11},{10,... | collective-permute-start | bytes 1966088 | tf_op jit(solution)/shard_map/ppermute | solution.py:58
  12.7 2.9 %copy-done.1 = bf16[640,5120]{1,0:T(8,128)(2,1)S(1)} copy-done((bf16[640,5120]{1,0:T(8,128)(2,1)S(1)}, bf16[640,5120]{1,0:T(8,128)(2,1)}, u32[]{:S(2)}) %copy-start.1) | copy-done | bytes 6553624
  15.5 1.1 %copy-done.2 = bf16[256,1280]{1,0:T(8,128)(2,1)S(1)} copy-done((bf16[256,1280]{1,0:T(8,128)(2,1)S(1)}, bf16[256,1280]{1,0:T(8,128)(2,1)}, u32[]{:S(2)}) %copy-start.2) | copy-done | bytes 655384
  16.6 3.2 %shard_map.87 = (f32[640,256]{1,0:T(8,128)S(1)}, bf16[640,2560]{1,0:T(8,128)(2,1)S(1)}) custom-call(s32[4]{0:T(128)S(1)} %pad_add_fusion.order_ref, bf16[640,5120]{1,0:T(8,128)(2,1)S(1)} %copy-done.1, bf16[256,1280]{1,0:T(8,128)(2,1)S(1)} %copy-done.2, bf16[256,1280]{1,0:T(8,128)(2,1)} %collective-permute-done.4.g_b), custom_call_target="tpu_custom_call" | custom-call | flops 838860800 | bytes 6553600 | tf_op jit(solution)/shard_map/pallas_call | solution.py:141
  19.8 7.1 %collective-permute-done.5.g_a = bf16[256,1280]{1,0:T(8,128)(2,1)} collective-permute-done((bf16[256,1280]{1,0:T(8,128)(2,1)}, bf16[256,1280]{1,0:T(8,128)(2,1)}, u32[]{:S(2)}, u32[]{:S(2)}) %collective-permute-start.5) | collective-permute-done | bytes 655392 | tf_op jit(solution)/shard_map/ppermute | solution.py:58
  27.0 0.8 %collective-permute-done.1.rest_2_.rest_1_.rest_3_ = bf16[768,640]{1,0:T(8,128)(2,1)S(1)} collective-permute-done((bf16[768,640]{1,0:T(8,128)(2,1)}, bf16[768,640]{1,0:T(8,128)(2,1)S(1)}, u32[]{:S(2)}, u32[]{:S(2)}) %collective-permute-start.1) | collective-permute-done | bytes 983072 | tf_op jit(solution)/shard_map/ppermute | solution.py:58
  27.8 3.0 %collective-permute-done.2.rest_3_.rest_2_.rest_6_ = bf16[768,640]{1,0:T(8,128)(2,1)S(1)} collective-permute-done((bf16[768,640]{1,0:T(8,128)(2,1)}, bf16[768,640]{1,0:T(8,128)(2,1)S(1)}, u32[]{:S(2)}, u32[]{:S(2)}) %collective-permute-start.2) | collective-permute-done | bytes 983072 | tf_op jit(solution)/shard_map/ppermute | solution.py:58
  31.0 3.6 %collective-permute-start.3 = (bf16[512,640]{1,0:T(8,128)(2,1)S(1)}, bf16[512,640]{1,0:T(8,128)(2,1)S(1)}, u32[]{:S(2)}, u32[]{:S(2)}) collective-permute-start(bf16[512,640]{1,0:T(8,128)(2,1)S(1)} %slice.8), channel_id=1, source_target_pairs={{0,8},{1,5},{2,10},{3,7},{5,1},{7,3},{8,16},{9,13},{10,18},{11,15}... | collective-permute-start | bytes 1966088 | tf_op jit(solution)/shard_map/ppermute | solution.py:58
  34.7 2.1 %shard_map.88.d_ref.rest_4_ = bf16[640,256]{1,0:T(8,128)(2,1)S(1)} custom-call(bf16[640,2560]{1,0:T(8,128)(2,1)S(1)} %get-tuple-element.29.w_ref, bf16[256,1280]{1,0:T(8,128)(2,1)} %collective-permute-done.5.g_a, bf16[256,1280]{1,0:T(8,128)(2,1)S(1)} %collective-permute-done.6.g_b, f32[640,256]{1,0:T(8,128)S(1)} %get-tuple-element.32.begun), custom_call_target="tpu_custom_call" | custom-call | flops 838860800 | bytes 5242880 | tf_op jit(solution)/shard_map/pallas_call | solution.py:38
  36.9 2.0 %shard_map.89 = (f32[640,256]{1,0:T(8,128)S(1)}, f32[80,256]{1,0:T(8,128)S(1)}, f32[5120,256]{1,0:T(8,128)S(1)}) custom-call(f32[16,256]{1,0:T(8,128)S(1)} %get-tuple-element.25.bias_ref, bf16[768,640]{1,0:T(8,128)(2,1)S(1)} %copy-done, bf16[768,640]{1,0:T(8,128)(2,1)S(1)} %collective-permute-done.rest_1_.rest_0_, ...), custom_call_target="tpu_custom_call" | custom-call | flops 671088640 | bytes 3948544 | tf_op jit(solution)/shard_map/pallas_call | solution.py:38
  38.8 1.9 %collective-permute-start.7 = (bf16[256,640]{1,0:T(8,128)(2,1)S(1)}, bf16[256,640]{1,0:T(8,128)(2,1)S(1)}, u32[]{:S(2)}, u32[]{:S(2)}) collective-permute-start(bf16[256,640]{1,0:T(8,128)(2,1)S(1)} %slice.9), channel_id=1, source_target_pairs={{0,8},{1,5},{2,10},{3,7},{5,1},{7,3},{8,16},{9,13},{10,18},{11,15}... | collective-permute-start | bytes 983048 | tf_op jit(solution)/shard_map/ppermute | solution.py:58
  40.8 1.9 %collective-permute-start.8 = (bf16[640,256]{1,0:T(8,128)(2,1)S(1)}, bf16[640,256]{1,0:T(8,128)(2,1)S(1)}, u32[]{:S(2)}, u32[]{:S(2)}) collective-permute-start(bf16[640,256]{1,0:T(8,128)(2,1)S(1)} %shard_map.88.d_ref.rest_4_), channel_id=1, source_target_pairs={{4,8},{5,9},{6,10},{7,11},{8,4},{9,5},{10,6},{11,7},{12,16},{13,17... | collective-permute-start | bytes 983048 | tf_op jit(solution)/shard_map/ppermute | solution.py:58
  43.5 0.9 %shard_map.90 = (bf16[32,256]{1,0:T(8,128)(2,1)S(1)}, bf16[672,256]{1,0:T(8,128)(2,1)S(1)}) custom-call(f32[16,256]{1,0:T(8,128)S(1)} %get-tuple-element.25.bias_ref, bf16[768,640]{1,0:T(8,128)(2,1)S(1)} %copy-done, bf16[512,640]{1,0:T(8,128)(2,1)S(1)} %collective-permute-done.3.w_ref.rest_3_, f32[640,256]{1,0:T(8,128)S(1)} %get-tuple-element.34.out_in, ...), custom_call_target="tpu_custom_call" | custom-call | flops 167772160 | bytes 2719744 | tf_op jit(solution)/shard_map/pallas_call | solution.py:38
  44.5 3.6 %collective-permute-start.11 = (bf16[672,256]{1,0:T(8,128)(2,1)S(1)}, bf16[672,256]{1,0:T(8,128)(2,1)S(1)}, u32[]{:S(2)}, u32[]{:S(2)}) collective-permute-start(bf16[672,256]{1,0:T(8,128)(2,1)S(1)} %get-tuple-element.40), channel_id=1, source_target_pairs={{8,16},{9,17},{10,18},{11,19},{12,20},{13,21},{14,22},{15,23},{16,... | collective-permute-start | bytes 1032200 | tf_op jit(solution)/shard_map/ppermute | solution.py:58
  48.1 1.0 %collective-permute-start.9 = (bf16[672,256]{1,0:T(8,128)(2,1)S(1)}, bf16[672,256]{1,0:T(8,128)(2,1)S(1)}, u32[]{:S(2)}, u32[]{:S(2)}) collective-permute-start(bf16[672,256]{1,0:T(8,128)(2,1)S(1)} %get-tuple-element.40), channel_id=1, source_target_pairs={{0,4},{1,5},{2,6},{3,7},{4,0},{5,1},{6,2},{7,3},{8,12},{9,13},{10,... | collective-permute-start | bytes 1032200 | tf_op jit(solution)/shard_map/ppermute | solution.py:58
  49.1 1.7 %collective-permute-done.7.rest_8_.rest_9_ = bf16[256,640]{1,0:T(8,128)(2,1)S(1)} collective-permute-done((bf16[256,640]{1,0:T(8,128)(2,1)S(1)}, bf16[256,640]{1,0:T(8,128)(2,1)S(1)}, u32[]{:S(2)}, u32[]{:S(2)}) %collective-permute-start.7) | collective-permute-done | bytes 327712 | tf_op jit(solution)/shard_map/ppermute | solution.py:58
  50.8 1.9 %collective-permute-start.12 = (bf16[32,256]{1,0:T(8,128)(2,1)S(1)}, bf16[32,256]{1,0:T(8,128)(2,1)S(1)}, u32[]{:S(2)}, u32[]{:S(2)}) collective-permute-start(bf16[32,256]{1,0:T(8,128)(2,1)S(1)} %get-tuple-element.36.rest_5_), channel_id=1, source_target_pairs={{4,8},{5,9},{6,10},{7,11},{8,4},{9,5},{10,6},{11,7},{12,16},{13,17... | collective-permute-start | bytes 49160 | tf_op jit(solution)/shard_map/ppermute | solution.py:58
  52.8 1.4 %collective-permute-done.8.rest_9_.rest_10_ = bf16[640,256]{1,0:T(8,128)(2,1)S(1)} collective-permute-done((bf16[640,256]{1,0:T(8,128)(2,1)S(1)}, bf16[640,256]{1,0:T(8,128)(2,1)S(1)}, u32[]{:S(2)}, u32[]{:S(2)}) %collective-permute-start.8) | collective-permute-done | bytes 327712 | tf_op jit(solution)/shard_map/ppermute | solution.py:58
  54.2 3.6 %shard_map.91 = (bf16[256,640]{1,0:T(8,128)(2,1)}, f32[256,640]{1,0:T(8,128)S(1)}, f32[256,640]{1,0:T(8,128)S(1)}, f32[5120,256]{1,0:T(8,128)S(1)}, f32[1280,256]{1,0:T(8,128)S(1)}) custom-call(f32[16,256]{1,0:T(8,128)S(1)} %get-tuple-element.25.bias_ref, bf16[768,640]{1,0:T(8,128)(2,1)S(1)} %copy-done, ...), custom_call_target="tpu_custom_call" | custom-call | flops 1509949440 | bytes 10928128 | tf_op jit(solution)/shard_map/pallas_call | solution.py:38
  57.8 1.6 %collective-permute-done.12.rest_11_ = bf16[32,256]{1,0:T(8,128)(2,1)S(1)} collective-permute-done((bf16[32,256]{1,0:T(8,128)(2,1)S(1)}, bf16[32,256]{1,0:T(8,128)(2,1)S(1)}, u32[]{:S(2)}, u32[]{:S(2)}) %collective-permute-start.12) | collective-permute-done | bytes 16416 | tf_op jit(solution)/shard_map/ppermute | solution.py:58
  59.4 3.0 %shard_map.92 = (bf16[256,640]{1,0:T(8,128)(2,1)}, bf16[256,640]{1,0:T(8,128)(2,1)}) custom-call(f32[16,256]{1,0:T(8,128)S(1)} %get-tuple-element.27.bias_ref, bf16[768,640]{1,0:T(8,128)(2,1)S(1)} %copy-done, bf16[768,640]{1,0:T(8,128)(2,1)S(1)} %collective-permute-done.rest_1_.rest_0_, bf16[672,256]{1,0:T(8,128)(2,1)S(1)} %collective-permute-done.9.rest_1_.rest_2_, ...), custom_call_target="tpu_custom_call" | custom-call | flops 1090519040 | bytes 14548992 | tf_op jit(solution)/shard_map/pallas_call | solution.py:503
  (22 shorter events, 3.2 us)
Async XLA Ops:
  2.8 24.2 %collective-permute-start = (bf16[768,640]{1,0:T(8,128)(2,1)}, bf16[768,640]{1,0:T(8,128)(2,1)S(1)}, u32[]{:S(2)}, u32[]{:S(2)}) collective-permute-start(bf16[768,640]{1,0:T(8,128)(2,1)} %shard_map.86.rest_0_.own_ref), channel_id=1, source_target_pairs={{0,4},{1,5},{2,6},{3,7},{4,0},{5,1},{6,2},{7,3},{8,12},{9,13},{10,... | collective-permute-start | bytes 2949128 | tf_op jit(solution)/shard_map/ppermute | solution.py:58
  4.4 23.4 %collective-permute-start.1 = (bf16[768,640]{1,0:T(8,128)(2,1)}, bf16[768,640]{1,0:T(8,128)(2,1)S(1)}, u32[]{:S(2)}, u32[]{:S(2)}) collective-permute-start(bf16[768,640]{1,0:T(8,128)(2,1)} %shard_map.86.rest_0_.own_ref), channel_id=1, source_target_pairs={{0,8},{1,9},{2,10},{3,11},{4,12},{5,13},{6,14},{7,15},{8,0},{9,1},... | collective-permute-start | bytes 2949128 | tf_op jit(solution)/shard_map/ppermute | solution.py:58
  4.8 26.0 %collective-permute-start.2 = (bf16[768,640]{1,0:T(8,128)(2,1)}, bf16[768,640]{1,0:T(8,128)(2,1)S(1)}, u32[]{:S(2)}, u32[]{:S(2)}) collective-permute-start(bf16[768,640]{1,0:T(8,128)(2,1)} %shard_map.86.rest_0_.own_ref), channel_id=1, source_target_pairs={{8,16},{9,17},{10,18},{11,19},{12,20},{13,21},{14,22},{15,23},{16,... | collective-permute-start | bytes 2949128 | tf_op jit(solution)/shard_map/ppermute | solution.py:58
  9.4 3.2 %collective-permute-start.4 = (bf16[256,1280]{1,0:T(8,128)(2,1)}, bf16[256,1280]{1,0:T(8,128)(2,1)}, u32[]{:S(2)}, u32[]{:S(2)}) collective-permute-start(bf16[256,1280]{1,0:T(8,128)(2,1)} %g_a.1), channel_id=1, source_target_pairs={{0,1},{1,0},{2,3},{3,2},{4,5},{5,4},{6,7},{7,6},{8,9},{9,8},{10,11... | collective-permute-start | bytes 1966088 | tf_op jit(solution)/shard_map/ppermute | solution.py:58
  9.5 17.5 %collective-permute-start.5 = (bf16[256,1280]{1,0:T(8,128)(2,1)}, bf16[256,1280]{1,0:T(8,128)(2,1)}, u32[]{:S(2)}, u32[]{:S(2)}) collective-permute-start(bf16[256,1280]{1,0:T(8,128)(2,1)} %g_a.1), channel_id=1, source_target_pairs={{0,2},{1,3},{2,0},{3,1},{4,6},{5,7},{6,4},{7,5},{8,10},{9,11},{10,... | collective-permute-start | bytes 1966088 | tf_op jit(solution)/shard_map/ppermute | solution.py:58
  11.1 0.7 %copy-start.3 = (s32[16,10]{1,0:T(8,128)S(1)}, s32[16,10]{1,0:T(8,128)}, u32[]{:S(2)}) copy-start(s32[16,10]{1,0:T(8,128)} %mask_ref.1) | copy-start | bytes 1924
  12.7 2.9 %copy-start.1 = (bf16[640,5120]{1,0:T(8,128)(2,1)S(1)}, bf16[640,5120]{1,0:T(8,128)(2,1)}, u32[]{:S(2)}) copy-start(bf16[640,5120]{1,0:T(8,128)(2,1)} %w_ref.1) | copy-start | bytes 19660804
  15.5 1.1 %copy-start.2 = (bf16[256,1280]{1,0:T(8,128)(2,1)S(1)}, bf16[256,1280]{1,0:T(8,128)(2,1)}, u32[]{:S(2)}) copy-start(bf16[256,1280]{1,0:T(8,128)(2,1)} %g_a.1) | copy-start | bytes 1966084
  27.0 9.9 %copy-start = (bf16[768,640]{1,0:T(8,128)(2,1)S(1)}, bf16[768,640]{1,0:T(8,128)(2,1)}, u32[]{:S(2)}) copy-start(bf16[768,640]{1,0:T(8,128)(2,1)} %shard_map.86.rest_0_.own_ref) | copy-start | bytes 2949124
  27.0 7.7 %collective-permute-start.6 = (bf16[256,1280]{1,0:T(8,128)(2,1)}, bf16[256,1280]{1,0:T(8,128)(2,1)S(1)}, u32[]{:S(2)}, u32[]{:S(2)}) collective-permute-start(bf16[256,1280]{1,0:T(8,128)(2,1)} %collective-permute-done.5.g_a), channel_id=1, source_target_pairs={{0,1},{1,0},{2,3},{3,2},{4,5},{5,4},{6,7},{7,6},{8,9},{9,8},{10,11... | collective-permute-start | bytes 1966088 | tf_op jit(solution)/shard_map/ppermute | solution.py:58
  31.0 12.5 %collective-permute-start.3 = (bf16[512,640]{1,0:T(8,128)(2,1)S(1)}, bf16[512,640]{1,0:T(8,128)(2,1)S(1)}, u32[]{:S(2)}, u32[]{:S(2)}) collective-permute-start(bf16[512,640]{1,0:T(8,128)(2,1)S(1)} %slice.8), channel_id=1, source_target_pairs={{0,8},{1,5},{2,10},{3,7},{5,1},{7,3},{8,16},{9,13},{10,18},{11,15}... | collective-permute-start | bytes 1966088 | tf_op jit(solution)/shard_map/ppermute | solution.py:58
  38.8 12.0 %collective-permute-start.7 = (bf16[256,640]{1,0:T(8,128)(2,1)S(1)}, bf16[256,640]{1,0:T(8,128)(2,1)S(1)}, u32[]{:S(2)}, u32[]{:S(2)}) collective-permute-start(bf16[256,640]{1,0:T(8,128)(2,1)S(1)} %slice.9), channel_id=1, source_target_pairs={{0,8},{1,5},{2,10},{3,7},{5,1},{7,3},{8,16},{9,13},{10,18},{11,15}... | collective-permute-start | bytes 983048 | tf_op jit(solution)/shard_map/ppermute | solution.py:58
  40.8 13.4 %collective-permute-start.8 = (bf16[640,256]{1,0:T(8,128)(2,1)S(1)}, bf16[640,256]{1,0:T(8,128)(2,1)S(1)}, u32[]{:S(2)}, u32[]{:S(2)}) collective-permute-start(bf16[640,256]{1,0:T(8,128)(2,1)S(1)} %shard_map.88.d_ref.rest_4_), channel_id=1, source_target_pairs={{4,8},{5,9},{6,10},{7,11},{8,4},{9,5},{10,6},{11,7},{12,16},{13,17... | collective-permute-start | bytes 983048 | tf_op jit(solution)/shard_map/ppermute | solution.py:58
  44.4 15.0 %collective-permute-start.10 = (bf16[672,256]{1,0:T(8,128)(2,1)S(1)}, bf16[672,256]{1,0:T(8,128)(2,1)S(1)}, u32[]{:S(2)}, u32[]{:S(2)}) collective-permute-start(bf16[672,256]{1,0:T(8,128)(2,1)S(1)} %get-tuple-element.40), channel_id=1, source_target_pairs={{0,8},{1,9},{2,10},{3,11},{4,12},{5,13},{6,14},{7,15},{8,0},{9,1},... | collective-permute-start | bytes 1032200 | tf_op jit(solution)/shard_map/ppermute | solution.py:58
  44.5 15.0 %collective-permute-start.11 = (bf16[672,256]{1,0:T(8,128)(2,1)S(1)}, bf16[672,256]{1,0:T(8,128)(2,1)S(1)}, u32[]{:S(2)}, u32[]{:S(2)}) collective-permute-start(bf16[672,256]{1,0:T(8,128)(2,1)S(1)} %get-tuple-element.40), channel_id=1, source_target_pairs={{8,16},{9,17},{10,18},{11,19},{12,20},{13,21},{14,22},{15,23},{16,... | collective-permute-start | bytes 1032200 | tf_op jit(solution)/shard_map/ppermute | solution.py:58
  48.1 11.3 %collective-permute-start.9 = (bf16[672,256]{1,0:T(8,128)(2,1)S(1)}, bf16[672,256]{1,0:T(8,128)(2,1)S(1)}, u32[]{:S(2)}, u32[]{:S(2)}) collective-permute-start(bf16[672,256]{1,0:T(8,128)(2,1)S(1)} %get-tuple-element.40), channel_id=1, source_target_pairs={{0,4},{1,5},{2,6},{3,7},{4,0},{5,1},{6,2},{7,3},{8,12},{9,13},{10,... | collective-permute-start | bytes 1032200 | tf_op jit(solution)/shard_map/ppermute | solution.py:58
  50.8 8.6 %collective-permute-start.12 = (bf16[32,256]{1,0:T(8,128)(2,1)S(1)}, bf16[32,256]{1,0:T(8,128)(2,1)S(1)}, u32[]{:S(2)}, u32[]{:S(2)}) collective-permute-start(bf16[32,256]{1,0:T(8,128)(2,1)S(1)} %get-tuple-element.36.rest_5_), channel_id=1, source_target_pairs={{4,8},{5,9},{6,10},{7,11},{8,4},{9,5},{10,6},{11,7},{12,16},{13,17... | collective-permute-start | bytes 49160 | tf_op jit(solution)/shard_map/ppermute | solution.py:58

commit v8 on v7

--- a/solution.py
+++ b/solution.py
@@ -545,10 +545,10 @@
     kv_g = send(second[:2 * rows], forward)
     d_out_t = end_project(kept, far, far_near, after(begun, second))
     out, run, kept_weights = forward_part(
-        own_bias, after(kvq, d_out_t), [0, 1, 2, 3], [kvq_x, kvq_a, kvq_b]
+        own_bias, kvq, [0, 1, 2, 3], [kvq_x, kvq_a, kvq_b]
     )
     stats, packed = statistics(own_bias, kvq, 4, kv_g, out, run, d_out_t)
-    q_g = send(after(second[2 * rows:], out), forward)
+    q_g = send(second[2 * rows:], forward)
     d_g = send(d_out_t, across)
     p_b = send(packed, odd_chain)
     p_a = send(packed, even_chain)

time: 63 us -> 62.9 us (level)
  no operation moved by 1% of the time
where the time goes in v8:
time: 62.9 us; the launch traced here: 62.5 us
  starting transfers between devices  22.4 us (36%)
  Pallas kernels  17.8 us (28%)
  waiting for transfers between devices  16.5 us (26%)
  local copies, waits for them, and re-layouts  4.74 us (8%)
  between operations  0.78 us (1%)
    ppermute x13, starting transfers between devices, send(): return lax.ppermute(array, BOTH, pairs)  22.4 us
    ppermute x13, waiting for transfers between devices, send(): return lax.ppermute(array, BOTH, pairs)  16.5 us
    pallas_call x5, Pallas kernels, kernel_call(): pl.pallas_call(kernel, in_specs=[SMEM if x.dtype == jnp.int32 else VMEM f...  9.42 us
    unnamed x8, local copies, waits for them, and re-layouts  4.65 us
    pallas_call x1, Pallas kernels, begin_project(): pl.pallas_call(begin_kernel, in_specs=[SMEM, ANY, VMEM, VMEM], out_specs=...  3.2 us
    pallas_call x1, Pallas kernels, key_side(): pl.pallas_call(functools.partial(key_kernel, [source[0] for source in sou...  3.04 us
    pallas_call x1, Pallas kernels, pack(): pl.pallas_call(pack_kernel, in_specs=[ANY] * count, out_specs=VMEM, out_s...  2.16 us
  transfers between devices with their start and end apart: 13, of which 7 were waited for; matrix products, arithmetic and copies ran while one was open for 1% of the time, Pallas kernels for 20%

profile of v8, /device:TPU:8, one launch (start us, length us, event | category | flops | bytes accessed | tf_op | source)
XLA Modules:
  0.0 62.5 jit_solution(10584260045517222153)
XLA Ops:
  0.6 2.2 %shard_map.86.rest_0_.own_ref = bf16[768,640]{1,0:T(8,128)(2,1)} custom-call(bf16[256,640]{1,0:T(8,128)(2,1)} %refs_0_.1, bf16[256,640]{1,0:T(8,128)(2,1)} %refs_1_.1, bf16[256,640]{1,0:T(8,128)(2,1)} %refs_2_.1), custom_call_target="tpu_custom_call" | custom-call | bytes 1966080 | tf_op jit(solution)/shard_map/pallas_call | solution.py:109
  2.8 1.6 %collective-permute-start = (bf16[768,640]{1,0:T(8,128)(2,1)}, bf16[768,640]{1,0:T(8,128)(2,1)S(1)}, u32[]{:S(2)}, u32[]{:S(2)}) collective-permute-start(bf16[768,640]{1,0:T(8,128)(2,1)} %shard_map.86.rest_0_.own_ref), channel_id=1, source_target_pairs={{0,4},{1,5},{2,6},{3,7},{4,0},{5,1},{6,2},{7,3},{8,12},{9,13},{10,... | collective-permute-start | bytes 2949128 | tf_op jit(solution)/shard_map/ppermute | solution.py:58
  4.8 4.6 %collective-permute-start.2 = (bf16[768,640]{1,0:T(8,128)(2,1)}, bf16[768,640]{1,0:T(8,128)(2,1)S(1)}, u32[]{:S(2)}, u32[]{:S(2)}) collective-permute-start(bf16[768,640]{1,0:T(8,128)(2,1)} %shard_map.86.rest_0_.own_ref), channel_id=1, source_target_pairs={{8,16},{9,17},{10,18},{11,19},{12,20},{13,21},{14,22},{15,23},{16,... | collective-permute-start | bytes 2949128 | tf_op jit(solution)/shard_map/ppermute | solution.py:58
  9.5 1.6 %collective-permute-start.5 = (bf16[256,1280]{1,0:T(8,128)(2,1)}, bf16[256,1280]{1,0:T(8,128)(2,1)}, u32[]{:S(2)}, u32[]{:S(2)}) collective-permute-start(bf16[256,1280]{1,0:T(8,128)(2,1)} %g_a.1), channel_id=1, source_target_pairs={{0,2},{1,3},{2,0},{3,1},{4,6},{5,7},{6,4},{7,5},{8,10},{9,11},{10,... | collective-permute-start | bytes 1966088 | tf_op jit(solution)/shard_map/ppermute | solution.py:58
  12.7 2.9 %copy-done.1 = bf16[640,5120]{1,0:T(8,128)(2,1)S(1)} copy-done((bf16[640,5120]{1,0:T(8,128)(2,1)S(1)}, bf16[640,5120]{1,0:T(8,128)(2,1)}, u32[]{:S(2)}) %copy-start.1) | copy-done | bytes 6553624
  15.5 1.1 %copy-done.2 = bf16[256,1280]{1,0:T(8,128)(2,1)S(1)} copy-done((bf16[256,1280]{1,0:T(8,128)(2,1)S(1)}, bf16[256,1280]{1,0:T(8,128)(2,1)}, u32[]{:S(2)}) %copy-start.2) | copy-done | bytes 655384
  16.6 3.2 %shard_map.87 = (f32[640,256]{1,0:T(8,128)S(1)}, bf16[640,2560]{1,0:T(8,128)(2,1)S(1)}) custom-call(s32[4]{0:T(128)S(1)} %pad_add_fusion.order_ref, bf16[640,5120]{1,0:T(8,128)(2,1)S(1)} %copy-done.1, bf16[256,1280]{1,0:T(8,128)(2,1)S(1)} %copy-done.2, bf16[256,1280]{1,0:T(8,128)(2,1)} %collective-permute-done.4.g_b), custom_call_target="tpu_custom_call" | custom-call | flops 838860800 | bytes 6553600 | tf_op jit(solution)/shard_map/pallas_call | solution.py:141
  19.8 7.1 %collective-permute-done.5.g_a = bf16[256,1280]{1,0:T(8,128)(2,1)} collective-permute-done((bf16[256,1280]{1,0:T(8,128)(2,1)}, bf16[256,1280]{1,0:T(8,128)(2,1)}, u32[]{:S(2)}, u32[]{:S(2)}) %collective-permute-start.5) | collective-permute-done | bytes 655392 | tf_op jit(solution)/shard_map/ppermute | solution.py:58
  27.0 0.8 %collective-permute-done.1.rest_2_.rest_1_.rest_3_ = bf16[768,640]{1,0:T(8,128)(2,1)S(1)} collective-permute-done((bf16[768,640]{1,0:T(8,128)(2,1)}, bf16[768,640]{1,0:T(8,128)(2,1)S(1)}, u32[]{:S(2)}, u32[]{:S(2)}) %collective-permute-start.1) | collective-permute-done | bytes 983072 | tf_op jit(solution)/shard_map/ppermute | solution.py:58
  27.8 3.0 %collective-permute-done.2.rest_3_.rest_2_.rest_6_ = bf16[768,640]{1,0:T(8,128)(2,1)S(1)} collective-permute-done((bf16[768,640]{1,0:T(8,128)(2,1)}, bf16[768,640]{1,0:T(8,128)(2,1)S(1)}, u32[]{:S(2)}, u32[]{:S(2)}) %collective-permute-start.2) | collective-permute-done | bytes 983072 | tf_op jit(solution)/shard_map/ppermute | solution.py:58
  31.0 3.6 %collective-permute-start.3 = (bf16[512,640]{1,0:T(8,128)(2,1)S(1)}, bf16[512,640]{1,0:T(8,128)(2,1)S(1)}, u32[]{:S(2)}, u32[]{:S(2)}) collective-permute-start(bf16[512,640]{1,0:T(8,128)(2,1)S(1)} %slice.8), channel_id=1, source_target_pairs={{0,8},{1,5},{2,10},{3,7},{5,1},{7,3},{8,16},{9,13},{10,18},{11,15}... | collective-permute-start | bytes 1966088 | tf_op jit(solution)/shard_map/ppermute | solution.py:58
  34.7 1.9 %collective-permute-start.7 = (bf16[256,640]{1,0:T(8,128)(2,1)S(1)}, bf16[256,640]{1,0:T(8,128)(2,1)S(1)}, u32[]{:S(2)}, u32[]{:S(2)}) collective-permute-start(bf16[256,640]{1,0:T(8,128)(2,1)S(1)} %slice.9), channel_id=1, source_target_pairs={{0,8},{1,5},{2,10},{3,7},{5,1},{7,3},{8,16},{9,13},{10,18},{11,15}... | collective-permute-start | bytes 983048 | tf_op jit(solution)/shard_map/ppermute | solution.py:58
  36.6 2.1 %shard_map.88.d_ref.rest_4_ = bf16[640,256]{1,0:T(8,128)(2,1)S(1)} custom-call(bf16[640,2560]{1,0:T(8,128)(2,1)S(1)} %get-tuple-element.27.w_ref, bf16[256,1280]{1,0:T(8,128)(2,1)} %collective-permute-done.5.g_a, bf16[256,1280]{1,0:T(8,128)(2,1)S(1)} %collective-permute-done.6.g_b, f32[640,256]{1,0:T(8,128)S(1)} %get-tuple-element.30.begun), custom_call_target="tpu_custom_call" | custom-call | flops 838860800 | bytes 5242880 | tf_op jit(solution)/shard_map/pallas_call | solution.py:38
  38.8 1.9 %collective-permute-start.8 = (bf16[640,256]{1,0:T(8,128)(2,1)S(1)}, bf16[640,256]{1,0:T(8,128)(2,1)S(1)}, u32[]{:S(2)}, u32[]{:S(2)}) collective-permute-start(bf16[640,256]{1,0:T(8,128)(2,1)S(1)} %shard_map.88.d_ref.rest_4_), channel_id=1, source_target_pairs={{4,8},{5,9},{6,10},{7,11},{8,4},{9,5},{10,6},{11,7},{12,16},{13,17... | collective-permute-start | bytes 983048 | tf_op jit(solution)/shard_map/ppermute | solution.py:58
  40.7 2.0 %shard_map.89 = (f32[640,256]{1,0:T(8,128)S(1)}, f32[80,256]{1,0:T(8,128)S(1)}, f32[5120,256]{1,0:T(8,128)S(1)}) custom-call(f32[16,256]{1,0:T(8,128)S(1)} %get-tuple-element.23.bias_ref, bf16[768,640]{1,0:T(8,128)(2,1)S(1)} %copy-done, bf16[768,640]{1,0:T(8,128)(2,1)S(1)} %collective-permute-done.rest_1_.rest_0_, ...), custom_call_target="tpu_custom_call" | custom-call | flops 671088640 | bytes 3948544 | tf_op jit(solution)/shard_map/pallas_call | solution.py:38
  43.5 0.9 %shard_map.90 = (bf16[32,256]{1,0:T(8,128)(2,1)S(1)}, bf16[672,256]{1,0:T(8,128)(2,1)S(1)}) custom-call(f32[16,256]{1,0:T(8,128)S(1)} %get-tuple-element.23.bias_ref, bf16[768,640]{1,0:T(8,128)(2,1)S(1)} %copy-done, bf16[512,640]{1,0:T(8,128)(2,1)S(1)} %collective-permute-done.3.w_ref.rest_3_, f32[640,256]{1,0:T(8,128)S(1)} %get-tuple-element.31.out_in, ...), custom_call_target="tpu_custom_call" | custom-call | flops 167772160 | bytes 2719744 | tf_op jit(solution)/shard_map/pallas_call | solution.py:38
  44.5 3.6 %collective-permute-start.11 = (bf16[672,256]{1,0:T(8,128)(2,1)S(1)}, bf16[672,256]{1,0:T(8,128)(2,1)S(1)}, u32[]{:S(2)}, u32[]{:S(2)}) collective-permute-start(bf16[672,256]{1,0:T(8,128)(2,1)S(1)} %get-tuple-element.36), channel_id=1, source_target_pairs={{8,16},{9,17},{10,18},{11,19},{12,20},{13,21},{14,22},{15,23},{16,... | collective-permute-start | bytes 1032200 | tf_op jit(solution)/shard_map/ppermute | solution.py:58
  48.1 1.0 %collective-permute-start.9 = (bf16[672,256]{1,0:T(8,128)(2,1)S(1)}, bf16[672,256]{1,0:T(8,128)(2,1)S(1)}, u32[]{:S(2)}, u32[]{:S(2)}) collective-permute-start(bf16[672,256]{1,0:T(8,128)(2,1)S(1)} %get-tuple-element.36), channel_id=1, source_target_pairs={{0,4},{1,5},{2,6},{3,7},{4,0},{5,1},{6,2},{7,3},{8,12},{9,13},{10,... | collective-permute-start | bytes 1032200 | tf_op jit(solution)/shard_map/ppermute | solution.py:58
  49.1 1.9 %collective-permute-start.12 = (bf16[32,256]{1,0:T(8,128)(2,1)S(1)}, bf16[32,256]{1,0:T(8,128)(2,1)S(1)}, u32[]{:S(2)}, u32[]{:S(2)}) collective-permute-start(bf16[32,256]{1,0:T(8,128)(2,1)S(1)} %get-tuple-element.33.rest_5_), channel_id=1, source_target_pairs={{4,8},{5,9},{6,10},{7,11},{8,4},{9,5},{10,6},{11,7},{12,16},{13,17... | collective-permute-start | bytes 49160 | tf_op jit(solution)/shard_map/ppermute | solution.py:58
  51.0 1.2 %collective-permute-done.8.rest_9_.rest_10_ = bf16[640,256]{1,0:T(8,128)(2,1)S(1)} collective-permute-done((bf16[640,256]{1,0:T(8,128)(2,1)S(1)}, bf16[640,256]{1,0:T(8,128)(2,1)S(1)}, u32[]{:S(2)}, u32[]{:S(2)}) %collective-permute-start.8) | collective-permute-done | bytes 327712 | tf_op jit(solution)/shard_map/ppermute | solution.py:58
  52.2 3.6 %shard_map.91 = (bf16[256,640]{1,0:T(8,128)(2,1)}, f32[256,640]{1,0:T(8,128)S(1)}, f32[256,640]{1,0:T(8,128)S(1)}, f32[5120,256]{1,0:T(8,128)S(1)}, f32[1280,256]{1,0:T(8,128)S(1)}) custom-call(f32[16,256]{1,0:T(8,128)S(1)} %get-tuple-element.23.bias_ref, bf16[768,640]{1,0:T(8,128)(2,1)S(1)} %copy-done, ...), custom_call_target="tpu_custom_call" | custom-call | flops 1509949440 | bytes 10928128 | tf_op jit(solution)/shard_map/pallas_call | solution.py:38
  55.9 1.6 %collective-permute-done.12.rest_11_ = bf16[32,256]{1,0:T(8,128)(2,1)S(1)} collective-permute-done((bf16[32,256]{1,0:T(8,128)(2,1)S(1)}, bf16[32,256]{1,0:T(8,128)(2,1)S(1)}, u32[]{:S(2)}, u32[]{:S(2)}) %collective-permute-start.12) | collective-permute-done | bytes 16416 | tf_op jit(solution)/shard_map/ppermute | solution.py:58
  57.4 2.0 %collective-permute-done.9.rest_1_.rest_2_ = bf16[672,256]{1,0:T(8,128)(2,1)S(1)} collective-permute-done((bf16[672,256]{1,0:T(8,128)(2,1)S(1)}, bf16[672,256]{1,0:T(8,128)(2,1)S(1)}, u32[]{:S(2)}, u32[]{:S(2)}) %collective-permute-start.9) | collective-permute-done | bytes 344096 | tf_op jit(solution)/shard_map/ppermute | solution.py:58
  59.4 3.0 %shard_map.92 = (bf16[256,640]{1,0:T(8,128)(2,1)}, bf16[256,640]{1,0:T(8,128)(2,1)}) custom-call(f32[16,256]{1,0:T(8,128)S(1)} %get-tuple-element.25.bias_ref, bf16[768,640]{1,0:T(8,128)(2,1)S(1)} %copy-done, bf16[768,640]{1,0:T(8,128)(2,1)S(1)} %collective-permute-done.rest_1_.rest_0_, bf16[672,256]{1,0:T(8,128)(2,1)S(1)} %collective-permute-done.9.rest_1_.rest_2_, ...), custom_call_target="tpu_custom_call" | custom-call | flops 1090519040 | bytes 14548992 | tf_op jit(solution)/shard_map/pallas_call | solution.py:503
  (22 shorter events, 3.2 us)
Async XLA Ops:
  2.8 24.2 %collective-permute-start = (bf16[768,640]{1,0:T(8,128)(2,1)}, bf16[768,640]{1,0:T(8,128)(2,1)S(1)}, u32[]{:S(2)}, u32[]{:S(2)}) collective-permute-start(bf16[768,640]{1,0:T(8,128)(2,1)} %shard_map.86.rest_0_.own_ref), channel_id=1, source_target_pairs={{0,4},{1,5},{2,6},{3,7},{4,0},{5,1},{6,2},{7,3},{8,12},{9,13},{10,... | collective-permute-start | bytes 2949128 | tf_op jit(solution)/shard_map/ppermute | solution.py:58
  4.4 23.4 %collective-permute-start.1 = (bf16[768,640]{1,0:T(8,128)(2,1)}, bf16[768,640]{1,0:T(8,128)(2,1)S(1)}, u32[]{:S(2)}, u32[]{:S(2)}) collective-permute-start(bf16[768,640]{1,0:T(8,128)(2,1)} %shard_map.86.rest_0_.own_ref), channel_id=1, source_target_pairs={{0,8},{1,9},{2,10},{3,11},{4,12},{5,13},{6,14},{7,15},{8,0},{9,1},... | collective-permute-start | bytes 2949128 | tf_op jit(solution)/shard_map/ppermute | solution.py:58
  4.8 26.0 %collective-permute-start.2 = (bf16[768,640]{1,0:T(8,128)(2,1)}, bf16[768,640]{1,0:T(8,128)(2,1)S(1)}, u32[]{:S(2)}, u32[]{:S(2)}) collective-permute-start(bf16[768,640]{1,0:T(8,128)(2,1)} %shard_map.86.rest_0_.own_ref), channel_id=1, source_target_pairs={{8,16},{9,17},{10,18},{11,19},{12,20},{13,21},{14,22},{15,23},{16,... | collective-permute-start | bytes 2949128 | tf_op jit(solution)/shard_map/ppermute | solution.py:58
  9.4 3.2 %collective-permute-start.4 = (bf16[256,1280]{1,0:T(8,128)(2,1)}, bf16[256,1280]{1,0:T(8,128)(2,1)}, u32[]{:S(2)}, u32[]{:S(2)}) collective-permute-start(bf16[256,1280]{1,0:T(8,128)(2,1)} %g_a.1), channel_id=1, source_target_pairs={{0,1},{1,0},{2,3},{3,2},{4,5},{5,4},{6,7},{7,6},{8,9},{9,8},{10,11... | collective-permute-start | bytes 1966088 | tf_op jit(solution)/shard_map/ppermute | solution.py:58
  9.5 17.5 %collective-permute-start.5 = (bf16[256,1280]{1,0:T(8,128)(2,1)}, bf16[256,1280]{1,0:T(8,128)(2,1)}, u32[]{:S(2)}, u32[]{:S(2)}) collective-permute-start(bf16[256,1280]{1,0:T(8,128)(2,1)} %g_a.1), channel_id=1, source_target_pairs={{0,2},{1,3},{2,0},{3,1},{4,6},{5,7},{6,4},{7,5},{8,10},{9,11},{10,... | collective-permute-start | bytes 1966088 | tf_op jit(solution)/shard_map/ppermute | solution.py:58
  11.1 0.7 %copy-start.3 = (s32[16,10]{1,0:T(8,128)S(1)}, s32[16,10]{1,0:T(8,128)}, u32[]{:S(2)}) copy-start(s32[16,10]{1,0:T(8,128)} %mask_ref.1) | copy-start | bytes 1924
  12.7 2.9 %copy-start.1 = (bf16[640,5120]{1,0:T(8,128)(2,1)S(1)}, bf16[640,5120]{1,0:T(8,128)(2,1)}, u32[]{:S(2)}) copy-start(bf16[640,5120]{1,0:T(8,128)(2,1)} %w_ref.1) | copy-start | bytes 19660804
  15.5 1.1 %copy-start.2 = (bf16[256,1280]{1,0:T(8,128)(2,1)S(1)}, bf16[256,1280]{1,0:T(8,128)(2,1)}, u32[]{:S(2)}) copy-start(bf16[256,1280]{1,0:T(8,128)(2,1)} %g_a.1) | copy-start | bytes 1966084
  27.0 13.8 %copy-start = (bf16[768,640]{1,0:T(8,128)(2,1)S(1)}, bf16[768,640]{1,0:T(8,128)(2,1)}, u32[]{:S(2)}) copy-start(bf16[768,640]{1,0:T(8,128)(2,1)} %shard_map.86.rest_0_.own_ref) | copy-start | bytes 2949124
  27.0 9.7 %collective-permute-start.6 = (bf16[256,1280]{1,0:T(8,128)(2,1)}, bf16[256,1280]{1,0:T(8,128)(2,1)S(1)}, u32[]{:S(2)}, u32[]{:S(2)}) collective-permute-start(bf16[256,1280]{1,0:T(8,128)(2,1)} %collective-permute-done.5.g_a), channel_id=1, source_target_pairs={{0,1},{1,0},{2,3},{3,2},{4,5},{5,4},{6,7},{7,6},{8,9},{9,8},{10,11... | collective-permute-start | bytes 1966088 | tf_op jit(solution)/shard_map/ppermute | solution.py:58
  31.0 12.5 %collective-permute-start.3 = (bf16[512,640]{1,0:T(8,128)(2,1)S(1)}, bf16[512,640]{1,0:T(8,128)(2,1)S(1)}, u32[]{:S(2)}, u32[]{:S(2)}) collective-permute-start(bf16[512,640]{1,0:T(8,128)(2,1)S(1)} %slice.8), channel_id=1, source_target_pairs={{0,8},{1,5},{2,10},{3,7},{5,1},{7,3},{8,16},{9,13},{10,18},{11,15}... | collective-permute-start | bytes 1966088 | tf_op jit(solution)/shard_map/ppermute | solution.py:58
  34.7 14.4 %collective-permute-start.7 = (bf16[256,640]{1,0:T(8,128)(2,1)S(1)}, bf16[256,640]{1,0:T(8,128)(2,1)S(1)}, u32[]{:S(2)}, u32[]{:S(2)}) collective-permute-start(bf16[256,640]{1,0:T(8,128)(2,1)S(1)} %slice.9), channel_id=1, source_target_pairs={{0,8},{1,5},{2,10},{3,7},{5,1},{7,3},{8,16},{9,13},{10,18},{11,15}... | collective-permute-start | bytes 983048 | tf_op jit(solution)/shard_map/ppermute | solution.py:58
  38.8 13.4 %collective-permute-start.8 = (bf16[640,256]{1,0:T(8,128)(2,1)S(1)}, bf16[640,256]{1,0:T(8,128)(2,1)S(1)}, u32[]{:S(2)}, u32[]{:S(2)}) collective-permute-start(bf16[640,256]{1,0:T(8,128)(2,1)S(1)} %shard_map.88.d_ref.rest_4_), channel_id=1, source_target_pairs={{4,8},{5,9},{6,10},{7,11},{8,4},{9,5},{10,6},{11,7},{12,16},{13,17... | collective-permute-start | bytes 983048 | tf_op jit(solution)/shard_map/ppermute | solution.py:58
  44.4 13.0 %collective-permute-start.10 = (bf16[672,256]{1,0:T(8,128)(2,1)S(1)}, bf16[672,256]{1,0:T(8,128)(2,1)S(1)}, u32[]{:S(2)}, u32[]{:S(2)}) collective-permute-start(bf16[672,256]{1,0:T(8,128)(2,1)S(1)} %get-tuple-element.36), channel_id=1, source_target_pairs={{0,8},{1,9},{2,10},{3,11},{4,12},{5,13},{6,14},{7,15},{8,0},{9,1},... | collective-permute-start | bytes 1032200 | tf_op jit(solution)/shard_map/ppermute | solution.py:58
  44.5 13.0 %collective-permute-start.11 = (bf16[672,256]{1,0:T(8,128)(2,1)S(1)}, bf16[672,256]{1,0:T(8,128)(2,1)S(1)}, u32[]{:S(2)}, u32[]{:S(2)}) collective-permute-start(bf16[672,256]{1,0:T(8,128)(2,1)S(1)} %get-tuple-element.36), channel_id=1, source_target_pairs={{8,16},{9,17},{10,18},{11,19},{12,20},{13,21},{14,22},{15,23},{16,... | collective-permute-start | bytes 1032200 | tf_op jit(solution)/shard_map/ppermute | solution.py:58
  48.1 11.3 %collective-permute-start.9 = (bf16[672,256]{1,0:T(8,128)(2,1)S(1)}, bf16[672,256]{1,0:T(8,128)(2,1)S(1)}, u32[]{:S(2)}, u32[]{:S(2)}) collective-permute-start(bf16[672,256]{1,0:T(8,128)(2,1)S(1)} %get-tuple-element.36), channel_id=1, source_target_pairs={{0,4},{1,5},{2,6},{3,7},{4,0},{5,1},{6,2},{7,3},{8,12},{9,13},{10,... | collective-permute-start | bytes 1032200 | tf_op jit(solution)/shard_map/ppermute | solution.py:58
  49.1 8.3 %collective-permute-start.12 = (bf16[32,256]{1,0:T(8,128)(2,1)S(1)}, bf16[32,256]{1,0:T(8,128)(2,1)S(1)}, u32[]{:S(2)}, u32[]{:S(2)}) collective-permute-start(bf16[32,256]{1,0:T(8,128)(2,1)S(1)} %get-tuple-element.33.rest_5_), channel_id=1, source_target_pairs={{4,8},{5,9},{6,10},{7,11},{8,4},{9,5},{10,6},{11,7},{12,16},{13,17... | collective-permute-start | bytes 49160 | tf_op jit(solution)/shard_map/ppermute | solution.py:58

commit v9 on v8

--- a/solution.py
+++ b/solution.py
@@ -545,7 +545,7 @@
     kv_g = send(second[:2 * rows], forward)
     d_out_t = end_project(kept, far, far_near, after(begun, second))
     out, run, kept_weights = forward_part(
-        own_bias, kvq, [0, 1, 2, 3], [kvq_x, kvq_a, kvq_b]
+        own_bias, kvq, [0, 1, 3, 2], [kvq_x, kvq_b, kvq_a]
     )
     stats, packed = statistics(own_bias, kvq, 4, kv_g, out, run, d_out_t)
     q_g = send(second[2 * rows:], forward)
@@ -555,7 +555,7 @@
     p_x = send(packed, in_pair)
     s_g = send(stats, across)
     grad_queries, *begun_keys, scores, dprobs = query_side(
-        own_bias, kvq, [0, 1, 2, 3, 4], [kvq_x, kvq_a, kvq_b, kv_g], d_out_t,
+        own_bias, kvq, [0, 1, 3, 2, 4], [kvq_x, kvq_b, kvq_a, kv_g], d_out_t,
         stats, run, kept_weights, q_g, d_g,
     )
     grad_keys, grad_values = key_side(
@@ -563,8 +563,8 @@
         kvq,
         [
             (1, kvq_x, p_x, p_x),
+            (3, kvq_b, p_b, p_b),
             (2, kvq_a, p_a, p_a),
-            (3, kvq_b, p_b, p_b),
             (4, q_g, d_g, s_g),
         ],
         scores,

time: 62.9 us -> 62.9 us (level); the launches traced: 62.5 us -> 61.7 us
  starting transfers between devices: 22.4 us -> 21 us
  waiting for transfers between devices: 16.5 us -> 17.2 us
    ppermute x13, starting transfers between devices: 22.4 us -> 21 us  [send(): return lax.ppermute(array, BOTH, pairs)]
where the time goes in v9:
time: 62.9 us; the launch traced here: 61.7 us
  starting transfers between devices  21 us (33%)
  Pallas kernels  17.8 us (28%)
  waiting for transfers between devices  17.2 us (27%)
  local copies, waits for them, and re-layouts  4.74 us (8%)
  between operations  0.79 us (1%)
    ppermute x13, starting transfers between devices, send(): return lax.ppermute(array, BOTH, pairs)  21 us
    ppermute x13, waiting for transfers between devices, send(): return lax.ppermute(array, BOTH, pairs)  17.2 us
    pallas_call x5, Pallas kernels, kernel_call(): pl.pallas_call(kernel, in_specs=[SMEM if x.dtype == jnp.int32 else VMEM f...  9.42 us
    unnamed x8, local copies, waits for them, and re-layouts  4.65 us
    pallas_call x1, Pallas kernels, begin_project(): pl.pallas_call(begin_kernel, in_specs=[SMEM, ANY, VMEM, VMEM], out_specs=...  3.2 us
    pallas_call x1, Pallas kernels, key_side(): pl.pallas_call(functools.partial(key_kernel, [source[0] for source in sou...  3.03 us
    pallas_call x1, Pallas kernels, pack(): pl.pallas_call(pack_kernel, in_specs=[ANY] * count, out_specs=VMEM, out_s...  2.16 us
  transfers between devices with their start and end apart: 13, of which 7 were waited for; matrix products, arithmetic and copies ran while one was open for 1% of the time, Pallas kernels for 20%

profile of v9, /device:TPU:8, one launch (start us, length us, event | category | flops | bytes accessed | tf_op | source)
XLA Modules:
  0.0 61.7 jit_solution(8743931064268633312)
XLA Ops:
  0.6 2.2 %shard_map.86.rest_0_.own_ref = bf16[768,640]{1,0:T(8,128)(2,1)} custom-call(bf16[256,640]{1,0:T(8,128)(2,1)} %refs_0_.1, bf16[256,640]{1,0:T(8,128)(2,1)} %refs_1_.1, bf16[256,640]{1,0:T(8,128)(2,1)} %refs_2_.1), custom_call_target="tpu_custom_call" | custom-call | bytes 1966080 | tf_op jit(solution)/shard_map/pallas_call | solution.py:109
  2.8 1.6 %collective-permute-start = (bf16[768,640]{1,0:T(8,128)(2,1)}, bf16[768,640]{1,0:T(8,128)(2,1)S(1)}, u32[]{:S(2)}, u32[]{:S(2)}) collective-permute-start(bf16[768,640]{1,0:T(8,128)(2,1)} %shard_map.86.rest_0_.own_ref), channel_id=1, source_target_pairs={{0,4},{1,5},{2,6},{3,7},{4,0},{5,1},{6,2},{7,3},{8,12},{9,13},{10,... | collective-permute-start | bytes 2949128 | tf_op jit(solution)/shard_map/ppermute | solution.py:58
  4.4 3.5 %collective-permute-start.1 = (bf16[768,640]{1,0:T(8,128)(2,1)}, bf16[768,640]{1,0:T(8,128)(2,1)S(1)}, u32[]{:S(2)}, u32[]{:S(2)}) collective-permute-start(bf16[768,640]{1,0:T(8,128)(2,1)} %shard_map.86.rest_0_.own_ref), channel_id=1, source_target_pairs={{8,16},{9,17},{10,18},{11,19},{12,20},{13,21},{14,22},{15,23},{16,... | collective-permute-start | bytes 2949128 | tf_op jit(solution)/shard_map/ppermute | solution.py:58
  8.0 1.6 %collective-permute-start.5 = (bf16[256,1280]{1,0:T(8,128)(2,1)}, bf16[256,1280]{1,0:T(8,128)(2,1)}, u32[]{:S(2)}, u32[]{:S(2)}) collective-permute-start(bf16[256,1280]{1,0:T(8,128)(2,1)} %g_a.1), channel_id=1, source_target_pairs={{0,2},{1,3},{2,0},{3,1},{4,6},{5,7},{6,4},{7,5},{8,10},{9,11},{10,... | collective-permute-start | bytes 1966088 | tf_op jit(solution)/shard_map/ppermute | solution.py:58
  11.2 2.9 %copy-done.1 = bf16[640,5120]{1,0:T(8,128)(2,1)S(1)} copy-done((bf16[640,5120]{1,0:T(8,128)(2,1)S(1)}, bf16[640,5120]{1,0:T(8,128)(2,1)}, u32[]{:S(2)}) %copy-start.1) | copy-done | bytes 6553624
  14.0 1.1 %copy-done.2 = bf16[256,1280]{1,0:T(8,128)(2,1)S(1)} copy-done((bf16[256,1280]{1,0:T(8,128)(2,1)S(1)}, bf16[256,1280]{1,0:T(8,128)(2,1)}, u32[]{:S(2)}) %copy-start.2) | copy-done | bytes 655384
  15.1 3.2 %shard_map.87 = (f32[640,256]{1,0:T(8,128)S(1)}, bf16[640,2560]{1,0:T(8,128)(2,1)S(1)}) custom-call(s32[4]{0:T(128)S(1)} %pad_add_fusion.order_ref, bf16[640,5120]{1,0:T(8,128)(2,1)S(1)} %copy-done.1, bf16[256,1280]{1,0:T(8,128)(2,1)S(1)} %copy-done.2, bf16[256,1280]{1,0:T(8,128)(2,1)} %collective-permute-done.4.g_b), custom_call_target="tpu_custom_call" | custom-call | flops 838860800 | bytes 6553600 | tf_op jit(solution)/shard_map/pallas_call | solution.py:141
  18.3 7.1 %collective-permute-done.5.g_a = bf16[256,1280]{1,0:T(8,128)(2,1)} collective-permute-done((bf16[256,1280]{1,0:T(8,128)(2,1)}, bf16[256,1280]{1,0:T(8,128)(2,1)}, u32[]{:S(2)}, u32[]{:S(2)}) %collective-permute-start.5) | collective-permute-done | bytes 655392 | tf_op jit(solution)/shard_map/ppermute | solution.py:58
  25.5 1.1 %collective-permute-done.rest_1_.rest_0_ = bf16[768,640]{1,0:T(8,128)(2,1)S(1)} collective-permute-done((bf16[768,640]{1,0:T(8,128)(2,1)}, bf16[768,640]{1,0:T(8,128)(2,1)S(1)}, u32[]{:S(2)}, u32[]{:S(2)}) %collective-permute-start) | collective-permute-done | bytes 983072 | tf_op jit(solution)/shard_map/ppermute | solution.py:58
  26.6 3.1 %collective-permute-done.1.rest_2_.rest_1_.rest_3_ = bf16[768,640]{1,0:T(8,128)(2,1)S(1)} collective-permute-done((bf16[768,640]{1,0:T(8,128)(2,1)}, bf16[768,640]{1,0:T(8,128)(2,1)S(1)}, u32[]{:S(2)}, u32[]{:S(2)}) %collective-permute-start.1) | collective-permute-done | bytes 983072 | tf_op jit(solution)/shard_map/ppermute | solution.py:58
  29.7 1.4 %collective-permute-done.2.rest_3_.rest_2_.rest_6_ = bf16[768,640]{1,0:T(8,128)(2,1)S(1)} collective-permute-done((bf16[768,640]{1,0:T(8,128)(2,1)}, bf16[768,640]{1,0:T(8,128)(2,1)S(1)}, u32[]{:S(2)}, u32[]{:S(2)}) %collective-permute-start.2) | collective-permute-done | bytes 983072 | tf_op jit(solution)/shard_map/ppermute | solution.py:58
  31.3 2.4 %collective-permute-start.3 = (bf16[512,640]{1,0:T(8,128)(2,1)S(1)}, bf16[512,640]{1,0:T(8,128)(2,1)S(1)}, u32[]{:S(2)}, u32[]{:S(2)}) collective-permute-start(bf16[512,640]{1,0:T(8,128)(2,1)S(1)} %slice.8), channel_id=1, source_target_pairs={{0,8},{1,5},{2,10},{3,7},{5,1},{7,3},{8,16},{9,13},{10,18},{11,15}... | collective-permute-start | bytes 1966088 | tf_op jit(solution)/shard_map/ppermute | solution.py:58
  33.7 2.2 %collective-permute-start.7 = (bf16[256,640]{1,0:T(8,128)(2,1)S(1)}, bf16[256,640]{1,0:T(8,128)(2,1)S(1)}, u32[]{:S(2)}, u32[]{:S(2)}) collective-permute-start(bf16[256,640]{1,0:T(8,128)(2,1)S(1)} %slice.9), channel_id=1, source_target_pairs={{0,8},{1,5},{2,10},{3,7},{5,1},{7,3},{8,16},{9,13},{10,18},{11,15}... | collective-permute-start | bytes 983048 | tf_op jit(solution)/shard_map/ppermute | solution.py:58
  35.9 2.1 %shard_map.88.d_ref.rest_4_ = bf16[640,256]{1,0:T(8,128)(2,1)S(1)} custom-call(bf16[640,2560]{1,0:T(8,128)(2,1)S(1)} %get-tuple-element.27.w_ref, bf16[256,1280]{1,0:T(8,128)(2,1)} %collective-permute-done.5.g_a, bf16[256,1280]{1,0:T(8,128)(2,1)S(1)} %collective-permute-done.6.g_b, f32[640,256]{1,0:T(8,128)S(1)} %get-tuple-element.30.begun), custom_call_target="tpu_custom_call" | custom-call | flops 838860800 | bytes 5242880 | tf_op jit(solution)/shard_map/pallas_call | solution.py:38
  38.0 1.9 %collective-permute-start.8 = (bf16[640,256]{1,0:T(8,128)(2,1)S(1)}, bf16[640,256]{1,0:T(8,128)(2,1)S(1)}, u32[]{:S(2)}, u32[]{:S(2)}) collective-permute-start(bf16[640,256]{1,0:T(8,128)(2,1)S(1)} %shard_map.88.d_ref.rest_4_), channel_id=1, source_target_pairs={{4,8},{5,9},{6,10},{7,11},{8,4},{9,5},{10,6},{11,7},{12,16},{13,17... | collective-permute-start | bytes 983048 | tf_op jit(solution)/shard_map/ppermute | solution.py:58
  39.9 2.0 %shard_map.89 = (f32[640,256]{1,0:T(8,128)S(1)}, f32[80,256]{1,0:T(8,128)S(1)}, f32[5120,256]{1,0:T(8,128)S(1)}) custom-call(f32[16,256]{1,0:T(8,128)S(1)} %get-tuple-element.23.bias_ref, bf16[768,640]{1,0:T(8,128)(2,1)S(1)} %copy-done, bf16[768,640]{1,0:T(8,128)(2,1)S(1)} %collective-permute-done.rest_1_.rest_0_, ...), custom_call_target="tpu_custom_call" | custom-call | flops 671088640 | bytes 3948544 | tf_op jit(solution)/shard_map/pallas_call | solution.py:38
  41.9 1.8 %collective-permute-done.3.w_ref.rest_3_ = bf16[512,640]{1,0:T(8,128)(2,1)S(1)} collective-permute-done((bf16[512,640]{1,0:T(8,128)(2,1)S(1)}, bf16[512,640]{1,0:T(8,128)(2,1)S(1)}, u32[]{:S(2)}, u32[]{:S(2)}) %collective-permute-start.3) | collective-permute-done | bytes 655392 | tf_op jit(solution)/shard_map/ppermute | solution.py:58
  43.7 0.9 %shard_map.90 = (bf16[32,256]{1,0:T(8,128)(2,1)S(1)}, bf16[672,256]{1,0:T(8,128)(2,1)S(1)}) custom-call(f32[16,256]{1,0:T(8,128)S(1)} %get-tuple-element.23.bias_ref, bf16[768,640]{1,0:T(8,128)(2,1)S(1)} %copy-done, bf16[512,640]{1,0:T(8,128)(2,1)S(1)} %collective-permute-done.3.w_ref.rest_3_, f32[640,256]{1,0:T(8,128)S(1)} %get-tuple-element.31.out_in, ...), custom_call_target="tpu_custom_call" | custom-call | flops 167772160 | bytes 2719744 | tf_op jit(solution)/shard_map/pallas_call | solution.py:38
  44.6 2.4 %collective-permute-start.10 = (bf16[672,256]{1,0:T(8,128)(2,1)S(1)}, bf16[672,256]{1,0:T(8,128)(2,1)S(1)}, u32[]{:S(2)}, u32[]{:S(2)}) collective-permute-start(bf16[672,256]{1,0:T(8,128)(2,1)S(1)} %get-tuple-element.36), channel_id=1, source_target_pairs={{8,16},{9,17},{10,18},{11,19},{12,20},{13,21},{14,22},{15,23},{16,... | collective-permute-start | bytes 1032200 | tf_op jit(solution)/shard_map/ppermute | solution.py:58
  47.7 4.8 %collective-permute-start.12 = (bf16[32,256]{1,0:T(8,128)(2,1)S(1)}, bf16[32,256]{1,0:T(8,128)(2,1)S(1)}, u32[]{:S(2)}, u32[]{:S(2)}) collective-permute-start(bf16[32,256]{1,0:T(8,128)(2,1)S(1)} %get-tuple-element.33.rest_5_), channel_id=1, source_target_pairs={{4,8},{5,9},{6,10},{7,11},{8,4},{9,5},{10,6},{11,7},{12,16},{13,17... | collective-permute-start | bytes 49160 | tf_op jit(solution)/shard_map/ppermute | solution.py:58
  52.5 3.6 %shard_map.91 = (bf16[256,640]{1,0:T(8,128)(2,1)}, f32[256,640]{1,0:T(8,128)S(1)}, f32[256,640]{1,0:T(8,128)S(1)}, f32[5120,256]{1,0:T(8,128)S(1)}, f32[1280,256]{1,0:T(8,128)S(1)}) custom-call(f32[16,256]{1,0:T(8,128)S(1)} %get-tuple-element.23.bias_ref, bf16[768,640]{1,0:T(8,128)(2,1)S(1)} %copy-done, ...), custom_call_target="tpu_custom_call" | custom-call | flops 1509949440 | bytes 10928128 | tf_op jit(solution)/shard_map/pallas_call | solution.py:38
  56.1 1.1 %collective-permute-done.12.rest_11_ = bf16[32,256]{1,0:T(8,128)(2,1)S(1)} collective-permute-done((bf16[32,256]{1,0:T(8,128)(2,1)S(1)}, bf16[32,256]{1,0:T(8,128)(2,1)S(1)}, u32[]{:S(2)}, u32[]{:S(2)}) %collective-permute-start.12) | collective-permute-done | bytes 16416 | tf_op jit(solution)/shard_map/ppermute | solution.py:58
  57.2 1.5 %collective-permute-done.9.rest_1_.rest_2_ = bf16[672,256]{1,0:T(8,128)(2,1)S(1)} collective-permute-done((bf16[672,256]{1,0:T(8,128)(2,1)S(1)}, bf16[672,256]{1,0:T(8,128)(2,1)S(1)}, u32[]{:S(2)}, u32[]{:S(2)}) %collective-permute-start.9) | collective-permute-done | bytes 344096 | tf_op jit(solution)/shard_map/ppermute | solution.py:58
  58.7 3.0 %shard_map.92 = (bf16[256,640]{1,0:T(8,128)(2,1)}, bf16[256,640]{1,0:T(8,128)(2,1)}) custom-call(f32[16,256]{1,0:T(8,128)S(1)} %get-tuple-element.25.bias_ref, bf16[768,640]{1,0:T(8,128)(2,1)S(1)} %copy-done, bf16[768,640]{1,0:T(8,128)(2,1)S(1)} %collective-permute-done.rest_1_.rest_0_, bf16[672,256]{1,0:T(8,128)(2,1)S(1)} %collective-permute-done.9.rest_1_.rest_2_, ...), custom_call_target="tpu_custom_call" | custom-call | flops 1090519040 | bytes 14548992 | tf_op jit(solution)/shard_map/pallas_call | solution.py:503
  (22 shorter events, 2.7 us)
Async XLA Ops:
  2.8 23.8 %collective-permute-start = (bf16[768,640]{1,0:T(8,128)(2,1)}, bf16[768,640]{1,0:T(8,128)(2,1)S(1)}, u32[]{:S(2)}, u32[]{:S(2)}) collective-permute-start(bf16[768,640]{1,0:T(8,128)(2,1)} %shard_map.86.rest_0_.own_ref), channel_id=1, source_target_pairs={{0,4},{1,5},{2,6},{3,7},{4,0},{5,1},{6,2},{7,3},{8,12},{9,13},{10,... | collective-permute-start | bytes 2949128 | tf_op jit(solution)/shard_map/ppermute | solution.py:58
  4.4 25.3 %collective-permute-start.1 = (bf16[768,640]{1,0:T(8,128)(2,1)}, bf16[768,640]{1,0:T(8,128)(2,1)S(1)}, u32[]{:S(2)}, u32[]{:S(2)}) collective-permute-start(bf16[768,640]{1,0:T(8,128)(2,1)} %shard_map.86.rest_0_.own_ref), channel_id=1, source_target_pairs={{8,16},{9,17},{10,18},{11,19},{12,20},{13,21},{14,22},{15,23},{16,... | collective-permute-start | bytes 2949128 | tf_op jit(solution)/shard_map/ppermute | solution.py:58
  7.8 23.2 %collective-permute-start.2 = (bf16[768,640]{1,0:T(8,128)(2,1)}, bf16[768,640]{1,0:T(8,128)(2,1)S(1)}, u32[]{:S(2)}, u32[]{:S(2)}) collective-permute-start(bf16[768,640]{1,0:T(8,128)(2,1)} %shard_map.86.rest_0_.own_ref), channel_id=1, source_target_pairs={{0,8},{1,9},{2,10},{3,11},{4,12},{5,13},{6,14},{7,15},{8,0},{9,1},... | collective-permute-start | bytes 2949128 | tf_op jit(solution)/shard_map/ppermute | solution.py:58
  7.9 3.2 %collective-permute-start.4 = (bf16[256,1280]{1,0:T(8,128)(2,1)}, bf16[256,1280]{1,0:T(8,128)(2,1)}, u32[]{:S(2)}, u32[]{:S(2)}) collective-permute-start(bf16[256,1280]{1,0:T(8,128)(2,1)} %g_a.1), channel_id=1, source_target_pairs={{0,1},{1,0},{2,3},{3,2},{4,5},{5,4},{6,7},{7,6},{8,9},{9,8},{10,11... | collective-permute-start | bytes 1966088 | tf_op jit(solution)/shard_map/ppermute | solution.py:58
  8.0 17.5 %collective-permute-start.5 = (bf16[256,1280]{1,0:T(8,128)(2,1)}, bf16[256,1280]{1,0:T(8,128)(2,1)}, u32[]{:S(2)}, u32[]{:S(2)}) collective-permute-start(bf16[256,1280]{1,0:T(8,128)(2,1)} %g_a.1), channel_id=1, source_target_pairs={{0,2},{1,3},{2,0},{3,1},{4,6},{5,7},{6,4},{7,5},{8,10},{9,11},{10,... | collective-permute-start | bytes 1966088 | tf_op jit(solution)/shard_map/ppermute | solution.py:58
  9.6 0.7 %copy-start.3 = (s32[16,10]{1,0:T(8,128)S(1)}, s32[16,10]{1,0:T(8,128)}, u32[]{:S(2)}) copy-start(s32[16,10]{1,0:T(8,128)} %mask_ref.1) | copy-start | bytes 1924
  11.2 2.9 %copy-start.1 = (bf16[640,5120]{1,0:T(8,128)(2,1)S(1)}, bf16[640,5120]{1,0:T(8,128)(2,1)}, u32[]{:S(2)}) copy-start(bf16[640,5120]{1,0:T(8,128)(2,1)} %w_ref.1) | copy-start | bytes 19660804
  14.0 1.1 %copy-start.2 = (bf16[256,1280]{1,0:T(8,128)(2,1)S(1)}, bf16[256,1280]{1,0:T(8,128)(2,1)}, u32[]{:S(2)}) copy-start(bf16[256,1280]{1,0:T(8,128)(2,1)} %g_a.1) | copy-start | bytes 1966084
  25.5 14.5 %copy-start = (bf16[768,640]{1,0:T(8,128)(2,1)S(1)}, bf16[768,640]{1,0:T(8,128)(2,1)}, u32[]{:S(2)}) copy-start(bf16[768,640]{1,0:T(8,128)(2,1)} %shard_map.86.rest_0_.own_ref) | copy-start | bytes 2949124
  25.5 10.4 %collective-permute-start.6 = (bf16[256,1280]{1,0:T(8,128)(2,1)}, bf16[256,1280]{1,0:T(8,128)(2,1)S(1)}, u32[]{:S(2)}, u32[]{:S(2)}) collective-permute-start(bf16[256,1280]{1,0:T(8,128)(2,1)} %collective-permute-done.5.g_a), channel_id=1, source_target_pairs={{0,1},{1,0},{2,3},{3,2},{4,5},{5,4},{6,7},{7,6},{8,9},{9,8},{10,11... | collective-permute-start | bytes 1966088 | tf_op jit(solution)/shard_map/ppermute | solution.py:58
  31.3 12.5 %collective-permute-start.3 = (bf16[512,640]{1,0:T(8,128)(2,1)S(1)}, bf16[512,640]{1,0:T(8,128)(2,1)S(1)}, u32[]{:S(2)}, u32[]{:S(2)}) collective-permute-start(bf16[512,640]{1,0:T(8,128)(2,1)S(1)} %slice.8), channel_id=1, source_target_pairs={{0,8},{1,5},{2,10},{3,7},{5,1},{7,3},{8,16},{9,13},{10,18},{11,15}... | collective-permute-start | bytes 1966088 | tf_op jit(solution)/shard_map/ppermute | solution.py:58
  33.7 14.0 %collective-permute-start.7 = (bf16[256,640]{1,0:T(8,128)(2,1)S(1)}, bf16[256,640]{1,0:T(8,128)(2,1)S(1)}, u32[]{:S(2)}, u32[]{:S(2)}) collective-permute-start(bf16[256,640]{1,0:T(8,128)(2,1)S(1)} %slice.9), channel_id=1, source_target_pairs={{0,8},{1,5},{2,10},{3,7},{5,1},{7,3},{8,16},{9,13},{10,18},{11,15}... | collective-permute-start | bytes 983048 | tf_op jit(solution)/shard_map/ppermute | solution.py:58
  38.0 14.4 %collective-permute-start.8 = (bf16[640,256]{1,0:T(8,128)(2,1)S(1)}, bf16[640,256]{1,0:T(8,128)(2,1)S(1)}, u32[]{:S(2)}, u32[]{:S(2)}) collective-permute-start(bf16[640,256]{1,0:T(8,128)(2,1)S(1)} %shard_map.88.d_ref.rest_4_), channel_id=1, source_target_pairs={{4,8},{5,9},{6,10},{7,11},{8,4},{9,5},{10,6},{11,7},{12,16},{13,17... | collective-permute-start | bytes 983048 | tf_op jit(solution)/shard_map/ppermute | solution.py:58
  44.6 12.6 %collective-permute-start.10 = (bf16[672,256]{1,0:T(8,128)(2,1)S(1)}, bf16[672,256]{1,0:T(8,128)(2,1)S(1)}, u32[]{:S(2)}, u32[]{:S(2)}) collective-permute-start(bf16[672,256]{1,0:T(8,128)(2,1)S(1)} %get-tuple-element.36), channel_id=1, source_target_pairs={{8,16},{9,17},{10,18},{11,19},{12,20},{13,21},{14,22},{15,23},{16,... | collective-permute-start | bytes 1032200 | tf_op jit(solution)/shard_map/ppermute | solution.py:58
  47.0 10.2 %collective-permute-start.11 = (bf16[672,256]{1,0:T(8,128)(2,1)S(1)}, bf16[672,256]{1,0:T(8,128)(2,1)S(1)}, u32[]{:S(2)}, u32[]{:S(2)}) collective-permute-start(bf16[672,256]{1,0:T(8,128)(2,1)S(1)} %get-tuple-element.36), channel_id=1, source_target_pairs={{0,8},{1,9},{2,10},{3,11},{4,12},{5,13},{6,14},{7,15},{8,0},{9,1},... | collective-permute-start | bytes 1032200 | tf_op jit(solution)/shard_map/ppermute | solution.py:58
  47.1 11.7 %collective-permute-start.9 = (bf16[672,256]{1,0:T(8,128)(2,1)S(1)}, bf16[672,256]{1,0:T(8,128)(2,1)S(1)}, u32[]{:S(2)}, u32[]{:S(2)}) collective-permute-start(bf16[672,256]{1,0:T(8,128)(2,1)S(1)} %get-tuple-element.36), channel_id=1, source_target_pairs={{0,4},{1,5},{2,6},{3,7},{4,0},{5,1},{6,2},{7,3},{8,12},{9,13},{10,... | collective-permute-start | bytes 1032200 | tf_op jit(solution)/shard_map/ppermute | solution.py:58
  47.7 9.5 %collective-permute-start.12 = (bf16[32,256]{1,0:T(8,128)(2,1)S(1)}, bf16[32,256]{1,0:T(8,128)(2,1)S(1)}, u32[]{:S(2)}, u32[]{:S(2)}) collective-permute-start(bf16[32,256]{1,0:T(8,128)(2,1)S(1)} %get-tuple-element.33.rest_5_), channel_id=1, source_target_pairs={{4,8},{5,9},{6,10},{7,11},{8,4},{9,5},{10,6},{11,7},{12,16},{13,17... | collective-permute-start | bytes 49160 | tf_op jit(solution)/shard_map/ppermute | solution.py:58
